TPU v7x, 128 devices: a whole 4x4x4 slice. The times are simulated.
128 devices in a mesh: row: 8 (over z, core), col: 16 (over y, x).
Axes of the slice: x: 4, y: 4, z: 4, core: 2. Of those that a mesh axis runs over, the one named last changes fastest.
Arguments:
- panel: bfloat16 [64, 131072], P(None, ('row', 'col')), may hold values from -6 to 6
- block_values: bfloat16 [65536, 4096], P(('row', 'col')), may hold values from 0 to 0.049804688
- row_starts: int32 [32768], P(('row', 'col')), may hold values from 0 to 512, as said below
- block_columns: int32 [65536], P(('row', 'col')), may hold values from 0 to 127, as said below
- block_counts: int32 [128], P(('row', 'col')), may hold values from 128 to 512, as said below
Outputs:
- basis: float32 [64, 131072], P(None, ('row', 'col'))
- factor: float32 [64, 64], replicated
Inputs may be any that keep to these rules, and one draw needn't show every extreme that they name: `block_counts`: each device's count of stored blocks; some device fills all 512 slots, and column bands differ in load. `row_starts`: within each device's 256 entries the starts do not fall, the first is 0 and none passes that device's block count. `block_columns`: block columns within a device's band.
All inputs are finite; a program needn't handle non-finite values.
Results may differ from a plain program's by a relative error of at most 0.011.
Values may be sent and summed in bfloat16 or wider, within the bound.
No kernel may reach another device: no remote copies, remote signals or barrier semaphores. Data moves between devices by JAX's collectives and lax.ppermute only.
A program may use at most 64 MiB of HBM per device.

v0:
```python
import jax
import jax.numpy as jnp
from jax import lax
from jax.sharding import PartitionSpec as P

K = 64
BS = 64
GROUP = 128


def per_device(panel, block_values, row_starts, block_columns, block_counts):
    width, piece = panel.shape
    slots = block_values.shape[0]
    row_blocks = row_starts.shape[0]
    rows_size = lax.axis_size("row")
    cols_size = lax.axis_size("col")
    span = piece * rows_size
    col_place = lax.axis_index("col")
    whole = lax.all_gather(panel, ("row", "col"), axis=1, tiled=True)
    column_band = lax.dynamic_slice_in_dim(whole, col_place * span, span, 1)
    tiles = column_band.reshape(K, span // BS, BS).transpose(1, 0, 2).reshape(span // BS, K * BS)
    positions = lax.iota(jnp.int32, slots)
    block_rows = jnp.sum((row_starts[None, :] <= positions[:, None]).astype(jnp.int32), axis=1) - 1
    count = block_counts[0]
    segments = jnp.where(positions < count, block_rows, row_blocks)

    def add_group(index, total):
        first = index * GROUP
        values = lax.dynamic_slice_in_dim(block_values, first, GROUP, 0).reshape(GROUP, BS, BS)
        columns = lax.dynamic_slice_in_dim(block_columns, first, GROUP, 0)
        targets = lax.dynamic_slice_in_dim(segments, first, GROUP, 0)
        picked = jnp.take(tiles, columns, axis=0).reshape(GROUP, K, BS)
        products = jnp.einsum("gkc,grc->gkr", picked, values, preferred_element_type=jnp.float32)
        return total + jax.ops.segment_sum(
            products.reshape(GROUP, K * BS), targets, num_segments=row_blocks
        )

    rounds = (count + GROUP - 1) // GROUP
    total = lax.fori_loop(0, rounds, add_group, jnp.zeros((row_blocks, K * BS), jnp.float32))
    partial_value = total.reshape(row_blocks, K, BS).transpose(1, 0, 2).reshape(K, row_blocks * BS)
    image = lax.psum_scatter(
        partial_value.astype(jnp.bfloat16), "col", scatter_dimension=1, tiled=True
    ).astype(jnp.float32) + panel.astype(jnp.float32)
    total_points = piece * rows_size * cols_size
    local_gram = (
        jnp.dot(image, image.T, precision=lax.Precision.HIGHEST, preferred_element_type=jnp.float32)
        / total_points
    )
    gram = lax.psum(local_gram, ("row", "col"))
    factor = jnp.linalg.cholesky(gram)
    basis = jax.scipy.linalg.solve_triangular(factor, image, lower=True)
    return (basis, factor)


def solution(mesh):
    in_specs = (
        P(None, ("row", "col")),
        P(("row", "col"), None),
        P(("row", "col")),
        P(("row", "col")),
        P(("row", "col")),
    )
    out_specs = (P(None, ("row", "col")), P())
    return jax.shard_map(
        per_device, mesh=mesh, in_specs=in_specs, out_specs=out_specs, check_vma=False
    )
```

profile of v0, /device:TPU:0, one launch (start us, length us, event | category | flops | bytes accessed | tf_op | source)
XLA Modules:
  0.0 422.1 jit_solution(13527245978012780254)
XLA Ops:
  9.5 87.1 %all-gather.2.cloned.1.call-done = bf16[64,131072]{1,0:T(8,128)(2,1)} async-done(((bf16[64,1024]{1,0:T(8,128)(2,1)}), bf16[64,131072]{1,0:T(8,128)(2,1)}) %all-gather.2.cloned.1.call-update) | async-done | bytes 16777232 | tf_op jit(solution)/shard_map/all_gather | solution.py:19
  97.9 2.3 reshape.43
  101.7 2.5 broadcast.71
  104.1 71.6 %while.10 = (s32[]{:T(128)}, f32[256,4096]{1,0:T(8,128)}, s32[]{:T(128)}, s32[512]{0:T(512)S(1)}, s32[512]{0:T(512)}, /*index=5*/bf16[128,4096]{1,0:T(8,128)(2,1...) while((s32[]{:T(128)}, f32[256,4096]{1,0:T(8,128)}, s32[]{:T(128)}, ...), condition=%wide.region_3.4_spmd, body=%wide.region_1.3_spmd.sunk | while | flops 68159240 | bytes 33562536 | solution.py:39
  107.8 3.9 copy.54
  111.8 2.4 constant_dynamic-slice_fusion.3
  114.1 2.3 copy.55
  116.4 4.7 %copy.56 = bf16[128,64,64]{2,1,0:T(8,128)(2,1)} copy(bf16[128,64,64]{0,2,1:T(8,128)(2,1)} %bitcast.33) | data formatting | bytes 2097152 | tf_op jit(solution)/shard_map/while/body/reshape | solution.py:29
  121.1 4.7 %fusion.11 = f32[128,64,64]{2,1,0:T(8,128)} fusion(bf16[128,64,64]{2,1,0:T(8,128)(2,1)S(1)} %copy.54, bf16[128,64,64]{2,1,0:T(8,128)(2,1)} %copy.56), kind=kOutput, calls=%fused_computation.24.clone.1 | convolution fusion | flops 67108864 | bytes 4194304 | tf_op jit(solution)/shard_map/while/body/gkc,grc->gkr/dot_general | solution.py:33
  125.8 4.8 %copy.57 = f32[128,64,64]{0,2,1:T(8,128)} copy(f32[128,64,64]{2,1,0:T(8,128)} %fusion.11) | data formatting | bytes 4194304 | tf_op jit(solution)/shard_map/while/body/gkc,grc->gkr/dot_general | solution.py:33
  132.6 7.3 %scatter_fusion = f32[256,4096]{1,0:T(8,128)} fusion(f32[256,4096]{1,0:T(8,128)} %get-tuple-element.140, s32[128]{0:T(128)S(1)} %dynamic_slice.20, f32[128,4096]{1,0:T(8,128)S(1)} %copy.58), kind=kCustom, calls=%fused_computation.1.clone.1 | custom fusion | flops 524288 | bytes 6291968 | tf_op jit(solution)/shard_map/while/body/scatter-add | solution.py:34
  143.7 3.9 copy.54
  147.6 2.4 constant_dynamic-slice_fusion.3
  152.2 4.7 %copy.56 = bf16[128,64,64]{2,1,0:T(8,128)(2,1)} copy(bf16[128,64,64]{0,2,1:T(8,128)(2,1)} %bitcast.33) | data formatting | bytes 2097152 | tf_op jit(solution)/shard_map/while/body/reshape | solution.py:29
  156.9 4.7 %fusion.11 = f32[128,64,64]{2,1,0:T(8,128)} fusion(bf16[128,64,64]{2,1,0:T(8,128)(2,1)S(1)} %copy.54, bf16[128,64,64]{2,1,0:T(8,128)(2,1)} %copy.56), kind=kOutput, calls=%fused_computation.24.clone.1 | convolution fusion | flops 67108864 | bytes 4194304 | tf_op jit(solution)/shard_map/while/body/gkc,grc->gkr/dot_general | solution.py:33
  161.7 4.8 %copy.57 = f32[128,64,64]{0,2,1:T(8,128)} copy(f32[128,64,64]{2,1,0:T(8,128)} %fusion.11) | data formatting | bytes 4194304 | tf_op jit(solution)/shard_map/while/body/gkc,grc->gkr/dot_general | solution.py:33
  168.4 7.3 %scatter_fusion = f32[256,4096]{1,0:T(8,128)} fusion(f32[256,4096]{1,0:T(8,128)} %get-tuple-element.140, s32[128]{0:T(128)S(1)} %dynamic_slice.20, f32[128,4096]{1,0:T(8,128)S(1)} %copy.58), kind=kCustom, calls=%fused_computation.1.clone.1 | custom fusion | flops 524288 | bytes 6291968 | tf_op jit(solution)/shard_map/while/body/scatter-add | solution.py:34
  175.8 3.7 copy.41
  179.5 3.2 copy.42
  182.7 6.0 %convert_element_type.25 = bf16[64,16384]{1,0:T(8,128)(2,1)} reshape(bf16[64,256,64]{2,1,0:T(8,128)(2,1)} %copy.42) | data formatting | bytes 4194304 | tf_op jit(solution)/shard_map/convert_element_type | solution.py:42
  188.7 145.4 %reduce-scatter.2.cloned.1.call-done = bf16[64,1024]{1,0:T(8,128)(2,1)} async-done(((bf16[64,16384]{1,0:T(8,128)(2,1)}), bf16[64,1024]{1,0:T(8,128)(2,1)}) %reduce-scatter.2.cloned.1.call-update) | async-done | bytes 131088 | tf_op jit(solution)/shard_map/reduce_scatter | solution.py:41
  335.5 65.0 %psum.7 = f32[64,64]{0,1:T(8,128)S(1)} all-reduce(f32[64,64]{0,1:T(8,128)S(1)} %convolution_multiply_fusion), channel_id=1, replica_groups=mesh['row'=8,'col'=16] {'row','col'}, use_global_device_ids=true, to_apply=%region_5.6 | all-reduce | flops 4096 | bytes 32768 | tf_op jit(solution)/shard_map/psum | solution.py:49
  400.5 5.8 %cholesky.16 = f32[64,64]{1,0:T(8,128)S(1)} custom-call(f32[64,64]{1,0:T(8,128)S(1)} %fusion.2), custom_call_target="Cholesky" | custom-call | tf_op jit(solution)/shard_map/jit(cholesky)/cholesky | solution.py:50
  408.3 4.9 %custom-call.7 = f32[1,64,64]{1,2,0:T(8,128)S(1)} custom-call(f32[1,64,64]{2,1,0:T(8,128)S(1)} %get-tuple-element.78), custom_call_target="InvertDiagBlocksLowerTriangular" | custom-call | tf_op jit(solution)/shard_map/jit(_solve_triangular)/triangular_solve | solution.py:51
  (33 shorter events, 23.5 us)
Async XLA Ops:
  7.2 89.4 %all-gather.2.cloned.1.call-start = ((), (), s32[]{:S(2)}) async-start(), calls=%async_computation.1 | async-start | bytes 16908288 | tf_op jit(solution)/shard_map/all_gather | solution.py:19
  7.9 326.2 %reduce-scatter.2.cloned.1.call-start = ((), (), s32[]{:S(2)}) async-start(), calls=%async_computation.2 | async-start | bytes 2228224 | tf_op jit(solution)/shard_map/reduce_scatter | solution.py:41
  188.7 145.4 %copy-start = (bf16[64,1024]{1,0:T(8,128)(2,1)S(1)}, bf16[64,1024]{1,0:T(8,128)(2,1)}, u32[]{:S(2)}) copy-start(bf16[64,1024]{1,0:T(8,128)(2,1)} %param.7) | copy-start | bytes 393220
Sparse Core Ops, SparseCore 0:
  11.0 85.5 all-gather.1
  188.8 145.2 reduce-scatter.1
where the time goes:
time: 424 us; the launch traced here: 422 us
  waiting for transfers between devices  233 us (55%)
  blocking collectives  65 us (15%)
  local copies, waits for them, and re-layouts  64.3 us (15%)
  other arithmetic  31.9 us (8%)
  between operations  14.8 us (3%)
  matrix products  12.9 us (3%)
    reduce_scatter x1, waiting for transfers between devices, per_device(): lax.psum_scatter(partial_value.astype(jnp.bfloat16), 'col', scatter_dimen...  145 us
    all_gather x1, waiting for transfers between devices, per_device(): whole = lax.all_gather(panel, ('row', 'col'), axis=1, tiled=True)  87.1 us
    psum x1, blocking collectives, per_device(): gram = lax.psum(local_gram, ('row', 'col'))  65 us
    scatter-add x2, other arithmetic, add_group(): jax.ops.segment_sum(products.reshape(GROUP, K * BS), targets, num_segment...  14.6 us
    dot_general x2, local copies, waits for them, and re-layouts, add_group(): jnp.einsum('gkc,grc->gkr', picked, values, preferred_element_type=jnp.flo...  9.52 us
    dot_general x2, matrix products, add_group(): jnp.einsum('gkc,grc->gkr', picked, values, preferred_element_type=jnp.flo...  9.46 us
    reshape x2, local copies, waits for them, and re-layouts, add_group(): lax.dynamic_slice_in_dim(block_values, first, GROUP, 0)  9.4 us
    dynamic_slice x4, local copies, waits for them, and re-layouts, add_group(): lax.dynamic_slice_in_dim(block_values, first, GROUP, 0)  9.27 us
  transfers between devices with their start and end apart: 2, of which 2 were waited for; matrix products, arithmetic and copies ran while one was open for 0% of the time, Pallas kernels for 0%

commit v1 on v0

v1 whole, which is shorter than its diff:
```python
import jax
import jax.numpy as jnp
from jax import lax
from jax.experimental import pallas as pl
from jax.experimental.pallas import tpu as pltpu
from jax.sharding import Mesh
from jax.sharding import PartitionSpec as P

K = 64
BS = 64
CAP = 512
RBLK = 256
CBLK = 128
PIECE = 1024
POINTS = 131072
COLS = 16
HALF = BS // 2
UNROLL = 8
AXES = ("z", "core", "y", "x")
ROW = ("z", "core")
COL = ("y", "x")
F32 = jnp.float32
BF16 = jnp.bfloat16


def values_kernel(values, out, spread):
    for group in range(values.shape[0] // 16):
        for tile in range(HALF):
            part = values[group * 16 : (group + 1) * 16, tile * 128 : (tile + 1) * 128]
            spread[pl.ds(tile, 16, stride=HALF), :] = part.astype(F32)
        out[group * 16 * HALF : (group + 1) * 16 * HALF, :] = spread[...].astype(BF16)


def relayout_values(block_values):
    step = 64
    return pl.pallas_call(
        values_kernel,
        grid=(CAP // step,),
        in_specs=[pl.BlockSpec((step, BS * BS), lambda i: (i, 0))],
        out_specs=pl.BlockSpec((step * HALF, 128), lambda i: (i, 0)),
        out_shape=jax.ShapeDtypeStruct((CAP * HALF, 128), BF16),
        scratch_shapes=[pltpu.VMEM((16 * HALF, 128), F32)],
        compiler_params=pltpu.CompilerParams(vmem_limit_bytes=16 * 1024 * 1024),
        cost_estimate=pl.CostEstimate(flops=0, bytes_accessed=8 * 1024 * 1024, transcendentals=0),
    )(block_values)


def multiply_kernel(rows, tiles, rounds, band, values, out, weights, total):
    low = lax.broadcasted_iota(jnp.int32, (K, 128), 1) < BS
    zero = jnp.zeros((K, 128), F32)

    def fill(piece, carry):
        for lane in range(PIECE // 128):
            pair = band[piece, :, lane * 128 : (lane + 1) * 128].astype(F32)
            swapped = pltpu.roll(pair, BS, 1)
            first = pl.multiple_of((piece * (PIECE // BS) + 2 * lane) * 128, 128)
            weights[pl.ds(first, 64), :] = jnp.where(low, pair, zero).astype(BF16)
            weights[pl.ds(first + 64, 64), :] = jnp.where(low, zero, swapped).astype(BF16)
            weights[pl.ds(first + 128, 64), :] = jnp.where(low, swapped, zero).astype(BF16)
            weights[pl.ds(first + 192, 64), :] = jnp.where(low, zero, pair).astype(BF16)
        return carry

    lax.fori_loop(0, band.shape[0], fill, 0)
    total[...] = jnp.zeros_like(total)

    def add_group(index, carry):
        products = []
        for offset in range(UNROLL):
            slot = index * UNROLL + offset
            block = values[pl.ds(pl.multiple_of(slot * HALF, HALF), HALF), :]
            tile = weights[pl.ds(pl.multiple_of(tiles[slot] * 128, 128), 128), :]
            products.append(
                lax.dot_general(block, tile, (((1,), (1,)), ((), ())), preferred_element_type=F32)
            )
        for offset in range(UNROLL):
            slot = index * UNROLL + offset
            place = pl.ds(pl.multiple_of(rows[slot] * HALF, HALF), HALF)
            total[place, :] = total[place, :] + products[offset]
        return carry

    lax.fori_loop(0, rounds[0], add_group, 0)
    out[...] = total[: RBLK * HALF, :].astype(BF16)


def multiply(rows, tiles, rounds, band, values):
    smem = pl.BlockSpec(memory_space=pltpu.SMEM)
    vmem = pl.BlockSpec(memory_space=pltpu.VMEM)
    return pl.pallas_call(
        multiply_kernel,
        in_specs=[smem, smem, smem, vmem, vmem],
        out_specs=vmem,
        out_shape=jax.ShapeDtypeStruct((RBLK * HALF, 128), BF16),
        scratch_shapes=[
            pltpu.VMEM((CBLK * 128, 128), BF16),
            pltpu.VMEM(((RBLK + 1) * HALF, 128), F32),
        ],
        compiler_params=pltpu.CompilerParams(vmem_limit_bytes=40 * 1024 * 1024),
        cost_estimate=pl.CostEstimate(
            flops=2 * CAP * BS * BS * K, bytes_accessed=8 * 1024 * 1024, transcendentals=0
        ),
    )(rows, tiles, rounds, band, values)


def image_kernel(parts, panel, image, gram, spread):
    total = parts[0].astype(F32)
    for index in range(1, COLS):
        total = total + parts[index].astype(F32)
    points = total.shape[0]
    spread[pl.ds(0, points, stride=2), :] = total
    spread[pl.ds(1, points, stride=2), :] = pltpu.roll(total, BS, 1)
    whole = spread[...].T[:K, :] + panel[...].astype(F32)
    image[...] = whole
    gram[...] = lax.dot_general(
        whole,
        whole,
        (((1,), (1,)), ((), ())),
        precision=lax.Precision.HIGHEST,
        preferred_element_type=F32,
    ) * (1.0 / POINTS)


def finish_image(parts, panel):
    vmem = pl.BlockSpec(memory_space=pltpu.VMEM)
    return pl.pallas_call(
        image_kernel,
        in_specs=[vmem, vmem],
        out_specs=[vmem, vmem],
        out_shape=[
            jax.ShapeDtypeStruct((K, PIECE), F32),
            jax.ShapeDtypeStruct((K, K), F32),
        ],
        scratch_shapes=[pltpu.VMEM((PIECE, 128), F32)],
        compiler_params=pltpu.CompilerParams(vmem_limit_bytes=16 * 1024 * 1024),
    )(parts, panel)


def gather_band(panel):
    pieces = []
    for turn in range(4):
        pairs = []
        for z in range(4):
            for core in range(2):
                for col in range(COLS):
                    piece = core * 4 + (z - turn) % 4
                    source = (col // 2) * COLS + 8 * (col % 2) + piece
                    pairs.append((source, (z * 2 + core) * COLS + col))
        pieces.append(lax.ppermute(panel, AXES, pairs))
    own = jnp.stack(pieces)
    return lax.all_gather(own, "core", axis=0, tiled=True)


def sum_along(value, axis, size):
    arrived = [
        lax.ppermute(value, axis, [(i, (i + shift) % size) for i in range(size)])
        for shift in range(1, size)
    ]
    if size == 2:
        return value + arrived[0]
    return (value + arrived[1]) + (arrived[0] + arrived[2])


def per_device(panel, block_values, row_starts, block_columns, block_counts):
    band = gather_band(panel)
    values = relayout_values(block_values)
    positions = lax.iota(jnp.int32, CAP)
    block_rows = jnp.sum((row_starts[None, :] <= positions[:, None]).astype(jnp.int32), axis=1) - 1
    count = block_counts[0]
    rows = jnp.where(positions < count, block_rows, RBLK)
    piece = block_columns // (PIECE // BS)
    turn = (lax.axis_index("z") - piece) % 4
    tiles = ((piece // 4) * 4 + turn) * (PIECE // BS) + block_columns % (PIECE // BS)
    rounds = (block_counts + UNROLL - 1) // UNROLL
    partial = multiply(rows, tiles, rounds, band, values)
    parts = lax.all_to_all(
        partial.reshape(COLS, PIECE // 2, 128), COL, split_axis=0, concat_axis=0, tiled=True
    )
    image, gram = finish_image(parts, panel)
    gram = sum_along(gram, "core", 2)
    for axis in ("x", "y", "z"):
        gram = sum_along(gram, axis, 4)
    factor = jnp.linalg.cholesky(gram)
    basis = jax.scipy.linalg.solve_triangular(factor, image, lower=True)
    return (basis, factor)


def solution(mesh):
    fine = Mesh(mesh.devices.reshape(4, 2, 4, 4), AXES)
    in_specs = (P(None, AXES), P(AXES, None), P(AXES), P(AXES), P(AXES))
    out_specs = (P(None, AXES), P())
    return jax.shard_map(
        per_device, mesh=fine, in_specs=in_specs, out_specs=out_specs, check_vma=False
    )
```

time: 424 us -> 171 us (0.40)
  waiting for transfers between devices: 233 us -> 43.7 us
  local copies, waits for them, and re-layouts: 64.3 us -> 7.71 us
  starting transfers between devices: 0.08 us -> 41.1 us
  blocking collectives: 65 us -> 34.7 us
  other arithmetic: 31.9 us -> 13.8 us
  Pallas kernels: 0 us -> 15.2 us
  matrix products: 12.9 us -> 1.13 us
    reduce_scatter x1 -> x0, waiting for transfers between devices: 145 us -> none  [per_device(): lax.psum_scatter(partial_value.astype(jnp.bfloat16), 'col', scatter_dimen...]
    all_gather x1, waiting for transfers between devices: 87.1 us -> 22.1 us  [gather_band(): return lax.all_gather(own, 'core', axis=0, tiled=True)]
    psum x1 -> x0, blocking collectives: 65 us -> none  [per_device(): gram = lax.psum(local_gram, ('row', 'col'))]
    ppermute x0 -> x14, starting transfers between devices: none -> 41 us  [the longest x10 22.3 us: sum_along(): lax.ppermute(value, axis, [(i, (i + shift) % size) for i in range(size)])]
    all_to_all x0 -> x1, blocking collectives: none -> 34.7 us  [per_device(): lax.all_to_all(partial.reshape(COLS, PIECE // 2, 128), COL, split_axis=0,...]
    ppermute x0 -> x14, waiting for transfers between devices: none -> 21.7 us  [the longest x10 12.5 us: sum_along(): lax.ppermute(value, axis, [(i, (i + shift) % size) for i in range(size)])]
    reshape x5 -> x0, local copies, waits for them, and re-layouts: 15.5 us -> none  [the longest x2 9.4 us: add_group(): lax.dynamic_slice_in_dim(block_values, first, GROUP, 0)]
    pallas_call x0 -> x3, Pallas kernels: none -> 15.2 us  [the longest x1 7.22 us: relayout_values(): pl.pallas_call(values_kernel, grid=(CAP // step,), in_specs=[pl.BlockSpec...]
  transfers between devices with their start and end apart: 2 -> 15, of which waited for: 2 -> 11; matrix products, arithmetic and copies ran while one was open for 0% -> 0% of each run, Pallas kernels for 0% -> 4%
where the time goes in v1:
time: 171 us; the launch traced here: 172 us
  waiting for transfers between devices  43.7 us (26%)
  starting transfers between devices  41.1 us (24%)
  blocking collectives  34.7 us (20%)
  Pallas kernels  15.2 us (9%)
  between operations  14.8 us (9%)
  other arithmetic  13.8 us (8%)
  local copies, waits for them, and re-layouts  7.71 us (5%)
    all_to_all x1, blocking collectives, per_device(): lax.all_to_all(partial.reshape(COLS, PIECE // 2, 128), COL, split_axis=0,...  34.7 us
    ppermute x10, starting transfers between devices, sum_along(): lax.ppermute(value, axis, [(i, (i + shift) % size) for i in range(size)])  22.3 us
    all_gather x1, waiting for transfers between devices, gather_band(): return lax.all_gather(own, 'core', axis=0, tiled=True)  22.1 us
    ppermute x4, starting transfers between devices, gather_band(): pieces.append(lax.ppermute(panel, AXES, pairs))  18.7 us
    ppermute x10, waiting for transfers between devices, sum_along(): lax.ppermute(value, axis, [(i, (i + shift) % size) for i in range(size)])  12.5 us
    ppermute x4, waiting for transfers between devices, gather_band(): pieces.append(lax.ppermute(panel, AXES, pairs))  9.2 us
    unnamed x14, local copies, waits for them, and re-layouts  7.56 us
    pallas_call x1, Pallas kernels, relayout_values(): pl.pallas_call(values_kernel, grid=(CAP // step,), in_specs=[pl.BlockSpec...  7.22 us
  transfers between devices with their start and end apart: 15, of which 11 were waited for; matrix products, arithmetic and copies ran while one was open for 0% of the time, Pallas kernels for 4%

profile of v1, /device:TPU:0, one launch (start us, length us, event | category | flops | bytes accessed | tf_op | source)
XLA Modules:
  0.0 172.1 jit_solution(9668966481483862034)
XLA Ops:
  7.2 4.0 %collective-permute-start.2 = (bf16[64,1024]{1,0:T(8,128)(2,1)}, bf16[64,1024]{1,0:T(8,128)(2,1)S(1)}, u32[]{:S(2)}, u32[]{:S(2)}) collective-permute-start(bf16[64,1024]{1,0:T(8,128)(2,1)} %panel.1), channel_id=1, source_target_pairs={{2,0},{10,1},{18,2},{26,3},{34,4},{42,5},{50,6},{58,7},{66,8},{74,... | collective-permute-start | bytes 393224 | tf_op jit(solution)/shard_map/ppermute | solution.py:147
  11.2 2.9 %collective-permute-start.1 = (bf16[64,1024]{1,0:T(8,128)(2,1)}, bf16[64,1024]{1,0:T(8,128)(2,1)S(1)}, u32[]{:S(2)}, u32[]{:S(2)}) collective-permute-start(bf16[64,1024]{1,0:T(8,128)(2,1)} %panel.1), channel_id=1, source_target_pairs={{3,0},{11,1},{19,2},{27,3},{35,4},{43,5},{51,6},{59,7},{67,8},{75,... | collective-permute-start | bytes 393224 | tf_op jit(solution)/shard_map/ppermute | solution.py:147
  14.1 1.6 collective-permute-start
  15.7 10.2 %collective-permute-start.3 = (bf16[64,1024]{1,0:T(8,128)(2,1)}, bf16[64,1024]{1,0:T(8,128)(2,1)S(1)}, u32[]{:S(2)}, u32[]{:S(2)}) collective-permute-start(bf16[64,1024]{1,0:T(8,128)(2,1)} %panel.1), channel_id=1, source_target_pairs={{1,0},{9,1},{17,2},{25,3},{33,4},{41,5},{49,6},{57,7},{65,8},{73,9... | collective-permute-start | bytes 393224 | tf_op jit(solution)/shard_map/ppermute | solution.py:147
  25.9 9.2 %collective-permute-done.1 = bf16[64,1024]{1,0:T(8,128)(2,1)S(1)} collective-permute-done((bf16[64,1024]{1,0:T(8,128)(2,1)}, bf16[64,1024]{1,0:T(8,128)(2,1)S(1)}, u32[]{:S(2)}, u32[]{:S(2)}) %collective-permute-start.1) | collective-permute-done | bytes 131104 | tf_op jit(solution)/shard_map/ppermute | solution.py:147
  36.8 2.2 %copy-done.2 = bf16[512,4096]{1,0:T(8,128)(2,1)S(1)} copy-done((bf16[512,4096]{1,0:T(8,128)(2,1)S(1)}, bf16[512,4096]{1,0:T(8,128)(2,1)}, u32[]{:S(2)}) %copy-start.2) | copy-done | bytes 4194328
  38.9 7.2 %shard_map.68.values = bf16[16384,128]{1,0:T(8,128)(2,1)S(1)} custom-call(bf16[512,4096]{1,0:T(8,128)(2,1)S(1)} %copy-done.2), custom_call_target="tpu_custom_call" | custom-call | bytes 8388608 | tf_op jit(solution)/shard_map/pallas_call | solution.py:36
  46.2 1.9 %copy-done = bf16[16384,128]{1,0:T(8,128)(2,1)} copy-done((bf16[16384,128]{1,0:T(8,128)(2,1)}, bf16[16384,128]{1,0:T(8,128)(2,1)S(1)}, u32[]{:S(2)}) %copy-start) | copy-done | bytes 4194328
  48.3 22.1 %all-gather.2.cloned.1.call-done.band = bf16[8,64,1024]{2,1,0:T(8,128)(2,1)} async-done(((bf16[4,64,1024]{2,1,0:T(8,128)(2,1)}), bf16[8,64,1024]{2,1,0:T(8,128)(2,1)}) %all-gather.2.cloned.1.call-update) | async-done | bytes 1048592 | tf_op jit(solution)/shard_map/all_gather | solution.py:149
  70.4 2.2 %copy-done.1 = bf16[16384,128]{1,0:T(8,128)(2,1)S(1)} copy-done((bf16[16384,128]{1,0:T(8,128)(2,1)S(1)}, bf16[16384,128]{1,0:T(8,128)(2,1)}, u32[]{:S(2)}) %copy-start.1) | copy-done | bytes 4194328
  73.8 7.1 %shard_map.69 = bf16[8192,128]{1,0:T(8,128)(2,1)S(1)} custom-call(s32[512]{0:T(512)S(1)} %get-tuple-element.9.rows, s32[512]{0:T(512)S(1)} %get-tuple-element.8.tiles, s32[1]{0:T(128)S(6)} %select_n.37.rounds, bf16[8,64,1024]{2,1,0:T(8,128)(2,1)S(1)} %copy-done.3, bf16[16384,128]{1,0:T(8,128)(2,1)S(1)} %copy-done.1), custom_call_target="tpu_custom_call" | custom-call | flops 268435456 | bytes 8388608 | tf_op jit(solution)/shard_map/pallas_call | solution.py:88
  80.9 34.7 %all_to_all.5.parts = bf16[16,512,128]{2,1,0:T(8,128)(2,1)S(1)} all-to-all(bf16[16,512,128]{2,1,0:T(8,128)(2,1)S(1)} %bitcast.17), channel_id=1, replica_groups=mesh['z'=4,'core'=2,'y'=4,'x'=4] {'y','x'}, dimensions={0} | all-to-all | bytes 4194304 | tf_op jit(solution)/shard_map/all_to_all | solution.py:174
  116.6 2.1 %collective-permute-start.4 = (f32[64,64]{0,1:T(8,128)S(1)}, f32[64,64]{0,1:T(8,128)S(1)}, u32[]{:S(2)}, u32[]{:S(2)}) collective-permute-start(f32[64,64]{0,1:T(8,128)S(1)} %copy.14), channel_id=1, source_target_pairs={{0,16},{16,0},{1,17},{17,1},{2,18},{18,2},{3,19},{19,3},{4,20},{20... | collective-permute-start | bytes 49160 | tf_op jit(solution)/shard_map/ppermute | solution.py:154
  119.5 2.0 %collective-permute-start.6 = (f32[64,64]{0,1:T(8,128)S(1)}, f32[64,64]{0,1:T(8,128)S(1)}, u32[]{:S(2)}, u32[]{:S(2)}) collective-permute-start(f32[64,64]{0,1:T(8,128)S(1)} %add.70), channel_id=1, source_target_pairs={{0,1},{1,2},{2,3},{3,0},{4,5},{5,6},{6,7},{7,4},{8,9},{9,10},{10,1... | collective-permute-start | bytes 49160 | tf_op jit(solution)/shard_map/ppermute | solution.py:154
  122.1 1.3 collective-permute-done.7
  124.7 2.2 %collective-permute-done.5 = f32[64,64]{0,1:T(8,128)S(1)} collective-permute-done((f32[64,64]{0,1:T(8,128)S(1)}, f32[64,64]{0,1:T(8,128)S(1)}, u32[]{:S(2)}, u32[]{:S(2)}) %collective-permute-start.5) | collective-permute-done | bytes 16416 | tf_op jit(solution)/shard_map/ppermute | solution.py:154
  127.3 1.7 collective-permute-start.9
  130.9 1.5 collective-permute-done.9
  132.5 2.0 %collective-permute-done.8 = f32[64,64]{0,1:T(8,128)S(1)} collective-permute-done((f32[64,64]{0,1:T(8,128)S(1)}, f32[64,64]{0,1:T(8,128)S(1)}, u32[]{:S(2)}, u32[]{:S(2)}) %collective-permute-start.8) | collective-permute-done | bytes 16416 | tf_op jit(solution)/shard_map/ppermute | solution.py:154
  134.5 3.7 %collective-permute-start.13 = (f32[64,64]{0,1:T(8,128)S(1)}, f32[64,64]{0,1:T(8,128)S(1)}, u32[]{:S(2)}, u32[]{:S(2)}) collective-permute-start(f32[64,64]{0,1:T(8,128)S(1)} %add_add_fusion.1), channel_id=1, source_target_pairs={{0,96},{32,0},{64,32},{96,64},{1,97},{33,1},{65,33},{97,65},{2,98}... | collective-permute-start | bytes 49160 | tf_op jit(solution)/shard_map/ppermute | solution.py:154
  138.2 10.9 %collective-permute-start.11 = (f32[64,64]{0,1:T(8,128)S(1)}, f32[64,64]{0,1:T(8,128)S(1)}, u32[]{:S(2)}, u32[]{:S(2)}) collective-permute-start(f32[64,64]{0,1:T(8,128)S(1)} %add_add_fusion.1), channel_id=1, source_target_pairs={{0,64},{32,96},{64,0},{96,32},{1,65},{33,97},{65,1},{97,33},{2,66}... | collective-permute-start | bytes 49160 | tf_op jit(solution)/shard_map/ppermute | solution.py:154
  149.6 1.8 %collective-permute-done.11 = f32[64,64]{0,1:T(8,128)S(1)} collective-permute-done((f32[64,64]{0,1:T(8,128)S(1)}, f32[64,64]{0,1:T(8,128)S(1)}, u32[]{:S(2)}, u32[]{:S(2)}) %collective-permute-start.11) | collective-permute-done | bytes 16416 | tf_op jit(solution)/shard_map/ppermute | solution.py:154
  151.5 5.8 %cholesky.16 = f32[64,64]{1,0:T(8,128)S(1)} custom-call(f32[64,64]{1,0:T(8,128)S(1)} %fusion.2), custom_call_target="Cholesky" | custom-call | tf_op jit(solution)/shard_map/jit(cholesky)/cholesky | solution.py:181
  159.3 4.9 %custom-call.7 = f32[1,64,64]{1,2,0:T(8,128)S(1)} custom-call(f32[1,64,64]{2,1,0:T(8,128)S(1)} %get-tuple-element.6), custom_call_target="InvertDiagBlocksLowerTriangular" | custom-call | tf_op jit(solution)/shard_map/jit(_solve_triangular)/triangular_solve | solution.py:182
  (41 shorter events, 11.9 us)
Async XLA Ops:
  7.2 63.2 %all-gather.2.cloned.1.call-start = ((), (), s32[]{:S(2)}) async-start(), calls=%async_computation.1 | async-start | bytes 1572864 | tf_op jit(solution)/shard_map/all_gather | solution.py:149
  7.2 18.7 %collective-permute-start.2 = (bf16[64,1024]{1,0:T(8,128)(2,1)}, bf16[64,1024]{1,0:T(8,128)(2,1)S(1)}, u32[]{:S(2)}, u32[]{:S(2)}) collective-permute-start(bf16[64,1024]{1,0:T(8,128)(2,1)} %panel.1), channel_id=1, source_target_pairs={{2,0},{10,1},{18,2},{26,3},{34,4},{42,5},{50,6},{58,7},{66,8},{74,... | collective-permute-start | bytes 393224 | tf_op jit(solution)/shard_map/ppermute | solution.py:147
  11.2 23.9 %collective-permute-start.1 = (bf16[64,1024]{1,0:T(8,128)(2,1)}, bf16[64,1024]{1,0:T(8,128)(2,1)S(1)}, u32[]{:S(2)}, u32[]{:S(2)}) collective-permute-start(bf16[64,1024]{1,0:T(8,128)(2,1)} %panel.1), channel_id=1, source_target_pairs={{3,0},{11,1},{19,2},{27,3},{35,4},{43,5},{51,6},{59,7},{67,8},{75,... | collective-permute-start | bytes 393224 | tf_op jit(solution)/shard_map/ppermute | solution.py:147
  14.1 21.0 %collective-permute-start = (bf16[64,1024]{1,0:T(8,128)(2,1)}, bf16[64,1024]{1,0:T(8,128)(2,1)S(1)}, u32[]{:S(2)}, u32[]{:S(2)}) collective-permute-start(bf16[64,1024]{1,0:T(8,128)(2,1)} %panel.1), channel_id=1, source_target_pairs={{0,0},{8,1},{16,2},{24,3},{32,4},{40,5},{48,6},{56,7},{64,8},{72,9... | collective-permute-start | bytes 393224 | tf_op jit(solution)/shard_map/ppermute | solution.py:147
  15.7 19.5 %collective-permute-start.3 = (bf16[64,1024]{1,0:T(8,128)(2,1)}, bf16[64,1024]{1,0:T(8,128)(2,1)S(1)}, u32[]{:S(2)}, u32[]{:S(2)}) collective-permute-start(bf16[64,1024]{1,0:T(8,128)(2,1)} %panel.1), channel_id=1, source_target_pairs={{1,0},{9,1},{17,2},{25,3},{33,4},{41,5},{49,6},{57,7},{65,8},{73,9... | collective-permute-start | bytes 393224 | tf_op jit(solution)/shard_map/ppermute | solution.py:147
  36.7 2.2 %copy-start.2 = (bf16[512,4096]{1,0:T(8,128)(2,1)S(1)}, bf16[512,4096]{1,0:T(8,128)(2,1)}, u32[]{:S(2)}) copy-start(bf16[512,4096]{1,0:T(8,128)(2,1)} %values.1) | copy-start | bytes 12582916
  38.9 9.2 %copy-start.6 = (s32[256]{0:T(256)S(1)}, s32[256]{0:T(256)}, u32[]{:S(2)}) copy-start(s32[256]{0:T(256)} %param.7) | copy-start | bytes 3076
  38.9 9.3 %copy-start.5 = (s32[512]{0:T(512)S(1)}, s32[512]{0:T(512)}, u32[]{:S(2)}) copy-start(s32[512]{0:T(512)} %param.8) | copy-start | bytes 6148
  46.2 2.0 %copy-start = (bf16[16384,128]{1,0:T(8,128)(2,1)}, bf16[16384,128]{1,0:T(8,128)(2,1)S(1)}, u32[]{:S(2)}) copy-start(bf16[16384,128]{1,0:T(8,128)(2,1)S(1)} %shard_map.68.values) | copy-start | bytes 12582916
  70.4 2.2 %copy-start.1 = (bf16[16384,128]{1,0:T(8,128)(2,1)S(1)}, bf16[16384,128]{1,0:T(8,128)(2,1)}, u32[]{:S(2)}) copy-start(bf16[16384,128]{1,0:T(8,128)(2,1)} %copy-done) | copy-start | bytes 12582916
  72.5 1.2 copy-start.3
  73.8 41.9 %copy-start.4 = (bf16[64,1024]{1,0:T(8,128)(2,1)S(1)}, bf16[64,1024]{1,0:T(8,128)(2,1)}, u32[]{:S(2)}) copy-start(bf16[64,1024]{1,0:T(8,128)(2,1)} %panel.1) | copy-start | bytes 393220
  116.6 2.9 %collective-permute-start.4 = (f32[64,64]{0,1:T(8,128)S(1)}, f32[64,64]{0,1:T(8,128)S(1)}, u32[]{:S(2)}, u32[]{:S(2)}) collective-permute-start(f32[64,64]{0,1:T(8,128)S(1)} %copy.14), channel_id=1, source_target_pairs={{0,16},{16,0},{1,17},{17,1},{2,18},{18,2},{3,19},{19,3},{4,20},{20... | collective-permute-start | bytes 49160 | tf_op jit(solution)/shard_map/ppermute | solution.py:154
  119.5 3.9 %collective-permute-start.7 = (f32[64,64]{0,1:T(8,128)S(1)}, f32[64,64]{0,1:T(8,128)S(1)}, u32[]{:S(2)}, u32[]{:S(2)}) collective-permute-start(f32[64,64]{0,1:T(8,128)S(1)} %add.70), channel_id=1, source_target_pairs={{0,3},{1,0},{2,1},{3,2},{4,7},{5,4},{6,5},{7,6},{8,11},{9,8},{10,9... | collective-permute-start | bytes 49160 | tf_op jit(solution)/shard_map/ppermute | solution.py:154
  119.5 5.2 %collective-permute-start.6 = (f32[64,64]{0,1:T(8,128)S(1)}, f32[64,64]{0,1:T(8,128)S(1)}, u32[]{:S(2)}, u32[]{:S(2)}) collective-permute-start(f32[64,64]{0,1:T(8,128)S(1)} %add.70), channel_id=1, source_target_pairs={{0,1},{1,2},{2,3},{3,0},{4,5},{5,6},{6,7},{7,4},{8,9},{9,10},{10,1... | collective-permute-start | bytes 49160 | tf_op jit(solution)/shard_map/ppermute | solution.py:154
  121.5 5.4 %collective-permute-start.5 = (f32[64,64]{0,1:T(8,128)S(1)}, f32[64,64]{0,1:T(8,128)S(1)}, u32[]{:S(2)}, u32[]{:S(2)}) collective-permute-start(f32[64,64]{0,1:T(8,128)S(1)} %add.70), channel_id=1, source_target_pairs={{0,2},{1,3},{2,0},{3,1},{4,6},{5,7},{6,4},{7,5},{8,10},{9,11},{10,... | collective-permute-start | bytes 49160 | tf_op jit(solution)/shard_map/ppermute | solution.py:154
  127.0 4.0 %collective-permute-start.10 = (f32[64,64]{0,1:T(8,128)S(1)}, f32[64,64]{0,1:T(8,128)S(1)}, u32[]{:S(2)}, u32[]{:S(2)}) collective-permute-start(f32[64,64]{0,1:T(8,128)S(1)} %add_add_fusion.2), channel_id=1, source_target_pairs={{0,12},{4,0},{8,4},{12,8},{1,13},{5,1},{9,5},{13,9},{2,14},{6,2},{... | collective-permute-start | bytes 49160 | tf_op jit(solution)/shard_map/ppermute | solution.py:154
  127.3 5.1 %collective-permute-start.9 = (f32[64,64]{0,1:T(8,128)S(1)}, f32[64,64]{0,1:T(8,128)S(1)}, u32[]{:S(2)}, u32[]{:S(2)}) collective-permute-start(f32[64,64]{0,1:T(8,128)S(1)} %add_add_fusion.2), channel_id=1, source_target_pairs={{0,4},{4,8},{8,12},{12,0},{1,5},{5,9},{9,13},{13,1},{2,6},{6,10},{... | collective-permute-start | bytes 49160 | tf_op jit(solution)/shard_map/ppermute | solution.py:154
  129.1 5.4 %collective-permute-start.8 = (f32[64,64]{0,1:T(8,128)S(1)}, f32[64,64]{0,1:T(8,128)S(1)}, u32[]{:S(2)}, u32[]{:S(2)}) collective-permute-start(f32[64,64]{0,1:T(8,128)S(1)} %add_add_fusion.2), channel_id=1, source_target_pairs={{0,8},{4,12},{8,0},{12,4},{1,9},{5,13},{9,1},{13,5},{2,10},{6,14},... | collective-permute-start | bytes 49160 | tf_op jit(solution)/shard_map/ppermute | solution.py:154
  134.5 14.6 %collective-permute-start.13 = (f32[64,64]{0,1:T(8,128)S(1)}, f32[64,64]{0,1:T(8,128)S(1)}, u32[]{:S(2)}, u32[]{:S(2)}) collective-permute-start(f32[64,64]{0,1:T(8,128)S(1)} %add_add_fusion.1), channel_id=1, source_target_pairs={{0,96},{32,0},{64,32},{96,64},{1,97},{33,1},{65,33},{97,65},{2,98}... | collective-permute-start | bytes 49160 | tf_op jit(solution)/shard_map/ppermute | solution.py:154
  138.2 11.4 %collective-permute-start.12 = (f32[64,64]{0,1:T(8,128)S(1)}, f32[64,64]{0,1:T(8,128)S(1)}, u32[]{:S(2)}, u32[]{:S(2)}) collective-permute-start(f32[64,64]{0,1:T(8,128)S(1)} %add_add_fusion.1), channel_id=1, source_target_pairs={{0,32},{32,64},{64,96},{96,0},{1,33},{33,65},{65,97},{97,1},{2,34}... | collective-permute-start | bytes 49160 | tf_op jit(solution)/shard_map/ppermute | solution.py:154
  138.2 13.2 %collective-permute-start.11 = (f32[64,64]{0,1:T(8,128)S(1)}, f32[64,64]{0,1:T(8,128)S(1)}, u32[]{:S(2)}, u32[]{:S(2)}) collective-permute-start(f32[64,64]{0,1:T(8,128)S(1)} %add_add_fusion.1), channel_id=1, source_target_pairs={{0,64},{32,96},{64,0},{96,32},{1,65},{33,97},{65,1},{97,33},{2,66}... | collective-permute-start | bytes 49160 | tf_op jit(solution)/shard_map/ppermute | solution.py:154
Sparse Core Ops, SparseCore 0:
  36.2 34.1 all-gather.1

commit v2 on v1

v2 whole, which is shorter than its diff:
```python
import jax
import jax.numpy as jnp
from jax import lax
from jax.experimental import pallas as pl
from jax.experimental.pallas import tpu as pltpu
from jax.sharding import Mesh
from jax.sharding import PartitionSpec as P

K = 64
BS = 64
CAP = 512
RBLK = 256
CBLK = 128
PIECE = 1024
POINTS = 131072
COLS = 16
HALF = BS // 2
PART = 256
UNROLL = 8
AXES = ("z", "core", "y", "x")
F32 = jnp.float32
BF16 = jnp.bfloat16


def values_kernel(values, out, token, spread):
    for group in range(values.shape[0] // 16):
        for tile in range(HALF):
            part = values[group * 16 : (group + 1) * 16, tile * 128 : (tile + 1) * 128]
            spread[pl.ds(tile, 16, stride=HALF), :] = part.astype(F32)
        out[group * 16 * HALF : (group + 1) * 16 * HALF, :] = spread[...].astype(BF16)
    token[...] = jnp.zeros_like(token)


def relayout_values(block_values):
    step = 64
    return pl.pallas_call(
        values_kernel,
        grid=(CAP // step,),
        in_specs=[pl.BlockSpec((step, BS * BS), lambda i: (i, 0))],
        out_specs=[
            pl.BlockSpec((step * HALF, 128), lambda i: (i, 0)),
            pl.BlockSpec((K, 128), lambda i: (0, 0)),
        ],
        out_shape=[
            jax.ShapeDtypeStruct((CAP * HALF, 128), BF16),
            jax.ShapeDtypeStruct((K, 128), BF16),
        ],
        scratch_shapes=[pltpu.VMEM((16 * HALF, 128), F32)],
        compiler_params=pltpu.CompilerParams(vmem_limit_bytes=16 * 1024 * 1024),
        cost_estimate=pl.CostEstimate(flops=0, bytes_accessed=24 * 1024 * 1024, transcendentals=0),
    )(block_values)


def multiply_kernel(place, rows, tiles, rounds, own, other, stored, *rest):
    outs, (weights, total, values, sem) = rest[:8], rest[8:]
    copy = pltpu.make_async_copy(stored, values, sem)
    copy.start()
    low = lax.broadcasted_iota(jnp.int32, (K, 128), 1) < BS
    zero = jnp.zeros((K, 128), F32)

    for side, band in enumerate((own, other)):

        def fill(piece, carry):
            for lane in range(PIECE // 128):
                pair = band[piece, :, lane * 128 : (lane + 1) * 128].astype(F32)
                swapped = pltpu.roll(pair, BS, 1)
                tile = (side * 4 + piece) * (PIECE // BS) + 2 * lane
                first = pl.multiple_of(tile * 128, 128)
                weights[pl.ds(first, 64), :] = jnp.where(low, pair, zero).astype(BF16)
                weights[pl.ds(first + 64, 64), :] = jnp.where(low, zero, swapped).astype(BF16)
                weights[pl.ds(first + 128, 64), :] = jnp.where(low, swapped, zero).astype(BF16)
                weights[pl.ds(first + 192, 64), :] = jnp.where(low, zero, pair).astype(BF16)
            return carry

        lax.fori_loop(0, 4, fill, 0)
    total[...] = jnp.zeros_like(total)
    copy.wait()

    def add_group(index, carry):
        products = []
        for offset in range(UNROLL):
            slot = index * UNROLL + offset
            block = values[pl.ds(pl.multiple_of(slot * HALF, HALF), HALF), :]
            tile = weights[pl.ds(pl.multiple_of(tiles[slot] * 128, 128), 128), :]
            products.append(
                lax.dot_general(block, tile, (((1,), (1,)), ((), ())), preferred_element_type=F32)
            )
        for offset in range(UNROLL):
            slot = index * UNROLL + offset
            where = pl.ds(pl.multiple_of(rows[slot] * HALF, HALF), HALF)
            total[where, :] = total[where, :] + products[offset]
        return carry

    lax.fori_loop(0, rounds[0], add_group, 0)
    y, x = place[0], place[1]
    for shift in range(4):
        to_x = lax.rem(x + shift, 4)
        to_y = lax.rem(y + shift, 4)
        for index in range(4):
            first = pl.multiple_of((index * 4 + to_x) * 2 * PART, PART)
            outs[shift][index] = total[pl.ds(first, PART), :].astype(BF16)
            first = pl.multiple_of((to_y * 4 + index) * 2 * PART + PART, PART)
            outs[4 + shift][index] = total[pl.ds(first, PART), :].astype(BF16)


def multiply(place, rows, tiles, rounds, own, other, values):
    smem = pl.BlockSpec(memory_space=pltpu.SMEM)
    vmem = pl.BlockSpec(memory_space=pltpu.VMEM)
    return pl.pallas_call(
        multiply_kernel,
        in_specs=[smem] * 4 + [vmem, vmem, pl.BlockSpec(memory_space=pl.ANY)],
        out_specs=[vmem] * 8,
        out_shape=[jax.ShapeDtypeStruct((4, PART, 128), BF16)] * 8,
        scratch_shapes=[
            pltpu.VMEM((CBLK * 128, 128), BF16),
            pltpu.VMEM(((RBLK + 1) * HALF, 128), F32),
            pltpu.VMEM((CAP * HALF, 128), BF16),
            pltpu.SemaphoreType.DMA,
        ],
        compiler_params=pltpu.CompilerParams(vmem_limit_bytes=40 * 1024 * 1024),
        cost_estimate=pl.CostEstimate(
            flops=2 * CAP * BS * BS * K, bytes_accessed=8 * 1024 * 1024, transcendentals=0
        ),
    )(place, rows, tiles, rounds, own, other, values)


def stage_kernel(place, *refs):
    ins, outs = refs[:8], refs[8:]
    for half in range(2):
        base = place[half]
        for shift in range(4):
            to = lax.rem(base + shift, 4)
            total = ins[half * 4][to].astype(F32)
            for index in range(1, 4):
                total = total + ins[half * 4 + index][to].astype(F32)
            outs[half * 4 + shift][...] = total.astype(outs[half * 4 + shift].dtype)


def stage_sums(place, arrays):
    vmem = pl.BlockSpec(memory_space=pltpu.VMEM)
    shapes = [jax.ShapeDtypeStruct((PART, 128), F32)]
    shapes += [jax.ShapeDtypeStruct((PART, 128), BF16)] * 3
    return pl.pallas_call(
        stage_kernel,
        in_specs=[pl.BlockSpec(memory_space=pltpu.SMEM)] + [vmem] * 8,
        out_specs=[vmem] * 8,
        out_shape=shapes * 2,
        compiler_params=pltpu.CompilerParams(vmem_limit_bytes=16 * 1024 * 1024),
    )(place, *arrays)


def image_kernel(*refs):
    ins, (panel, image, gram, spread) = refs[:8], refs[8:]
    for half in range(2):
        total = ins[half * 4][...]
        for index in range(1, 4):
            total = total + ins[half * 4 + index][...].astype(F32)
        spread[pl.ds(half * 2 * PART, PART, stride=2), :] = total
        spread[pl.ds(half * 2 * PART + 1, PART, stride=2), :] = pltpu.roll(total, BS, 1)
    whole = spread[...].T[:K, :] + panel[...].astype(F32)
    image[...] = whole
    gram[...] = lax.dot_general(
        whole,
        whole,
        (((1,), (1,)), ((), ())),
        precision=lax.Precision.HIGHEST,
        preferred_element_type=F32,
    ) * (1.0 / POINTS)


def finish_image(arrays, panel):
    vmem = pl.BlockSpec(memory_space=pltpu.VMEM)
    return pl.pallas_call(
        image_kernel,
        in_specs=[vmem] * 9,
        out_specs=[vmem, vmem],
        out_shape=[
            jax.ShapeDtypeStruct((K, PIECE), F32),
            jax.ShapeDtypeStruct((K, K), F32),
        ],
        scratch_shapes=[pltpu.VMEM((PIECE, 128), F32)],
        compiler_params=pltpu.CompilerParams(vmem_limit_bytes=16 * 1024 * 1024),
    )(*arrays, panel)


def basis_kernel(g0, g1, g2, g3, image, basis, factor, work):
    gram = (g0[...] + g2[...]) + (g1[...] + g3[...])
    work[...] = jnp.zeros_like(work)
    work[:, :K] = gram
    lane = lax.broadcasted_iota(jnp.int32, (8, 128), 1)
    sub = lax.broadcasted_iota(jnp.int32, (8, 128), 0)
    groups = []
    for g in range(8):
        shifted = pltpu.roll(work[g * 8 : (g + 1) * 8, :], K, 1)
        groups.append(jnp.where(lane == sub + g * 8, 1.0, shifted))
    for b in range(8):
        columns = []
        for j in range(8):
            at = K + b * 8 + j
            columns.append(
                [jnp.broadcast_to(groups[g][:, at : at + 1], (8, 128)) for g in range(b, 8)]
            )
        done = []
        for j in range(8):
            scale = lax.rsqrt(columns[j][0][j : j + 1, :])
            scaled = [c * scale for c in columns[j]]
            columns[j] = scaled
            for later in range(j + 1, 8):
                times = scaled[0][later : later + 1, :]
                columns[later] = [c - s * times for c, s in zip(columns[later], scaled)]
            row = groups[b][j : j + 1, :]
            for before in range(j):
                row = row - columns[before][0][j : j + 1, :] * done[before]
            done.append(row * scale)
        for g in range(b + 1, 8):
            value = groups[g]
            for j in range(8):
                value = value - columns[j][g - b] * done[j]
            groups[g] = value
        for j in range(8):
            work[b * 8 + j : b * 8 + j + 1, :] = done[j]
    final = work[...]
    rows = lax.broadcasted_iota(jnp.int32, (K, 128), 0)
    lanes = lax.broadcasted_iota(jnp.int32, (K, 128), 1)
    upper = jnp.where(lanes - K >= rows, final, 0.0)
    factor[...] = upper.T[K:, :]
    inverse = final[:, :K]
    basis[...] = lax.dot_general(
        inverse,
        image[...],
        (((1,), (0,)), ((), ())),
        precision=lax.Precision.HIGHEST,
        preferred_element_type=F32,
    )


def orthogonalize(grams, image):
    vmem = pl.BlockSpec(memory_space=pltpu.VMEM)
    return pl.pallas_call(
        basis_kernel,
        in_specs=[vmem] * 5,
        out_specs=[vmem, vmem],
        out_shape=[
            jax.ShapeDtypeStruct((K, PIECE), F32),
            jax.ShapeDtypeStruct((K, K), F32),
        ],
        scratch_shapes=[pltpu.VMEM((K, 128), F32)],
        compiler_params=pltpu.CompilerParams(vmem_limit_bytes=16 * 1024 * 1024),
    )(*grams, image)


def shifted(value, axis, shift, size=4):
    return lax.ppermute(value, axis, [(i, (i + shift) % size) for i in range(size)])


def gather_band(panel, token):
    pairs = []
    for z in range(4):
        for core in range(2):
            for y in range(4):
                for x in range(4):
                    source = (z * 2 + core) * COLS + y * 4 + x
                    target = ((z + y + x) % 4 * 2 + y % 2) * COLS + z * 4 + 2 * core + y // 2
                    pairs.append((source, target))
    piece = lax.ppermute(panel, AXES, pairs) + jnp.tile(token, (1, PIECE // 128))
    own = jnp.stack([piece] + [shifted(piece, "z", turn) for turn in range(1, 4)])
    return own, shifted(own, "core", 1, 2)


def sum_along(value, axis):
    near, across, far = (shifted(value, axis, shift) for shift in range(1, 4))
    return (value + across) + (near + far)


def per_device(panel, block_values, row_starts, block_columns, block_counts):
    z, core = lax.axis_index("z"), lax.axis_index("core")
    y, x = lax.axis_index("y"), lax.axis_index("x")
    place = jnp.stack([y, x]).astype(jnp.int32)
    values, token = relayout_values(block_values)
    own, other = gather_band(panel, token)
    positions = lax.iota(jnp.int32, CAP)
    block_rows = jnp.sum((row_starts[None, :] <= positions[:, None]).astype(jnp.int32), axis=1) - 1
    rows = jnp.where(positions < block_counts[0], block_rows, RBLK)
    piece = block_columns // (PIECE // BS)
    side, from_x = piece // 4, piece % 4
    turn = (z - y - (2 * (x % 2) + side) - from_x) % 4
    place_of = jnp.where(side == core, 0, 4) + turn
    tiles = place_of * (PIECE // BS) + block_columns % (PIECE // BS)
    rounds = (block_counts + UNROLL - 1) // UNROLL
    partial = multiply(place, rows, tiles, rounds, own, other, values)
    arrived = [partial[0]] + [shifted(partial[shift], "x", shift) for shift in range(1, 4)]
    arrived += [partial[4]] + [shifted(partial[4 + shift], "y", shift) for shift in range(1, 4)]
    sums = stage_sums(place, arrived)
    arrived = [sums[0]] + [shifted(sums[shift], "y", shift) for shift in range(1, 4)]
    arrived += [sums[4]] + [shifted(sums[4 + shift], "x", shift) for shift in range(1, 4)]
    image, gram = finish_image(arrived, panel)
    gram = gram + shifted(gram, "core", 1, 2)
    gram = sum_along(sum_along(gram, "x"), "y")
    grams = [gram] + [shifted(gram, "z", shift) for shift in range(1, 4)]
    basis, factor = orthogonalize(grams, image)
    return (basis, factor)


def solution(mesh):
    fine = Mesh(mesh.devices.reshape(4, 2, 4, 4), AXES)
    in_specs = (P(None, AXES), P(AXES, None), P(AXES), P(AXES), P(AXES))
    out_specs = (P(None, AXES), P())
    return jax.shard_map(
        per_device, mesh=fine, in_specs=in_specs, out_specs=out_specs, check_vma=False
    )
```

time: 171 us -> 113 us (0.66)
  blocking collectives: 34.7 us -> 0 us
  Pallas kernels: 15.2 us -> 29.8 us
  other arithmetic: 13.8 us -> 0.38 us
  between operations: 14.8 us -> 1.45 us
  starting transfers between devices: 41.1 us -> 34 us
  waiting for transfers between devices: 43.7 us -> 40.6 us
    all_to_all x1 -> x0, blocking collectives: 34.7 us -> none  [per_device(): lax.all_to_all(partial.reshape(COLS, PIECE // 2, 128), COL, split_axis=0,...]
    all_gather x1 -> x0, waiting for transfers between devices: 22.1 us -> none  [gather_band(): return lax.all_gather(own, 'core', axis=0, tiled=True)]
    ppermute x14 -> x27, waiting for transfers between devices: 21.7 us -> 40.6 us  [the longest x26 40.6 us: shifted(): lax.ppermute(value, axis, [(i, (i + shift) % size) for i in range(size)])]
    pallas_call x2 -> x4, Pallas kernels: 7.93 us -> 22.6 us  [the longest x1 18.3 us: multiply(): pl.pallas_call(multiply_kernel, in_specs=[smem] * 4 + [vmem, vmem, pl.Blo...]
    another operation x6 -> x2, other arithmetic: 13.6 us -> 0.14 us  [the longest x1 0.08 us: per_device(): place = jnp.stack([y, x]).astype(jnp.int32)]
    ppermute x14 -> x27, starting transfers between devices: 41 us -> 34 us  [the longest x26 32.4 us: shifted(): lax.ppermute(value, axis, [(i, (i + shift) % size) for i in range(size)])]
    unnamed x14 -> x12, local copies, waits for them, and re-layouts: 7.56 us -> 6.35 us
  transfers between devices with their start and end apart: 15 -> 27, of which waited for: 11 -> 18; matrix products, arithmetic and copies ran while one was open for 0% -> 0% of each run, Pallas kernels for 4% -> 6%
where the time goes in v2:
time: 113 us
  waiting for transfers between devices  40.6 us (36%)
  starting transfers between devices  34 us (30%)
  Pallas kernels  29.8 us (26%)
  local copies, waits for them, and re-layouts  6.36 us (6%)
  between operations  1.45 us (1%)
    ppermute x26, waiting for transfers between devices, shifted(): lax.ppermute(value, axis, [(i, (i + shift) % size) for i in range(size)])  40.6 us
    ppermute x26, starting transfers between devices, shifted(): lax.ppermute(value, axis, [(i, (i + shift) % size) for i in range(size)])  32.4 us
    pallas_call x1, Pallas kernels, multiply(): pl.pallas_call(multiply_kernel, in_specs=[smem] * 4 + [vmem, vmem, pl.Blo...  18.3 us
    pallas_call x1, Pallas kernels, relayout_values(): pl.pallas_call(values_kernel, grid=(CAP // step,), in_specs=[pl.BlockSpec...  7.24 us
    unnamed x12, local copies, waits for them, and re-layouts  6.35 us
    pallas_call x1, Pallas kernels, orthogonalize(): pl.pallas_call(basis_kernel, in_specs=[vmem] * 5, out_specs=[vmem, vmem],...  2.78 us
  transfers between devices with their start and end apart: 27, of which 18 were waited for; matrix products, arithmetic and copies ran while one was open for 0% of the time, Pallas kernels for 6%

profile of v2, /device:TPU:0, one launch (start us, length us, event | category | flops | bytes accessed | tf_op | source)
XLA Modules:
  0.0 112.6 jit_solution(7750942231248472334)
XLA Ops:
  0.6 1.6 %collective-permute-start = (bf16[64,1024]{1,0:T(8,128)(2,1)}, bf16[64,1024]{1,0:T(8,128)(2,1)S(1)}, u32[]{:S(2)}, u32[]{:S(2)}) collective-permute-start(bf16[64,1024]{1,0:T(8,128)(2,1)} %refs_8_.1), channel_id=1, source_target_pairs={{0,0},{1,32},{2,64},{3,96},{4,48},{5,80},{6,112},{7,16},{8,65},{9,... | collective-permute-start | bytes 393224 | tf_op jit(solution)/shard_map/ppermute | solution.py:265
  2.2 2.2 %copy-done.2 = bf16[512,4096]{1,0:T(8,128)(2,1)S(1)} copy-done((bf16[512,4096]{1,0:T(8,128)(2,1)S(1)}, bf16[512,4096]{1,0:T(8,128)(2,1)}, u32[]{:S(2)}) %copy-start.2) | copy-done | bytes 4194328
  4.4 7.2 %shard_map.68 = (bf16[16384,128]{1,0:T(8,128)(2,1)S(1)}, bf16[64,128]{1,0:T(8,128)(2,1)S(1)}) custom-call(bf16[512,4096]{1,0:T(8,128)(2,1)S(1)} %copy-done.2), custom_call_target="tpu_custom_call" | custom-call | bytes 25165824 | tf_op jit(solution)/shard_map/pallas_call | solution.py:36
  11.6 2.0 %copy-done = bf16[16384,128]{1,0:T(8,128)(2,1)} copy-done((bf16[16384,128]{1,0:T(8,128)(2,1)}, bf16[16384,128]{1,0:T(8,128)(2,1)S(1)}, u32[]{:S(2)}) %copy-start) | copy-done | bytes 4194328
  13.7 7.6 %collective-permute-start.3 = (bf16[64,1024]{1,0:T(8,128)(2,1)S(1)}, bf16[64,1024]{1,0:T(8,128)(2,1)S(1)}, u32[]{:S(2)}, u32[]{:S(2)}) collective-permute-start(bf16[64,1024]{1,0:T(8,128)(2,1)S(1)} %bitcast_add_fusion), channel_id=1, source_target_pairs={{0,96},{32,0},{64,32},{96,64},{1,97},{33,1},{65,33},{97,65},{2,98}... | collective-permute-start | bytes 393224 | tf_op jit(solution)/shard_map/ppermute | solution.py:253
  22.7 4.1 %collective-permute-done.3 = bf16[64,1024]{1,0:T(8,128)(2,1)S(1)} collective-permute-done((bf16[64,1024]{1,0:T(8,128)(2,1)S(1)}, bf16[64,1024]{1,0:T(8,128)(2,1)S(1)}, u32[]{:S(2)}, u32[]{:S(2)}) %collective-permute-start.3) | collective-permute-done | bytes 131104 | tf_op jit(solution)/shard_map/ppermute | solution.py:253
  27.9 3.6 %collective-permute-done.1 = bf16[64,1024]{1,0:T(8,128)(2,1)S(1)} collective-permute-done((bf16[64,1024]{1,0:T(8,128)(2,1)S(1)}, bf16[64,1024]{1,0:T(8,128)(2,1)S(1)}, u32[]{:S(2)}, u32[]{:S(2)}) %collective-permute-start.1) | collective-permute-done | bytes 131104 | tf_op jit(solution)/shard_map/ppermute | solution.py:253
  33.5 2.2 %copy-done.1 = bf16[16384,128]{1,0:T(8,128)(2,1)S(1)} copy-done((bf16[16384,128]{1,0:T(8,128)(2,1)S(1)}, bf16[16384,128]{1,0:T(8,128)(2,1)}, u32[]{:S(2)}) %copy-start.1) | copy-done | bytes 4194328
  35.7 18.3 %shard_map.69 = (bf16[4,256,128]{2,1,0:T(8,128)(2,1)S(1)}, bf16[4,256,128]{2,1,0:T(8,128)(2,1)S(1)}, bf16[4,256,128]{2,1,0:T(8,128)(2,1)S(1)}, bf16[4,256,128]{2...) custom-call(s32[2]{0:T(128)S(1)} %pad_add_fusion.place, ...), custom_call_target="tpu_custom_call" | custom-call | flops 268435456 | bytes 8388608 | tf_op jit(solution)/shard_map/pallas_call | solution.py:109
  54.2 3.1 %collective-permute-start.7 = (bf16[4,256,128]{2,1,0:T(8,128)(2,1)S(1)}, bf16[4,256,128]{2,1,0:T(8,128)(2,1)S(1)}, u32[]{:S(2)}, u32[]{:S(2)}) collective-permute-start(bf16[4,256,128]{2,1,0:T(8,128)(2,1)S(1)} %get-tuple-element.27), channel_id=1, source_target_pairs={{0,3},{1,0},{2,1},{3,2},{4,7},{5,4},{6,5},{7,6},{8,11},{9,8},{10,9... | collective-permute-start | bytes 786440 | tf_op jit(solution)/shard_map/ppermute | solution.py:253
  57.3 2.1 %collective-permute-start.8 = (bf16[4,256,128]{2,1,0:T(8,128)(2,1)S(1)}, bf16[4,256,128]{2,1,0:T(8,128)(2,1)S(1)}, u32[]{:S(2)}, u32[]{:S(2)}) collective-permute-start(bf16[4,256,128]{2,1,0:T(8,128)(2,1)S(1)} %get-tuple-element.29), channel_id=1, source_target_pairs={{0,4},{4,8},{8,12},{12,0},{1,5},{5,9},{9,13},{13,1},{2,6},{6,10},{... | collective-permute-start | bytes 786440 | tf_op jit(solution)/shard_map/ppermute | solution.py:253
  59.4 6.8 %collective-permute-done.5.refs_1_ = bf16[4,256,128]{2,1,0:T(8,128)(2,1)S(1)} collective-permute-done((bf16[4,256,128]{2,1,0:T(8,128)(2,1)S(1)}, bf16[4,256,128]{2,1,0:T(8,128)(2,1)S(1)}, u32[]{:S(2)}, u32[]{:S(2)}) %collective-permute-start.5) | collective-permute-done | bytes 262176 | tf_op jit(solution)/shard_map/ppermute | solution.py:253
  66.2 2.4 %collective-permute-done.8.refs_5_ = bf16[4,256,128]{2,1,0:T(8,128)(2,1)S(1)} collective-permute-done((bf16[4,256,128]{2,1,0:T(8,128)(2,1)S(1)}, bf16[4,256,128]{2,1,0:T(8,128)(2,1)S(1)}, u32[]{:S(2)}, u32[]{:S(2)}) %collective-permute-start.8) | collective-permute-done | bytes 262176 | tf_op jit(solution)/shard_map/ppermute | solution.py:253
  68.7 5.2 %collective-permute-done.10.refs_7_ = bf16[4,256,128]{2,1,0:T(8,128)(2,1)S(1)} collective-permute-done((bf16[4,256,128]{2,1,0:T(8,128)(2,1)S(1)}, bf16[4,256,128]{2,1,0:T(8,128)(2,1)S(1)}, u32[]{:S(2)}, u32[]{:S(2)}) %collective-permute-start.10) | collective-permute-done | bytes 262176 | tf_op jit(solution)/shard_map/ppermute | solution.py:253
  74.8 2.8 %collective-permute-start.12 = (bf16[256,128]{1,0:T(8,128)(2,1)S(1)}, bf16[256,128]{1,0:T(8,128)(2,1)S(1)}, u32[]{:S(2)}, u32[]{:S(2)}) collective-permute-start(bf16[256,128]{1,0:T(8,128)(2,1)S(1)} %get-tuple-element.34), channel_id=1, source_target_pairs={{0,8},{4,12},{8,0},{12,4},{1,9},{5,13},{9,1},{13,5},{2,10},{6,14},... | collective-permute-start | bytes 196616 | tf_op jit(solution)/shard_map/ppermute | solution.py:253
  79.4 1.6 %collective-permute-done.11.refs_1_ = bf16[256,128]{1,0:T(8,128)(2,1)S(1)} collective-permute-done((bf16[256,128]{1,0:T(8,128)(2,1)S(1)}, bf16[256,128]{1,0:T(8,128)(2,1)S(1)}, u32[]{:S(2)}, u32[]{:S(2)}) %collective-permute-start.11) | collective-permute-done | bytes 65568 | tf_op jit(solution)/shard_map/ppermute | solution.py:253
  82.0 2.2 %collective-permute-done.14.refs_5_ = bf16[256,128]{1,0:T(8,128)(2,1)S(1)} collective-permute-done((bf16[256,128]{1,0:T(8,128)(2,1)S(1)}, bf16[256,128]{1,0:T(8,128)(2,1)S(1)}, u32[]{:S(2)}, u32[]{:S(2)}) %collective-permute-start.14) | collective-permute-done | bytes 65568 | tf_op jit(solution)/shard_map/ppermute | solution.py:253
  87.2 2.5 %collective-permute-start.20 = (f32[64,64]{1,0:T(8,128)S(1)}, f32[64,64]{1,0:T(8,128)S(1)}, u32[]{:S(2)}, u32[]{:S(2)}) collective-permute-start(f32[64,64]{1,0:T(8,128)S(1)} %add.71), channel_id=1, source_target_pairs={{0,3},{1,0},{2,1},{3,2},{4,7},{5,4},{6,5},{7,6},{8,11},{9,8},{10,9... | collective-permute-start | bytes 49160 | tf_op jit(solution)/shard_map/ppermute | solution.py:253
  89.7 1.5 %collective-permute-start.18 = (f32[64,64]{1,0:T(8,128)S(1)}, f32[64,64]{1,0:T(8,128)S(1)}, u32[]{:S(2)}, u32[]{:S(2)}) collective-permute-start(f32[64,64]{1,0:T(8,128)S(1)} %add.71), channel_id=1, source_target_pairs={{0,2},{1,3},{2,0},{3,1},{4,6},{5,7},{6,4},{7,5},{8,10},{9,11},{10,... | collective-permute-start | bytes 49160 | tf_op jit(solution)/shard_map/ppermute | solution.py:253
  91.3 3.9 %collective-permute-done.19 = f32[64,64]{1,0:T(8,128)S(1)} collective-permute-done((f32[64,64]{1,0:T(8,128)S(1)}, f32[64,64]{1,0:T(8,128)S(1)}, u32[]{:S(2)}, u32[]{:S(2)}) %collective-permute-start.19) | collective-permute-done | bytes 16416 | tf_op jit(solution)/shard_map/ppermute | solution.py:253
  97.3 2.6 %collective-permute-start.21 = (f32[64,64]{1,0:T(8,128)S(1)}, f32[64,64]{1,0:T(8,128)S(1)}, u32[]{:S(2)}, u32[]{:S(2)}) collective-permute-start(f32[64,64]{1,0:T(8,128)S(1)} %add_add_fusion.1), channel_id=1, source_target_pairs={{0,8},{4,12},{8,0},{12,4},{1,9},{5,13},{9,1},{13,5},{2,10},{6,14},... | collective-permute-start | bytes 49160 | tf_op jit(solution)/shard_map/ppermute | solution.py:253
  102.8 1.9 %collective-permute-start.25 = (f32[64,64]{1,0:T(8,128)S(1)}, f32[64,64]{1,0:T(8,128)S(1)}, u32[]{:S(2)}, u32[]{:S(2)}) collective-permute-start(f32[64,64]{1,0:T(8,128)S(1)} %add_add_fusion.g0), channel_id=1, source_target_pairs={{0,64},{32,96},{64,0},{96,32},{1,65},{33,97},{65,1},{97,33},{2,66}... | collective-permute-start | bytes 49160 | tf_op jit(solution)/shard_map/ppermute | solution.py:253
  106.7 1.6 %collective-permute-done.25.g2 = f32[64,64]{1,0:T(8,128)S(1)} collective-permute-done((f32[64,64]{1,0:T(8,128)S(1)}, f32[64,64]{1,0:T(8,128)S(1)}, u32[]{:S(2)}, u32[]{:S(2)}) %collective-permute-start.25) | collective-permute-done | bytes 16416 | tf_op jit(solution)/shard_map/ppermute | solution.py:253
  109.8 2.8 %shard_map.72 = (f32[64,1024]{1,0:T(8,128)}, f32[64,64]{1,0:T(8,128)}) custom-call(f32[64,64]{1,0:T(8,128)S(1)} %add_add_fusion.g0, f32[64,64]{1,0:T(8,128)S(1)} %collective-permute-done.24.g1, f32[64,64]{1,0:T(8,128)S(1)} %collective-permute-done.25.g2, f32[64,64]{1,0:T(8,128)S(1)} %collective-permute-done.26.g3, f32[64,1024]{1,0:T(8,128)S(1)} %get-tuple-element.41.image), custom_call_target="tpu_custom_call" | custom-call | tf_op jit(solution)/shard_map/pallas_call | solution.py:239
  (56 shorter events, 19.4 us)
Async XLA Ops:
  0.6 13.0 %collective-permute-start = (bf16[64,1024]{1,0:T(8,128)(2,1)}, bf16[64,1024]{1,0:T(8,128)(2,1)S(1)}, u32[]{:S(2)}, u32[]{:S(2)}) collective-permute-start(bf16[64,1024]{1,0:T(8,128)(2,1)} %refs_8_.1), channel_id=1, source_target_pairs={{0,0},{1,32},{2,64},{3,96},{4,48},{5,80},{6,112},{7,16},{8,65},{9,... | collective-permute-start | bytes 393224 | tf_op jit(solution)/shard_map/ppermute | solution.py:265
  13.7 13.1 %collective-permute-start.3 = (bf16[64,1024]{1,0:T(8,128)(2,1)S(1)}, bf16[64,1024]{1,0:T(8,128)(2,1)S(1)}, u32[]{:S(2)}, u32[]{:S(2)}) collective-permute-start(bf16[64,1024]{1,0:T(8,128)(2,1)S(1)} %bitcast_add_fusion), channel_id=1, source_target_pairs={{0,96},{32,0},{64,32},{96,64},{1,97},{33,1},{65,33},{97,65},{2,98}... | collective-permute-start | bytes 393224 | tf_op jit(solution)/shard_map/ppermute | solution.py:253
  21.2 6.6 %collective-permute-start.2 = (bf16[64,1024]{1,0:T(8,128)(2,1)S(1)}, bf16[64,1024]{1,0:T(8,128)(2,1)S(1)}, u32[]{:S(2)}, u32[]{:S(2)}) collective-permute-start(bf16[64,1024]{1,0:T(8,128)(2,1)S(1)} %bitcast_add_fusion), channel_id=1, source_target_pairs={{0,64},{32,96},{64,0},{96,32},{1,65},{33,97},{65,1},{97,33},{2,66}... | collective-permute-start | bytes 393224 | tf_op jit(solution)/shard_map/ppermute | solution.py:253
  21.3 10.1 %collective-permute-start.1 = (bf16[64,1024]{1,0:T(8,128)(2,1)S(1)}, bf16[64,1024]{1,0:T(8,128)(2,1)S(1)}, u32[]{:S(2)}, u32[]{:S(2)}) collective-permute-start(bf16[64,1024]{1,0:T(8,128)(2,1)S(1)} %bitcast_add_fusion), channel_id=1, source_target_pairs={{0,32},{32,64},{64,96},{96,0},{1,33},{33,65},{65,97},{97,1},{2,34}... | collective-permute-start | bytes 393224 | tf_op jit(solution)/shard_map/ppermute | solution.py:253
  54.0 12.2 %collective-permute-start.5 = (bf16[4,256,128]{2,1,0:T(8,128)(2,1)S(1)}, bf16[4,256,128]{2,1,0:T(8,128)(2,1)S(1)}, u32[]{:S(2)}, u32[]{:S(2)}) collective-permute-start(bf16[4,256,128]{2,1,0:T(8,128)(2,1)S(1)} %get-tuple-element.25), channel_id=1, source_target_pairs={{0,1},{1,2},{2,3},{3,0},{4,5},{5,6},{6,7},{7,4},{8,9},{9,10},{10,1... | collective-permute-start | bytes 786440 | tf_op jit(solution)/shard_map/ppermute | solution.py:253
  54.1 12.1 %collective-permute-start.6 = (bf16[4,256,128]{2,1,0:T(8,128)(2,1)S(1)}, bf16[4,256,128]{2,1,0:T(8,128)(2,1)S(1)}, u32[]{:S(2)}, u32[]{:S(2)}) collective-permute-start(bf16[4,256,128]{2,1,0:T(8,128)(2,1)S(1)} %get-tuple-element.26), channel_id=1, source_target_pairs={{0,2},{1,3},{2,0},{3,1},{4,6},{5,7},{6,4},{7,5},{8,10},{9,11},{10,... | collective-permute-start | bytes 786440 | tf_op jit(solution)/shard_map/ppermute | solution.py:253
  54.2 12.0 %collective-permute-start.7 = (bf16[4,256,128]{2,1,0:T(8,128)(2,1)S(1)}, bf16[4,256,128]{2,1,0:T(8,128)(2,1)S(1)}, u32[]{:S(2)}, u32[]{:S(2)}) collective-permute-start(bf16[4,256,128]{2,1,0:T(8,128)(2,1)S(1)} %get-tuple-element.27), channel_id=1, source_target_pairs={{0,3},{1,0},{2,1},{3,2},{4,7},{5,4},{6,5},{7,6},{8,11},{9,8},{10,9... | collective-permute-start | bytes 786440 | tf_op jit(solution)/shard_map/ppermute | solution.py:253
  57.3 11.3 %collective-permute-start.8 = (bf16[4,256,128]{2,1,0:T(8,128)(2,1)S(1)}, bf16[4,256,128]{2,1,0:T(8,128)(2,1)S(1)}, u32[]{:S(2)}, u32[]{:S(2)}) collective-permute-start(bf16[4,256,128]{2,1,0:T(8,128)(2,1)S(1)} %get-tuple-element.29), channel_id=1, source_target_pairs={{0,4},{4,8},{8,12},{12,0},{1,5},{5,9},{9,13},{13,1},{2,6},{6,10},{... | collective-permute-start | bytes 786440 | tf_op jit(solution)/shard_map/ppermute | solution.py:253
  59.4 9.2 %collective-permute-start.9 = (bf16[4,256,128]{2,1,0:T(8,128)(2,1)S(1)}, bf16[4,256,128]{2,1,0:T(8,128)(2,1)S(1)}, u32[]{:S(2)}, u32[]{:S(2)}) collective-permute-start(bf16[4,256,128]{2,1,0:T(8,128)(2,1)S(1)} %get-tuple-element.30), channel_id=1, source_target_pairs={{0,8},{4,12},{8,0},{12,4},{1,9},{5,13},{9,1},{13,5},{2,10},{6,14},... | collective-permute-start | bytes 786440 | tf_op jit(solution)/shard_map/ppermute | solution.py:253
  66.2 7.7 %collective-permute-start.10 = (bf16[4,256,128]{2,1,0:T(8,128)(2,1)S(1)}, bf16[4,256,128]{2,1,0:T(8,128)(2,1)S(1)}, u32[]{:S(2)}, u32[]{:S(2)}) collective-permute-start(bf16[4,256,128]{2,1,0:T(8,128)(2,1)S(1)} %get-tuple-element.31), channel_id=1, source_target_pairs={{0,12},{4,0},{8,4},{12,8},{1,13},{5,1},{9,5},{13,9},{2,14},{6,2},{... | collective-permute-start | bytes 786440 | tf_op jit(solution)/shard_map/ppermute | solution.py:253
  74.7 6.2 %collective-permute-start.11 = (bf16[256,128]{1,0:T(8,128)(2,1)S(1)}, bf16[256,128]{1,0:T(8,128)(2,1)S(1)}, u32[]{:S(2)}, u32[]{:S(2)}) collective-permute-start(bf16[256,128]{1,0:T(8,128)(2,1)S(1)} %get-tuple-element.33), channel_id=1, source_target_pairs={{0,4},{4,8},{8,12},{12,0},{1,5},{5,9},{9,13},{13,1},{2,6},{6,10},{... | collective-permute-start | bytes 196616 | tf_op jit(solution)/shard_map/ppermute | solution.py:253
  74.8 7.2 %collective-permute-start.12 = (bf16[256,128]{1,0:T(8,128)(2,1)S(1)}, bf16[256,128]{1,0:T(8,128)(2,1)S(1)}, u32[]{:S(2)}, u32[]{:S(2)}) collective-permute-start(bf16[256,128]{1,0:T(8,128)(2,1)S(1)} %get-tuple-element.34), channel_id=1, source_target_pairs={{0,8},{4,12},{8,0},{12,4},{1,9},{5,13},{9,1},{13,5},{2,10},{6,14},... | collective-permute-start | bytes 196616 | tf_op jit(solution)/shard_map/ppermute | solution.py:253
  77.6 4.4 %collective-permute-start.13 = (bf16[256,128]{1,0:T(8,128)(2,1)S(1)}, bf16[256,128]{1,0:T(8,128)(2,1)S(1)}, u32[]{:S(2)}, u32[]{:S(2)}) collective-permute-start(bf16[256,128]{1,0:T(8,128)(2,1)S(1)} %get-tuple-element.35), channel_id=1, source_target_pairs={{0,12},{4,0},{8,4},{12,8},{1,13},{5,1},{9,5},{13,9},{2,14},{6,2},{... | collective-permute-start | bytes 196616 | tf_op jit(solution)/shard_map/ppermute | solution.py:253
  78.0 6.2 %collective-permute-start.14 = (bf16[256,128]{1,0:T(8,128)(2,1)S(1)}, bf16[256,128]{1,0:T(8,128)(2,1)S(1)}, u32[]{:S(2)}, u32[]{:S(2)}) collective-permute-start(bf16[256,128]{1,0:T(8,128)(2,1)S(1)} %get-tuple-element.37), channel_id=1, source_target_pairs={{0,1},{1,2},{2,3},{3,0},{4,5},{5,6},{6,7},{7,4},{8,9},{9,10},{10,1... | collective-permute-start | bytes 196616 | tf_op jit(solution)/shard_map/ppermute | solution.py:253
  78.0 6.2 %collective-permute-start.15 = (bf16[256,128]{1,0:T(8,128)(2,1)S(1)}, bf16[256,128]{1,0:T(8,128)(2,1)S(1)}, u32[]{:S(2)}, u32[]{:S(2)}) collective-permute-start(bf16[256,128]{1,0:T(8,128)(2,1)S(1)} %get-tuple-element.38), channel_id=1, source_target_pairs={{0,2},{1,3},{2,0},{3,1},{4,6},{5,7},{6,4},{7,5},{8,10},{9,11},{10,... | collective-permute-start | bytes 196616 | tf_op jit(solution)/shard_map/ppermute | solution.py:253
  81.0 4.3 %collective-permute-start.16 = (bf16[256,128]{1,0:T(8,128)(2,1)S(1)}, bf16[256,128]{1,0:T(8,128)(2,1)S(1)}, u32[]{:S(2)}, u32[]{:S(2)}) collective-permute-start(bf16[256,128]{1,0:T(8,128)(2,1)S(1)} %get-tuple-element.39), channel_id=1, source_target_pairs={{0,3},{1,0},{2,1},{3,2},{4,7},{5,4},{6,5},{7,6},{8,11},{9,8},{10,9... | collective-permute-start | bytes 196616 | tf_op jit(solution)/shard_map/ppermute | solution.py:253
  87.2 4.1 %collective-permute-start.20 = (f32[64,64]{1,0:T(8,128)S(1)}, f32[64,64]{1,0:T(8,128)S(1)}, u32[]{:S(2)}, u32[]{:S(2)}) collective-permute-start(f32[64,64]{1,0:T(8,128)S(1)} %add.71), channel_id=1, source_target_pairs={{0,3},{1,0},{2,1},{3,2},{4,7},{5,4},{6,5},{7,6},{8,11},{9,8},{10,9... | collective-permute-start | bytes 49160 | tf_op jit(solution)/shard_map/ppermute | solution.py:253
  89.7 5.5 %collective-permute-start.19 = (f32[64,64]{1,0:T(8,128)S(1)}, f32[64,64]{1,0:T(8,128)S(1)}, u32[]{:S(2)}, u32[]{:S(2)}) collective-permute-start(f32[64,64]{1,0:T(8,128)S(1)} %add.71), channel_id=1, source_target_pairs={{0,1},{1,2},{2,3},{3,0},{4,5},{5,6},{6,7},{7,4},{8,9},{9,10},{10,1... | collective-permute-start | bytes 49160 | tf_op jit(solution)/shard_map/ppermute | solution.py:253
  89.7 5.5 %collective-permute-start.18 = (f32[64,64]{1,0:T(8,128)S(1)}, f32[64,64]{1,0:T(8,128)S(1)}, u32[]{:S(2)}, u32[]{:S(2)}) collective-permute-start(f32[64,64]{1,0:T(8,128)S(1)} %add.71), channel_id=1, source_target_pairs={{0,2},{1,3},{2,0},{3,1},{4,6},{5,7},{6,4},{7,5},{8,10},{9,11},{10,... | collective-permute-start | bytes 49160 | tf_op jit(solution)/shard_map/ppermute | solution.py:253
  95.2 4.7 %collective-permute-start.23 = (f32[64,64]{1,0:T(8,128)S(1)}, f32[64,64]{1,0:T(8,128)S(1)}, u32[]{:S(2)}, u32[]{:S(2)}) collective-permute-start(f32[64,64]{1,0:T(8,128)S(1)} %add_add_fusion.1), channel_id=1, source_target_pairs={{0,12},{4,0},{8,4},{12,8},{1,13},{5,1},{9,5},{13,9},{2,14},{6,2},{... | collective-permute-start | bytes 49160 | tf_op jit(solution)/shard_map/ppermute | solution.py:253
  96.2 5.1 %collective-permute-start.22 = (f32[64,64]{1,0:T(8,128)S(1)}, f32[64,64]{1,0:T(8,128)S(1)}, u32[]{:S(2)}, u32[]{:S(2)}) collective-permute-start(f32[64,64]{1,0:T(8,128)S(1)} %add_add_fusion.1), channel_id=1, source_target_pairs={{0,4},{4,8},{8,12},{12,0},{1,5},{5,9},{9,13},{13,1},{2,6},{6,10},{... | collective-permute-start | bytes 49160 | tf_op jit(solution)/shard_map/ppermute | solution.py:253
  97.3 5.4 %collective-permute-start.21 = (f32[64,64]{1,0:T(8,128)S(1)}, f32[64,64]{1,0:T(8,128)S(1)}, u32[]{:S(2)}, u32[]{:S(2)}) collective-permute-start(f32[64,64]{1,0:T(8,128)S(1)} %add_add_fusion.1), channel_id=1, source_target_pairs={{0,8},{4,12},{8,0},{12,4},{1,9},{5,13},{9,1},{13,5},{2,10},{6,14},... | collective-permute-start | bytes 49160 | tf_op jit(solution)/shard_map/ppermute | solution.py:253
  102.8 5.5 %collective-permute-start.25 = (f32[64,64]{1,0:T(8,128)S(1)}, f32[64,64]{1,0:T(8,128)S(1)}, u32[]{:S(2)}, u32[]{:S(2)}) collective-permute-start(f32[64,64]{1,0:T(8,128)S(1)} %add_add_fusion.g0), channel_id=1, source_target_pairs={{0,64},{32,96},{64,0},{96,32},{1,65},{33,97},{65,1},{97,33},{2,66}... | collective-permute-start | bytes 49160 | tf_op jit(solution)/shard_map/ppermute | solution.py:253
  104.7 5.1 %collective-permute-start.24 = (f32[64,64]{1,0:T(8,128)S(1)}, f32[64,64]{1,0:T(8,128)S(1)}, u32[]{:S(2)}, u32[]{:S(2)}) collective-permute-start(f32[64,64]{1,0:T(8,128)S(1)} %add_add_fusion.g0), channel_id=1, source_target_pairs={{0,32},{32,64},{64,96},{96,0},{1,33},{33,65},{65,97},{97,1},{2,34}... | collective-permute-start | bytes 49160 | tf_op jit(solution)/shard_map/ppermute | solution.py:253
  (9 other events, 123.7 us)

commit v3 on v2

v3 whole, which is shorter than its diff:
```python
import jax
import jax.numpy as jnp
from jax import lax
from jax.experimental import pallas as pl
from jax.experimental.pallas import tpu as pltpu
from jax.sharding import Mesh
from jax.sharding import PartitionSpec as P

K = 64
BS = 64
CAP = 512
RBLK = 256
CBLK = 128
PIECE = 1024
POINTS = 131072
COLS = 16
HALF = BS // 2
PART = 512
PITCH = 40
UNROLL = 32
AXES = ("z", "core", "y", "x")
F32 = jnp.float32
BF16 = jnp.bfloat16


def values_kernel(starts, counts, values, out, rows, spread):
    @pl.when(pl.program_id(0) == 0)
    def _():
        slots = lax.broadcasted_iota(jnp.int32, (8, 128), 0) * 128
        slots = slots + lax.broadcasted_iota(jnp.int32, (8, 128), 1)

        def count_up(step, total):
            for offset in range(8):
                total = total + jnp.where(slots >= starts[step * 8 + offset], 1, 0)
            return total

        total = lax.fori_loop(0, RBLK // 8, count_up, jnp.full((8, 128), -1, jnp.int32))
        rows[...] = jnp.where(slots < counts[0], total, RBLK)

    for group in range(values.shape[0] // 16):
        for tile in range(HALF):
            part = values[group * 16 : (group + 1) * 16, tile * 128 : (tile + 1) * 128]
            spread[pl.ds(tile, 16, stride=PITCH), :] = part.astype(F32)
        for slot in range(16):
            first = (group * 16 + slot) * HALF
            block = spread[slot * PITCH : slot * PITCH + HALF, :]
            out[first : first + HALF, :] = block.astype(BF16)


def relayout_values(starts, counts, block_values):
    step = 64
    smem = pl.BlockSpec(memory_space=pltpu.SMEM)
    return pl.pallas_call(
        values_kernel,
        grid=(CAP // step,),
        in_specs=[smem, smem, pl.BlockSpec((step, BS * BS), lambda i: (i, 0))],
        out_specs=[
            pl.BlockSpec((step * HALF, 128), lambda i: (i, 0)),
            pl.BlockSpec((8, 128), lambda i: (0, 0)),
        ],
        out_shape=[
            jax.ShapeDtypeStruct((CAP * HALF, 128), BF16),
            jax.ShapeDtypeStruct((8, 128), jnp.int32),
        ],
        scratch_shapes=[pltpu.VMEM((16 * PITCH, 128), F32)],
        compiler_params=pltpu.CompilerParams(vmem_limit_bytes=16 * 1024 * 1024),
        cost_estimate=pl.CostEstimate(flops=0, bytes_accessed=24 * 1024 * 1024, transcendentals=0),
    )(starts, counts, block_values)


def transpose_kernel(panel, rows, out, work):
    work[:K, :] = panel[...].astype(F32)
    work[K:, :] = jnp.zeros_like(work[K:, :])
    points = work[...].T
    low = lax.broadcasted_iota(jnp.int32, (HALF, 128), 1) < BS
    for block in range(PIECE // BS):
        first = points[block * BS : block * BS + HALF, :]
        second = points[block * BS + HALF : (block + 1) * BS, :]
        pair = jnp.where(low, first, pltpu.roll(second, BS, 1))
        out[block * HALF : (block + 1) * HALF, :] = pair.astype(BF16)


def transpose_panel(panel, rows):
    vmem = pl.BlockSpec(memory_space=pltpu.VMEM)
    unread = pl.BlockSpec(memory_space=pl.ANY)
    return pl.pallas_call(
        transpose_kernel,
        in_specs=[vmem, unread],
        out_specs=vmem,
        out_shape=jax.ShapeDtypeStruct((PIECE // 2, 128), BF16),
        scratch_shapes=[pltpu.VMEM((128, PIECE), F32)],
        compiler_params=pltpu.CompilerParams(vmem_limit_bytes=16 * 1024 * 1024),
    )(panel, rows)


def multiply_kernel(rows, tiles, counts, own, other, values, *rest):
    outs, (weights, total) = rest[:4], rest[4:]
    z, core = lax.axis_index("z"), lax.axis_index("core")
    y, x = lax.axis_index("y"), lax.axis_index("x")
    low = lax.broadcasted_iota(jnp.int32, (HALF, 128), 1) < BS
    zero = jnp.zeros((HALF, 128), F32)

    for side, band in enumerate((own, other)):

        side = core if side == 0 else 1 - core
        start = z + 12 - y - 2 * lax.rem(x, 2) - side

        def fill(turn, carry, side=side, start=start, band=band):
            piece = side * 4 + lax.rem(start - turn, 4)
            for block in range(PIECE // BS):
                pair = band[turn, block * HALF : (block + 1) * HALF, :].astype(F32)
                swapped = pltpu.roll(pair, BS, 1)
                tile = piece * (PIECE // BS) + block
                first = pl.multiple_of(tile * 128, 128)
                weights[pl.ds(first, HALF), :] = jnp.where(low, pair, zero).astype(BF16)
                weights[pl.ds(first + 32, HALF), :] = jnp.where(low, swapped, zero).astype(BF16)
                weights[pl.ds(first + 64, HALF), :] = jnp.where(low, zero, swapped).astype(BF16)
                weights[pl.ds(first + 96, HALF), :] = jnp.where(low, zero, pair).astype(BF16)
            return carry

        lax.fori_loop(0, 4, fill, 0)
    total[...] = jnp.zeros_like(total)

    def add_group(index, carry):
        products = []
        for offset in range(UNROLL):
            slot = index * UNROLL + offset
            block = values[pl.ds(pl.multiple_of(slot * HALF, HALF), HALF), :]
            tile = weights[pl.ds(pl.multiple_of(tiles[slot] * 128, 128), 128), :]
            products.append(jnp.dot(block, tile, preferred_element_type=F32))
        for offset in range(UNROLL):
            slot = index * UNROLL + offset
            where = pl.ds(pl.multiple_of(rows[lax.div(slot, 128), lax.rem(slot, 128)] * HALF, HALF), HALF)
            total[where, :] = total[where, :] + products[offset]
        return carry

    rounds = lax.div(counts[0] + UNROLL - 1, UNROLL)
    lax.fori_loop(0, rounds, add_group, 0)
    for shift in range(4):
        to_x = lax.rem(x + shift, 4)
        to_y = lax.rem(y + shift, 4)
        for index in range(4):
            chunk = jnp.where(core == 0, index * 4 + to_x, to_y * 4 + index)
            first = pl.multiple_of(chunk * PART, PART)
            outs[shift][index] = total[pl.ds(first, PART), :].astype(BF16)


def multiply(rows, tiles, counts, own, other, values):
    smem = pl.BlockSpec(memory_space=pltpu.SMEM)
    vmem = pl.BlockSpec(memory_space=pltpu.VMEM)
    return pl.pallas_call(
        multiply_kernel,
        in_specs=[smem] * 3 + [vmem] * 3,
        out_specs=[vmem] * 4,
        out_shape=[jax.ShapeDtypeStruct((4, PART, 128), BF16)] * 4,
        scratch_shapes=[
            pltpu.VMEM((CBLK * 128, 128), BF16),
            pltpu.VMEM(((RBLK + 1) * HALF, 128), F32),
        ],
        compiler_params=pltpu.CompilerParams(vmem_limit_bytes=24 * 1024 * 1024),
        cost_estimate=pl.CostEstimate(
            flops=2 * CAP * BS * BS * K, bytes_accessed=8 * 1024 * 1024, transcendentals=0
        ),
    )(rows, tiles, counts, own, other, values)


def stage_kernel(*refs):
    ins, outs = refs[:4], refs[4:]
    base = jnp.where(lax.axis_index("core") == 0, lax.axis_index("y"), lax.axis_index("x"))
    for shift in range(4):
        to = lax.rem(base + shift, 4)
        total = ins[0][to].astype(F32)
        for index in range(1, 4):
            total = total + ins[index][to].astype(F32)
        outs[shift][...] = total.astype(outs[shift].dtype)


def stage_sums(arrays):
    vmem = pl.BlockSpec(memory_space=pltpu.VMEM)
    shapes = [jax.ShapeDtypeStruct((PART, 128), F32)]
    shapes += [jax.ShapeDtypeStruct((PART, 128), BF16)] * 3
    return pl.pallas_call(
        stage_kernel,
        in_specs=[vmem] * 4,
        out_specs=[vmem] * 4,
        out_shape=shapes,
        compiler_params=pltpu.CompilerParams(vmem_limit_bytes=16 * 1024 * 1024),
    )(*arrays)


def image_kernel(*refs):
    ins, (panel, image, gram, spread) = refs[:4], refs[4:]
    total = ins[0][...]
    for index in range(1, 4):
        total = total + ins[index][...].astype(F32)
    spread[pl.ds(0, PART, stride=2), :] = total
    spread[pl.ds(1, PART, stride=2), :] = pltpu.roll(total, BS, 1)
    whole = spread[...].T[:K, :] + panel[...].astype(F32)
    image[...] = whole
    gram[...] = lax.dot_general(
        whole,
        whole,
        (((1,), (1,)), ((), ())),
        precision=lax.Precision.HIGHEST,
        preferred_element_type=F32,
    ) * (1.0 / POINTS)


def finish_image(arrays, panel):
    vmem = pl.BlockSpec(memory_space=pltpu.VMEM)
    return pl.pallas_call(
        image_kernel,
        in_specs=[vmem] * 5,
        out_specs=[vmem, vmem],
        out_shape=[
            jax.ShapeDtypeStruct((K, PIECE), F32),
            jax.ShapeDtypeStruct((K, K), F32),
        ],
        scratch_shapes=[pltpu.VMEM((PIECE, 128), F32)],
        compiler_params=pltpu.CompilerParams(vmem_limit_bytes=16 * 1024 * 1024),
    )(*arrays, panel)


def basis_kernel(g0, g1, g2, g3, image, basis, factor, work):
    gram = (g0[...] + g2[...]) + (g1[...] + g3[...])
    work[...] = jnp.zeros_like(work)
    work[:, :K] = gram
    lane = lax.broadcasted_iota(jnp.int32, (8, 128), 1)
    sub = lax.broadcasted_iota(jnp.int32, (8, 128), 0)
    groups = []
    for g in range(8):
        shifted = pltpu.roll(work[g * 8 : (g + 1) * 8, :], K, 1)
        groups.append(jnp.where(lane == sub + g * 8, 1.0, shifted))
    for b in range(8):
        columns = []
        for j in range(8):
            at = K + b * 8 + j
            columns.append(
                [jnp.broadcast_to(groups[g][:, at : at + 1], (8, 128)) for g in range(b, 8)]
            )
        done = []
        for j in range(8):
            scale = lax.rsqrt(columns[j][0][j : j + 1, :])
            scaled = [c * scale for c in columns[j]]
            columns[j] = scaled
            for later in range(j + 1, 8):
                times = scaled[0][later : later + 1, :]
                columns[later] = [c - s * times for c, s in zip(columns[later], scaled)]
            row = groups[b][j : j + 1, :]
            for before in range(j):
                row = row - columns[before][0][j : j + 1, :] * done[before]
            done.append(row * scale)
        for g in range(b + 1, 8):
            value = groups[g]
            for j in range(8):
                value = value - columns[j][g - b] * done[j]
            groups[g] = value
        for j in range(8):
            work[b * 8 + j : b * 8 + j + 1, :] = done[j]
    final = work[...]
    rows = lax.broadcasted_iota(jnp.int32, (K, 128), 0)
    lanes = lax.broadcasted_iota(jnp.int32, (K, 128), 1)
    upper = jnp.where(lanes - K >= rows, final, 0.0)
    factor[...] = upper.T[K:, :]
    inverse = final[:, :K]
    basis[...] = lax.dot_general(
        inverse,
        image[...],
        (((1,), (0,)), ((), ())),
        precision=lax.Precision.HIGHEST,
        preferred_element_type=F32,
    )


def orthogonalize(grams, image):
    vmem = pl.BlockSpec(memory_space=pltpu.VMEM)
    return pl.pallas_call(
        basis_kernel,
        in_specs=[vmem] * 5,
        out_specs=[vmem, vmem],
        out_shape=[
            jax.ShapeDtypeStruct((K, PIECE), F32),
            jax.ShapeDtypeStruct((K, K), F32),
        ],
        scratch_shapes=[pltpu.VMEM((K, 128), F32)],
        compiler_params=pltpu.CompilerParams(vmem_limit_bytes=16 * 1024 * 1024),
    )(*grams, image)


def shifted(value, axis, shift, size=4):
    return lax.ppermute(value, axis, [(i, (i + shift) % size) for i in range(size)])


def gather_band(panel, rows):
    pairs = []
    for z in range(4):
        for core in range(2):
            for y in range(4):
                for x in range(4):
                    source = (z * 2 + core) * COLS + y * 4 + x
                    target = ((z + y + x) % 4 * 2 + y % 2) * COLS + z * 4 + 2 * core + y // 2
                    pairs.append((source, target))
    piece = transpose_panel(lax.ppermute(panel, AXES, pairs), rows)
    own = jnp.stack([piece] + [shifted(piece, "z", turn) for turn in range(1, 4)])
    return own, shifted(own, "core", 1, 2)


def across(value, shift, first):
    pairs = []
    for z in range(4):
        for core in range(2):
            for y in range(4):
                for x in range(4):
                    along_x = (core == 0) == first
                    to = y * 4 + (x + shift) % 4 if along_x else (y + shift) % 4 * 4 + x
                    row = (z * 2 + core) * COLS
                    pairs.append((row + y * 4 + x, row + to))
    return lax.ppermute(value, AXES, pairs)


def sum_along(value, axis):
    near, across, far = (shifted(value, axis, shift) for shift in range(1, 4))
    return (value + across) + (near + far)


def per_device(panel, block_values, row_starts, block_columns, block_counts):
    values, rows = relayout_values(row_starts, block_counts, block_values)
    own, other = gather_band(panel, rows)
    partial = multiply(rows, block_columns, block_counts, own, other, values)
    order = (2, 1, 3)
    sums = stage_sums([partial[0]] + [across(partial[shift], shift, True) for shift in order])
    arrived = [sums[0]] + [across(sums[shift], shift, False) for shift in order]
    image, gram = finish_image(arrived, panel)
    gram = gram + shifted(gram, "core", 1, 2)
    gram = sum_along(sum_along(gram, "x"), "y")
    grams = [gram] + [shifted(gram, "z", shift) for shift in range(1, 4)]
    basis, factor = orthogonalize(grams, image)
    return (basis, factor)


def solution(mesh):
    fine = Mesh(mesh.devices.reshape(4, 2, 4, 4), AXES)
    in_specs = (P(None, AXES), P(AXES, None), P(AXES), P(AXES), P(AXES))
    out_specs = (P(None, AXES), P())
    return jax.shard_map(
        per_device, mesh=fine, in_specs=in_specs, out_specs=out_specs, check_vma=False
    )
```

time: 113 us -> 92.4 us (0.82)
  Pallas kernels: 29.8 us -> 12.1 us
  starting transfers between devices: 34 us -> 37.6 us
  local copies, waits for them, and re-layouts: 6.36 us -> 2.87 us
  waiting for transfers between devices: 40.6 us -> 37.7 us
    ppermute x26 -> x14, waiting for transfers between devices: 40.6 us -> 22 us  [shifted(): lax.ppermute(value, axis, [(i, (i + shift) % size) for i in range(size)])]
    pallas_call x4 -> x5, Pallas kernels: 27 us -> 9.28 us  [the longest x1 5.41 us: multiply(): pl.pallas_call(multiply_kernel, in_specs=[smem] * 3 + [vmem] * 3, out_spe...]
    ppermute x1 -> x7, waiting for transfers between devices: 0.01 us -> 15.8 us  [the longest x6 15.8 us: across(): return lax.ppermute(value, AXES, pairs)]
    ppermute x1 -> x7, starting transfers between devices: 1.56 us -> 12.5 us  [the longest x6 10.9 us: across(): return lax.ppermute(value, AXES, pairs)]
    ppermute x26 -> x14, starting transfers between devices: 32.4 us -> 25.1 us  [shifted(): lax.ppermute(value, axis, [(i, (i + shift) % size) for i in range(size)])]
    unnamed x12 -> x8, local copies, waits for them, and re-layouts: 6.35 us -> 2.87 us
  transfers between devices with their start and end apart: 27 -> 21, of which waited for: 18 -> 18; matrix products, arithmetic and copies ran while one was open for 0% -> 0% of each run, Pallas kernels for 6% -> 3%
where the time goes in v3:
time: 92.4 us; the launch traced here: 91.7 us
  waiting for transfers between devices  37.7 us (41%)
  starting transfers between devices  37.6 us (41%)
  Pallas kernels  12.1 us (13%)
  local copies, waits for them, and re-layouts  2.87 us (3%)
  between operations  1.38 us (1%)
    ppermute x14, starting transfers between devices, shifted(): lax.ppermute(value, axis, [(i, (i + shift) % size) for i in range(size)])  25.1 us
    ppermute x14, waiting for transfers between devices, shifted(): lax.ppermute(value, axis, [(i, (i + shift) % size) for i in range(size)])  22 us
    ppermute x6, waiting for transfers between devices, across(): return lax.ppermute(value, AXES, pairs)  15.8 us
    ppermute x6, starting transfers between devices, across(): return lax.ppermute(value, AXES, pairs)  10.9 us
    pallas_call x1, Pallas kernels, multiply(): pl.pallas_call(multiply_kernel, in_specs=[smem] * 3 + [vmem] * 3, out_spe...  5.41 us
    unnamed x8, local copies, waits for them, and re-layouts  2.87 us
    pallas_call x1, Pallas kernels, orthogonalize(): pl.pallas_call(basis_kernel, in_specs=[vmem] * 5, out_specs=[vmem, vmem],...  2.78 us
    pallas_call x1, Pallas kernels, relayout_values(): pl.pallas_call(values_kernel, grid=(CAP // step,), in_specs=[smem, smem,...  2.75 us
  transfers between devices with their start and end apart: 21, of which 18 were waited for; matrix products, arithmetic and copies ran while one was open for 0% of the time, Pallas kernels for 3%

profile of v3, /device:TPU:0, one launch (start us, length us, event | category | flops | bytes accessed | tf_op | source)
XLA Modules:
  0.0 91.7 jit_solution(2360206269354770937)
XLA Ops:
  0.6 1.6 %collective-permute-start = (bf16[64,1024]{1,0:T(8,128)(2,1)}, bf16[64,1024]{1,0:T(8,128)(2,1)S(1)}, u32[]{:S(2)}, u32[]{:S(2)}) collective-permute-start(bf16[64,1024]{1,0:T(8,128)(2,1)} %refs_4_.1), channel_id=1, source_target_pairs={{0,0},{1,32},{2,64},{3,96},{4,48},{5,80},{6,112},{7,16},{8,65},{9,... | collective-permute-start | bytes 393224 | tf_op jit(solution)/shard_map/ppermute | solution.py:303
  2.9 2.2 %copy-done = bf16[512,4096]{1,0:T(8,128)(2,1)S(1)} copy-done((bf16[512,4096]{1,0:T(8,128)(2,1)S(1)}, bf16[512,4096]{1,0:T(8,128)(2,1)}, u32[]{:S(2)}) %copy-start) | copy-done | bytes 4194328
  5.7 2.8 %shard_map.68 = (bf16[16384,128]{1,0:T(8,128)(2,1)S(1)}, s32[8,128]{1,0:T(8,128)S(1)}) custom-call(s32[256]{0:T(256)S(1)} %copy-done.3, s32[1]{0:T(128)S(6)} %copy.7.counts, bf16[512,4096]{1,0:T(8,128)(2,1)S(1)} %copy-done), custom_call_target="tpu_custom_call" | custom-call | bytes 25165824 | tf_op jit(solution)/shard_map/pallas_call | solution.py:53
  8.7 12.2 %collective-permute-start.3 = (bf16[512,128]{1,0:T(8,128)(2,1)S(1)}, bf16[512,128]{1,0:T(8,128)(2,1)S(1)}, u32[]{:S(2)}, u32[]{:S(2)}) collective-permute-start(bf16[512,128]{1,0:T(8,128)(2,1)S(1)} %shard_map.69), channel_id=1, source_target_pairs={{0,96},{32,0},{64,32},{96,64},{1,97},{33,1},{65,33},{97,65},{2,98}... | collective-permute-start | bytes 393224 | tf_op jit(solution)/shard_map/ppermute | solution.py:291
  21.9 3.0 %collective-permute-done.3 = bf16[512,128]{1,0:T(8,128)(2,1)S(1)} collective-permute-done((bf16[512,128]{1,0:T(8,128)(2,1)S(1)}, bf16[512,128]{1,0:T(8,128)(2,1)S(1)}, u32[]{:S(2)}, u32[]{:S(2)}) %collective-permute-start.3) | collective-permute-done | bytes 131104 | tf_op jit(solution)/shard_map/ppermute | solution.py:291
  24.9 2.7 %collective-permute-done.2 = bf16[512,128]{1,0:T(8,128)(2,1)S(1)} collective-permute-done((bf16[512,128]{1,0:T(8,128)(2,1)S(1)}, bf16[512,128]{1,0:T(8,128)(2,1)S(1)}, u32[]{:S(2)}, u32[]{:S(2)}) %collective-permute-start.2) | collective-permute-done | bytes 131104 | tf_op jit(solution)/shard_map/ppermute | solution.py:291
  28.7 1.9 %collective-permute-done.4.other = bf16[4,512,128]{2,1,0:T(8,128)(2,1)S(1)} collective-permute-done((bf16[4,512,128]{2,1,0:T(8,128)(2,1)S(1)}, bf16[4,512,128]{2,1,0:T(8,128)(2,1)S(1)}, u32[]{:S(2)}, u32[]{:S(2)}) %collective-permute-start.4) | collective-permute-done | bytes 524320 | tf_op jit(solution)/shard_map/ppermute | solution.py:291
  30.6 5.4 %shard_map.70 = (bf16[4,512,128]{2,1,0:T(8,128)(2,1)S(1)}, bf16[4,512,128]{2,1,0:T(8,128)(2,1)S(1)}, bf16[4,512,128]{2,1,0:T(8,128)(2,1)S(1)}, bf16[4,512,128]{2,1,0:T(8,128)(2,1)S(1)}) custom-call(s32[8,128]{1,0:T(8,128)S(1)} %get-tuple-element.14.rows, s32[512]{0:T(512)S(1)} %copy-done.2, s32[1]{0:T(128)S(6)} %copy.7.counts, ...), custom_call_target="tpu_custom_call" | custom-call | flops 268435456 | bytes 8388608 | tf_op jit(solution)/shard_map/pallas_call | solution.py:151
  36.8 4.2 %collective-permute-start.6 = (bf16[4,512,128]{2,1,0:T(8,128)(2,1)S(1)}, bf16[4,512,128]{2,1,0:T(8,128)(2,1)S(1)}, u32[]{:S(2)}, u32[]{:S(2)}) collective-permute-start(bf16[4,512,128]{2,1,0:T(8,128)(2,1)S(1)} %get-tuple-element.18), channel_id=1, source_target_pairs={{0,1},{1,2},{2,3},{3,0},{4,5},{5,6},{6,7},{7,4},{8,9},{9,10},{10,1... | collective-permute-start | bytes 1572872 | tf_op jit(solution)/shard_map/ppermute | solution.py:318
  41.1 5.8 %collective-permute-done.5.refs_1_ = bf16[4,512,128]{2,1,0:T(8,128)(2,1)S(1)} collective-permute-done((bf16[4,512,128]{2,1,0:T(8,128)(2,1)S(1)}, bf16[4,512,128]{2,1,0:T(8,128)(2,1)S(1)}, u32[]{:S(2)}, u32[]{:S(2)}) %collective-permute-start.5) | collective-permute-done | bytes 524320 | tf_op jit(solution)/shard_map/ppermute | solution.py:318
  46.9 5.5 %collective-permute-done.6.refs_2_ = bf16[4,512,128]{2,1,0:T(8,128)(2,1)S(1)} collective-permute-done((bf16[4,512,128]{2,1,0:T(8,128)(2,1)S(1)}, bf16[4,512,128]{2,1,0:T(8,128)(2,1)S(1)}, u32[]{:S(2)}, u32[]{:S(2)}) %collective-permute-start.6) | collective-permute-done | bytes 524320 | tf_op jit(solution)/shard_map/ppermute | solution.py:318
  52.4 1.5 %collective-permute-done.7.refs_3_ = bf16[4,512,128]{2,1,0:T(8,128)(2,1)S(1)} collective-permute-done((bf16[4,512,128]{2,1,0:T(8,128)(2,1)S(1)}, bf16[4,512,128]{2,1,0:T(8,128)(2,1)S(1)}, u32[]{:S(2)}, u32[]{:S(2)}) %collective-permute-start.7) | collective-permute-done | bytes 524320 | tf_op jit(solution)/shard_map/ppermute | solution.py:318
  54.1 2.6 %collective-permute-start.8 = (bf16[512,128]{1,0:T(8,128)(2,1)S(1)}, bf16[512,128]{1,0:T(8,128)(2,1)S(1)}, u32[]{:S(2)}, u32[]{:S(2)}) collective-permute-start(bf16[512,128]{1,0:T(8,128)(2,1)S(1)} %get-tuple-element.21), channel_id=1, source_target_pairs={{0,8},{1,9},{2,10},{3,11},{4,12},{5,13},{6,14},{7,15},{8,0},{9,1},... | collective-permute-start | bytes 393224 | tf_op jit(solution)/shard_map/ppermute | solution.py:318
  57.0 3.0 %collective-permute-start.10 = (bf16[512,128]{1,0:T(8,128)(2,1)S(1)}, bf16[512,128]{1,0:T(8,128)(2,1)S(1)}, u32[]{:S(2)}, u32[]{:S(2)}) collective-permute-start(bf16[512,128]{1,0:T(8,128)(2,1)S(1)} %get-tuple-element.23), channel_id=1, source_target_pairs={{0,12},{1,13},{2,14},{3,15},{4,0},{5,1},{6,2},{7,3},{8,4},{9,5},{1... | collective-permute-start | bytes 393224 | tf_op jit(solution)/shard_map/ppermute | solution.py:318
  60.7 2.3 %collective-permute-done.9.refs_2_ = bf16[512,128]{1,0:T(8,128)(2,1)S(1)} collective-permute-done((bf16[512,128]{1,0:T(8,128)(2,1)S(1)}, bf16[512,128]{1,0:T(8,128)(2,1)S(1)}, u32[]{:S(2)}, u32[]{:S(2)}) %collective-permute-start.9) | collective-permute-done | bytes 131104 | tf_op jit(solution)/shard_map/ppermute | solution.py:318
  64.9 1.8 %collective-permute-start.14 = (f32[64,64]{1,0:T(8,128)S(1)}, f32[64,64]{1,0:T(8,128)S(1)}, u32[]{:S(2)}, u32[]{:S(2)}) collective-permute-start(f32[64,64]{1,0:T(8,128)S(1)} %add.21), channel_id=1, source_target_pairs={{0,3},{1,0},{2,1},{3,2},{4,7},{5,4},{6,5},{7,6},{8,11},{9,8},{10,9... | collective-permute-start | bytes 49160 | tf_op jit(solution)/shard_map/ppermute | solution.py:291
  68.8 3.0 %collective-permute-done.13 = f32[64,64]{1,0:T(8,128)S(1)} collective-permute-done((f32[64,64]{1,0:T(8,128)S(1)}, f32[64,64]{1,0:T(8,128)S(1)}, u32[]{:S(2)}, u32[]{:S(2)}) %collective-permute-start.13) | collective-permute-done | bytes 16416 | tf_op jit(solution)/shard_map/ppermute | solution.py:291
  72.4 3.3 %collective-permute-start.17 = (f32[64,64]{1,0:T(8,128)S(1)}, f32[64,64]{1,0:T(8,128)S(1)}, u32[]{:S(2)}, u32[]{:S(2)}) collective-permute-start(f32[64,64]{1,0:T(8,128)S(1)} %add_add_fusion.1), channel_id=1, source_target_pairs={{0,12},{4,0},{8,4},{12,8},{1,13},{5,1},{9,5},{13,9},{2,14},{6,2},{... | collective-permute-start | bytes 49160 | tf_op jit(solution)/shard_map/ppermute | solution.py:291
  75.7 1.5 %collective-permute-start.15 = (f32[64,64]{1,0:T(8,128)S(1)}, f32[64,64]{1,0:T(8,128)S(1)}, u32[]{:S(2)}, u32[]{:S(2)}) collective-permute-start(f32[64,64]{1,0:T(8,128)S(1)} %add_add_fusion.1), channel_id=1, source_target_pairs={{0,8},{4,12},{8,0},{12,4},{1,9},{5,13},{9,1},{13,5},{2,10},{6,14},... | collective-permute-start | bytes 49160 | tf_op jit(solution)/shard_map/ppermute | solution.py:291
  77.3 3.5 %collective-permute-done.16 = f32[64,64]{1,0:T(8,128)S(1)} collective-permute-done((f32[64,64]{1,0:T(8,128)S(1)}, f32[64,64]{1,0:T(8,128)S(1)}, u32[]{:S(2)}, u32[]{:S(2)}) %collective-permute-start.16) | collective-permute-done | bytes 16416 | tf_op jit(solution)/shard_map/ppermute | solution.py:291
  81.2 2.3 %collective-permute-start.20 = (f32[64,64]{1,0:T(8,128)S(1)}, f32[64,64]{1,0:T(8,128)S(1)}, u32[]{:S(2)}, u32[]{:S(2)}) collective-permute-start(f32[64,64]{1,0:T(8,128)S(1)} %add_add_fusion.g0), channel_id=1, source_target_pairs={{0,96},{32,0},{64,32},{96,64},{1,97},{33,1},{65,33},{97,65},{2,98}... | collective-permute-start | bytes 49160 | tf_op jit(solution)/shard_map/ppermute | solution.py:291
  83.5 1.3 %collective-permute-start.18 = (f32[64,64]{1,0:T(8,128)S(1)}, f32[64,64]{1,0:T(8,128)S(1)}, u32[]{:S(2)}, u32[]{:S(2)}) collective-permute-start(f32[64,64]{1,0:T(8,128)S(1)} %add_add_fusion.g0), channel_id=1, source_target_pairs={{0,32},{32,64},{64,96},{96,0},{1,33},{33,65},{65,97},{97,1},{2,34}... | collective-permute-start | bytes 49160 | tf_op jit(solution)/shard_map/ppermute | solution.py:291
  85.1 3.8 %collective-permute-done.19.g2 = f32[64,64]{1,0:T(8,128)S(1)} collective-permute-done((f32[64,64]{1,0:T(8,128)S(1)}, f32[64,64]{1,0:T(8,128)S(1)}, u32[]{:S(2)}, u32[]{:S(2)}) %collective-permute-start.19) | collective-permute-done | bytes 16416 | tf_op jit(solution)/shard_map/ppermute | solution.py:291
  88.9 2.8 %shard_map.73 = (f32[64,1024]{1,0:T(8,128)}, f32[64,64]{1,0:T(8,128)}) custom-call(f32[64,64]{1,0:T(8,128)S(1)} %add_add_fusion.g0, f32[64,64]{1,0:T(8,128)S(1)} %collective-permute-done.18.g1, f32[64,64]{1,0:T(8,128)S(1)} %collective-permute-done.19.g2, f32[64,64]{1,0:T(8,128)S(1)} %collective-permute-done.20.g3, f32[64,1024]{1,0:T(8,128)S(1)} %get-tuple-element.25.image), custom_call_target="tpu_custom_call" | custom-call | tf_op jit(solution)/shard_map/pallas_call | solution.py:277
  (36 shorter events, 10.4 us)
Async XLA Ops:
  0.6 7.9 %collective-permute-start = (bf16[64,1024]{1,0:T(8,128)(2,1)}, bf16[64,1024]{1,0:T(8,128)(2,1)S(1)}, u32[]{:S(2)}, u32[]{:S(2)}) collective-permute-start(bf16[64,1024]{1,0:T(8,128)(2,1)} %refs_4_.1), channel_id=1, source_target_pairs={{0,0},{1,32},{2,64},{3,96},{4,48},{5,80},{6,112},{7,16},{8,65},{9,... | collective-permute-start | bytes 393224 | tf_op jit(solution)/shard_map/ppermute | solution.py:303
  2.8 2.2 %copy-start = (bf16[512,4096]{1,0:T(8,128)(2,1)S(1)}, bf16[512,4096]{1,0:T(8,128)(2,1)}, u32[]{:S(2)}) copy-start(bf16[512,4096]{1,0:T(8,128)(2,1)} %values.1) | copy-start | bytes 12582916
  5.7 24.9 %copy-start.2 = (s32[512]{0:T(512)S(1)}, s32[512]{0:T(512)}, u32[]{:S(2)}) copy-start(s32[512]{0:T(512)} %tiles.1) | copy-start | bytes 6148
  8.7 16.2 %collective-permute-start.3 = (bf16[512,128]{1,0:T(8,128)(2,1)S(1)}, bf16[512,128]{1,0:T(8,128)(2,1)S(1)}, u32[]{:S(2)}, u32[]{:S(2)}) collective-permute-start(bf16[512,128]{1,0:T(8,128)(2,1)S(1)} %shard_map.69), channel_id=1, source_target_pairs={{0,96},{32,0},{64,32},{96,64},{1,97},{33,1},{65,33},{97,65},{2,98}... | collective-permute-start | bytes 393224 | tf_op jit(solution)/shard_map/ppermute | solution.py:291
  21.0 6.6 %collective-permute-start.2 = (bf16[512,128]{1,0:T(8,128)(2,1)S(1)}, bf16[512,128]{1,0:T(8,128)(2,1)S(1)}, u32[]{:S(2)}, u32[]{:S(2)}) collective-permute-start(bf16[512,128]{1,0:T(8,128)(2,1)S(1)} %shard_map.69), channel_id=1, source_target_pairs={{0,64},{32,96},{64,0},{96,32},{1,65},{33,97},{65,1},{97,33},{2,66}... | collective-permute-start | bytes 393224 | tf_op jit(solution)/shard_map/ppermute | solution.py:291
  21.0 7.6 %collective-permute-start.1 = (bf16[512,128]{1,0:T(8,128)(2,1)S(1)}, bf16[512,128]{1,0:T(8,128)(2,1)S(1)}, u32[]{:S(2)}, u32[]{:S(2)}) collective-permute-start(bf16[512,128]{1,0:T(8,128)(2,1)S(1)} %shard_map.69), channel_id=1, source_target_pairs={{0,32},{32,64},{64,96},{96,0},{1,33},{33,65},{65,97},{97,1},{2,34}... | collective-permute-start | bytes 393224 | tf_op jit(solution)/shard_map/ppermute | solution.py:291
  28.5 34.4 %copy-start.1 = (bf16[64,1024]{1,0:T(8,128)(2,1)S(1)}, bf16[64,1024]{1,0:T(8,128)(2,1)}, u32[]{:S(2)}) copy-start(bf16[64,1024]{1,0:T(8,128)(2,1)} %refs_4_.1) | copy-start | bytes 393220
  28.6 2.0 %collective-permute-start.4 = (bf16[4,512,128]{2,1,0:T(8,128)(2,1)S(1)}, bf16[4,512,128]{2,1,0:T(8,128)(2,1)S(1)}, u32[]{:S(2)}, u32[]{:S(2)}) collective-permute-start(bf16[4,512,128]{2,1,0:T(8,128)(2,1)S(1)} %pad_maximum_fusion.own), channel_id=1, source_target_pairs={{0,16},{16,0},{1,17},{17,1},{2,18},{18,2},{3,19},{19,3},{4,20},{20... | collective-permute-start | bytes 1572872 | tf_op jit(solution)/shard_map/ppermute | solution.py:291
  36.0 10.9 %collective-permute-start.5 = (bf16[4,512,128]{2,1,0:T(8,128)(2,1)S(1)}, bf16[4,512,128]{2,1,0:T(8,128)(2,1)S(1)}, u32[]{:S(2)}, u32[]{:S(2)}) collective-permute-start(bf16[4,512,128]{2,1,0:T(8,128)(2,1)S(1)} %get-tuple-element.17), channel_id=1, source_target_pairs={{0,2},{1,3},{2,0},{3,1},{4,6},{5,7},{6,4},{7,5},{8,10},{9,11},{10,... | collective-permute-start | bytes 1572872 | tf_op jit(solution)/shard_map/ppermute | solution.py:318
  36.8 15.6 %collective-permute-start.6 = (bf16[4,512,128]{2,1,0:T(8,128)(2,1)S(1)}, bf16[4,512,128]{2,1,0:T(8,128)(2,1)S(1)}, u32[]{:S(2)}, u32[]{:S(2)}) collective-permute-start(bf16[4,512,128]{2,1,0:T(8,128)(2,1)S(1)} %get-tuple-element.18), channel_id=1, source_target_pairs={{0,1},{1,2},{2,3},{3,0},{4,5},{5,6},{6,7},{7,4},{8,9},{9,10},{10,1... | collective-permute-start | bytes 1572872 | tf_op jit(solution)/shard_map/ppermute | solution.py:318
  41.1 12.8 %collective-permute-start.7 = (bf16[4,512,128]{2,1,0:T(8,128)(2,1)S(1)}, bf16[4,512,128]{2,1,0:T(8,128)(2,1)S(1)}, u32[]{:S(2)}, u32[]{:S(2)}) collective-permute-start(bf16[4,512,128]{2,1,0:T(8,128)(2,1)S(1)} %get-tuple-element.19), channel_id=1, source_target_pairs={{0,3},{1,0},{2,1},{3,2},{4,7},{5,4},{6,5},{7,6},{8,11},{9,8},{10,9... | collective-permute-start | bytes 1572872 | tf_op jit(solution)/shard_map/ppermute | solution.py:318
  54.1 6.6 %collective-permute-start.8 = (bf16[512,128]{1,0:T(8,128)(2,1)S(1)}, bf16[512,128]{1,0:T(8,128)(2,1)S(1)}, u32[]{:S(2)}, u32[]{:S(2)}) collective-permute-start(bf16[512,128]{1,0:T(8,128)(2,1)S(1)} %get-tuple-element.21), channel_id=1, source_target_pairs={{0,8},{1,9},{2,10},{3,11},{4,12},{5,13},{6,14},{7,15},{8,0},{9,1},... | collective-permute-start | bytes 393224 | tf_op jit(solution)/shard_map/ppermute | solution.py:318
  56.8 6.2 %collective-permute-start.9 = (bf16[512,128]{1,0:T(8,128)(2,1)S(1)}, bf16[512,128]{1,0:T(8,128)(2,1)S(1)}, u32[]{:S(2)}, u32[]{:S(2)}) collective-permute-start(bf16[512,128]{1,0:T(8,128)(2,1)S(1)} %get-tuple-element.22), channel_id=1, source_target_pairs={{0,4},{1,5},{2,6},{3,7},{4,8},{5,9},{6,10},{7,11},{8,12},{9,13},{1... | collective-permute-start | bytes 393224 | tf_op jit(solution)/shard_map/ppermute | solution.py:318
  57.0 5.9 %collective-permute-start.10 = (bf16[512,128]{1,0:T(8,128)(2,1)S(1)}, bf16[512,128]{1,0:T(8,128)(2,1)S(1)}, u32[]{:S(2)}, u32[]{:S(2)}) collective-permute-start(bf16[512,128]{1,0:T(8,128)(2,1)S(1)} %get-tuple-element.23), channel_id=1, source_target_pairs={{0,12},{1,13},{2,14},{3,15},{4,0},{5,1},{6,2},{7,3},{8,4},{9,5},{1... | collective-permute-start | bytes 393224 | tf_op jit(solution)/shard_map/ppermute | solution.py:318
  63.6 1.3 %collective-permute-start.11 = (f32[64,64]{1,0:T(8,128)S(1)}, f32[64,64]{1,0:T(8,128)S(1)}, u32[]{:S(2)}, u32[]{:S(2)}) collective-permute-start(f32[64,64]{1,0:T(8,128)S(1)} %get-tuple-element.24), channel_id=1, source_target_pairs={{0,16},{16,0},{1,17},{17,1},{2,18},{18,2},{3,19},{19,3},{4,20},{20... | collective-permute-start | bytes 49160 | tf_op jit(solution)/shard_map/ppermute | solution.py:291
  64.9 3.9 %collective-permute-start.14 = (f32[64,64]{1,0:T(8,128)S(1)}, f32[64,64]{1,0:T(8,128)S(1)}, u32[]{:S(2)}, u32[]{:S(2)}) collective-permute-start(f32[64,64]{1,0:T(8,128)S(1)} %add.21), channel_id=1, source_target_pairs={{0,3},{1,0},{2,1},{3,2},{4,7},{5,4},{6,5},{7,6},{8,11},{9,8},{10,9... | collective-permute-start | bytes 49160 | tf_op jit(solution)/shard_map/ppermute | solution.py:291
  66.7 5.1 %collective-permute-start.13 = (f32[64,64]{1,0:T(8,128)S(1)}, f32[64,64]{1,0:T(8,128)S(1)}, u32[]{:S(2)}, u32[]{:S(2)}) collective-permute-start(f32[64,64]{1,0:T(8,128)S(1)} %add.21), channel_id=1, source_target_pairs={{0,1},{1,2},{2,3},{3,0},{4,5},{5,6},{6,7},{7,4},{8,9},{9,10},{10,1... | collective-permute-start | bytes 49160 | tf_op jit(solution)/shard_map/ppermute | solution.py:291
  66.9 5.4 %collective-permute-start.12 = (f32[64,64]{1,0:T(8,128)S(1)}, f32[64,64]{1,0:T(8,128)S(1)}, u32[]{:S(2)}, u32[]{:S(2)}) collective-permute-start(f32[64,64]{1,0:T(8,128)S(1)} %add.21), channel_id=1, source_target_pairs={{0,2},{1,3},{2,0},{3,1},{4,6},{5,7},{6,4},{7,5},{8,10},{9,11},{10,... | collective-permute-start | bytes 49160 | tf_op jit(solution)/shard_map/ppermute | solution.py:291
  72.4 4.9 %collective-permute-start.17 = (f32[64,64]{1,0:T(8,128)S(1)}, f32[64,64]{1,0:T(8,128)S(1)}, u32[]{:S(2)}, u32[]{:S(2)}) collective-permute-start(f32[64,64]{1,0:T(8,128)S(1)} %add_add_fusion.1), channel_id=1, source_target_pairs={{0,12},{4,0},{8,4},{12,8},{1,13},{5,1},{9,5},{13,9},{2,14},{6,2},{... | collective-permute-start | bytes 49160 | tf_op jit(solution)/shard_map/ppermute | solution.py:291
  75.7 5.1 %collective-permute-start.16 = (f32[64,64]{1,0:T(8,128)S(1)}, f32[64,64]{1,0:T(8,128)S(1)}, u32[]{:S(2)}, u32[]{:S(2)}) collective-permute-start(f32[64,64]{1,0:T(8,128)S(1)} %add_add_fusion.1), channel_id=1, source_target_pairs={{0,4},{4,8},{8,12},{12,0},{1,5},{5,9},{9,13},{13,1},{2,6},{6,10},{... | collective-permute-start | bytes 49160 | tf_op jit(solution)/shard_map/ppermute | solution.py:291
  75.7 5.5 %collective-permute-start.15 = (f32[64,64]{1,0:T(8,128)S(1)}, f32[64,64]{1,0:T(8,128)S(1)}, u32[]{:S(2)}, u32[]{:S(2)}) collective-permute-start(f32[64,64]{1,0:T(8,128)S(1)} %add_add_fusion.1), channel_id=1, source_target_pairs={{0,8},{4,12},{8,0},{12,4},{1,9},{5,13},{9,1},{13,5},{2,10},{6,14},... | collective-permute-start | bytes 49160 | tf_op jit(solution)/shard_map/ppermute | solution.py:291
  81.2 4.0 %collective-permute-start.20 = (f32[64,64]{1,0:T(8,128)S(1)}, f32[64,64]{1,0:T(8,128)S(1)}, u32[]{:S(2)}, u32[]{:S(2)}) collective-permute-start(f32[64,64]{1,0:T(8,128)S(1)} %add_add_fusion.g0), channel_id=1, source_target_pairs={{0,96},{32,0},{64,32},{96,64},{1,97},{33,1},{65,33},{97,65},{2,98}... | collective-permute-start | bytes 49160 | tf_op jit(solution)/shard_map/ppermute | solution.py:291
  83.5 5.5 %collective-permute-start.19 = (f32[64,64]{1,0:T(8,128)S(1)}, f32[64,64]{1,0:T(8,128)S(1)}, u32[]{:S(2)}, u32[]{:S(2)}) collective-permute-start(f32[64,64]{1,0:T(8,128)S(1)} %add_add_fusion.g0), channel_id=1, source_target_pairs={{0,64},{32,96},{64,0},{96,32},{1,65},{33,97},{65,1},{97,33},{2,66}... | collective-permute-start | bytes 49160 | tf_op jit(solution)/shard_map/ppermute | solution.py:291
  83.5 5.5 %collective-permute-start.18 = (f32[64,64]{1,0:T(8,128)S(1)}, f32[64,64]{1,0:T(8,128)S(1)}, u32[]{:S(2)}, u32[]{:S(2)}) collective-permute-start(f32[64,64]{1,0:T(8,128)S(1)} %add_add_fusion.g0), channel_id=1, source_target_pairs={{0,32},{32,64},{64,96},{96,0},{1,33},{33,65},{65,97},{97,1},{2,34}... | collective-permute-start | bytes 49160 | tf_op jit(solution)/shard_map/ppermute | solution.py:291
  (1 other events, 0.7 us)

commit v4 on v3

--- a/solution.py
+++ b/solution.py
@@ -189,7 +189,7 @@
 
 
 def image_kernel(*refs):
-    ins, (panel, image, gram, spread) = refs[:4], refs[4:]
+    ins, (panel, image, gram, spread, packed) = refs[:4], refs[4:]
     total = ins[0][...]
     for index in range(1, 4):
         total = total + ins[index][...].astype(F32)
@@ -197,13 +197,17 @@
     spread[pl.ds(1, PART, stride=2), :] = pltpu.roll(total, BS, 1)
     whole = spread[...].T[:K, :] + panel[...].astype(F32)
     image[...] = whole
-    gram[...] = lax.dot_general(
+    product = lax.dot_general(
         whole,
         whole,
         (((1,), (1,)), ((), ())),
         precision=lax.Precision.HIGHEST,
         preferred_element_type=F32,
     ) * (1.0 / POINTS)
+    packed[:, :K] = product[: K // 2, :]
+    packed[:, K:] = product[K // 2 :, :]
+    for index in range(COLS):
+        gram[index] = packed[...]
 
 
 def finish_image(arrays, panel):
@@ -214,9 +218,9 @@
         out_specs=[vmem, vmem],
         out_shape=[
             jax.ShapeDtypeStruct((K, PIECE), F32),
-            jax.ShapeDtypeStruct((K, K), F32),
-        ],
-        scratch_shapes=[pltpu.VMEM((PIECE, 128), F32)],
+            jax.ShapeDtypeStruct((COLS, K // 2, 128), F32),
+        ],
+        scratch_shapes=[pltpu.VMEM((PIECE, 128), F32), pltpu.VMEM((K // 2, 128), F32)],
         compiler_params=pltpu.CompilerParams(vmem_limit_bytes=16 * 1024 * 1024),
     )(*arrays, panel)
 
@@ -224,7 +228,8 @@
 def basis_kernel(g0, g1, g2, g3, image, basis, factor, work):
     gram = (g0[...] + g2[...]) + (g1[...] + g3[...])
     work[...] = jnp.zeros_like(work)
-    work[:, :K] = gram
+    work[: K // 2, :K] = gram[:, :K]
+    work[K // 2 :, :K] = pltpu.roll(gram, K, 1)[:, :K]
     lane = lax.broadcasted_iota(jnp.int32, (8, 128), 1)
     sub = lax.broadcasted_iota(jnp.int32, (8, 128), 0)
     groups = []
@@ -331,8 +336,8 @@
     sums = stage_sums([partial[0]] + [across(partial[shift], shift, True) for shift in order])
     arrived = [sums[0]] + [across(sums[shift], shift, False) for shift in order]
     image, gram = finish_image(arrived, panel)
+    gram = jnp.sum(lax.all_to_all(gram, ("y", "x"), 0, 0, tiled=True), axis=0)
     gram = gram + shifted(gram, "core", 1, 2)
-    gram = sum_along(sum_along(gram, "x"), "y")
     grams = [gram] + [shifted(gram, "z", shift) for shift in range(1, 4)]
     basis, factor = orthogonalize(grams, image)
     return (basis, factor)

time: 92.4 us -> 89 us (0.963)
  blocking collectives: 0 us -> 14.1 us
  starting transfers between devices: 37.6 us -> 27.4 us
  waiting for transfers between devices: 37.7 us -> 27.9 us
  Pallas kernels: 12.1 us -> 14.6 us
    all_to_all x0 -> x1, blocking collectives: none -> 14.1 us  [per_device(): gram = jnp.sum(lax.all_to_all(gram, ('y', 'x'), 0, 0, tiled=True), axis=0)]
    ppermute x14 -> x8, starting transfers between devices: 25.1 us -> 15.7 us  [shifted(): lax.ppermute(value, axis, [(i, (i + shift) % size) for i in range(size)])]
    ppermute x14 -> x8, waiting for transfers between devices: 22 us -> 13.7 us  [shifted(): lax.ppermute(value, axis, [(i, (i + shift) % size) for i in range(size)])]
    pallas_call x1, Pallas kernels: 5.41 us -> 7.89 us  [multiply(): pl.pallas_call(multiply_kernel, in_specs=[smem] * 3 + [vmem] * 3, out_spe...]
    ppermute x6, waiting for transfers between devices: 15.8 us -> 14.2 us  [across(): return lax.ppermute(value, AXES, pairs)]
  transfers between devices with their start and end apart: 21 -> 15, of which waited for: 18 -> 12; matrix products, arithmetic and copies ran while one was open for 0% -> 0% of each run, Pallas kernels for 3% -> 3%
where the time goes in v4:
time: 89 us; the launch traced here: 88.5 us
  waiting for transfers between devices  27.9 us (31%)
  starting transfers between devices  27.4 us (31%)
  Pallas kernels  14.6 us (16%)
  blocking collectives  14.1 us (16%)
  local copies, waits for them, and re-layouts  2.87 us (3%)
  between operations  1.38 us (2%)
    ppermute x8, starting transfers between devices, shifted(): lax.ppermute(value, axis, [(i, (i + shift) % size) for i in range(size)])  15.7 us
    ppermute x6, waiting for transfers between devices, across(): return lax.ppermute(value, AXES, pairs)  14.2 us
    all_to_all x1, blocking collectives, per_device(): gram = jnp.sum(lax.all_to_all(gram, ('y', 'x'), 0, 0, tiled=True), axis=0)  14.1 us
    ppermute x8, waiting for transfers between devices, shifted(): lax.ppermute(value, axis, [(i, (i + shift) % size) for i in range(size)])  13.7 us
    ppermute x6, starting transfers between devices, across(): return lax.ppermute(value, AXES, pairs)  10.1 us
    pallas_call x1, Pallas kernels, multiply(): pl.pallas_call(multiply_kernel, in_specs=[smem] * 3 + [vmem] * 3, out_spe...  7.89 us
    unnamed x8, local copies, waits for them, and re-layouts  2.87 us
    pallas_call x1, Pallas kernels, orthogonalize(): pl.pallas_call(basis_kernel, in_specs=[vmem] * 5, out_specs=[vmem, vmem],...  2.78 us
  transfers between devices with their start and end apart: 15, of which 12 were waited for; matrix products, arithmetic and copies ran while one was open for 0% of the time, Pallas kernels for 3%

profile of v4, /device:TPU:0, one launch (start us, length us, event | category | flops | bytes accessed | tf_op | source)
XLA Modules:
  0.0 88.5 jit_solution(15668241791622371668)
XLA Ops:
  0.6 1.6 %collective-permute-start = (bf16[64,1024]{1,0:T(8,128)(2,1)}, bf16[64,1024]{1,0:T(8,128)(2,1)S(1)}, u32[]{:S(2)}, u32[]{:S(2)}) collective-permute-start(bf16[64,1024]{1,0:T(8,128)(2,1)} %refs_4_.1), channel_id=1, source_target_pairs={{0,0},{1,32},{2,64},{3,96},{4,48},{5,80},{6,112},{7,16},{8,65},{9,... | collective-permute-start | bytes 393224 | tf_op jit(solution)/shard_map/ppermute | solution.py:308
  2.9 2.2 %copy-done = bf16[512,4096]{1,0:T(8,128)(2,1)S(1)} copy-done((bf16[512,4096]{1,0:T(8,128)(2,1)S(1)}, bf16[512,4096]{1,0:T(8,128)(2,1)}, u32[]{:S(2)}) %copy-start) | copy-done | bytes 4194328
  5.7 2.8 %shard_map.68 = (bf16[16384,128]{1,0:T(8,128)(2,1)S(1)}, s32[8,128]{1,0:T(8,128)S(1)}) custom-call(s32[256]{0:T(256)S(1)} %copy-done.3, s32[1]{0:T(128)S(6)} %copy.7.counts, bf16[512,4096]{1,0:T(8,128)(2,1)S(1)} %copy-done), custom_call_target="tpu_custom_call" | custom-call | bytes 25165824 | tf_op jit(solution)/shard_map/pallas_call | solution.py:53
  8.7 12.2 %collective-permute-start.3 = (bf16[512,128]{1,0:T(8,128)(2,1)S(1)}, bf16[512,128]{1,0:T(8,128)(2,1)S(1)}, u32[]{:S(2)}, u32[]{:S(2)}) collective-permute-start(bf16[512,128]{1,0:T(8,128)(2,1)S(1)} %shard_map.69), channel_id=1, source_target_pairs={{0,96},{32,0},{64,32},{96,64},{1,97},{33,1},{65,33},{97,65},{2,98}... | collective-permute-start | bytes 393224 | tf_op jit(solution)/shard_map/ppermute | solution.py:296
  21.0 0.9 %collective-permute-start.1 = (bf16[512,128]{1,0:T(8,128)(2,1)S(1)}, bf16[512,128]{1,0:T(8,128)(2,1)S(1)}, u32[]{:S(2)}, u32[]{:S(2)}) collective-permute-start(bf16[512,128]{1,0:T(8,128)(2,1)S(1)} %shard_map.69), channel_id=1, source_target_pairs={{0,32},{32,64},{64,96},{96,0},{1,33},{33,65},{65,97},{97,1},{2,34}... | collective-permute-start | bytes 393224 | tf_op jit(solution)/shard_map/ppermute | solution.py:296
  21.9 3.0 %collective-permute-done.3 = bf16[512,128]{1,0:T(8,128)(2,1)S(1)} collective-permute-done((bf16[512,128]{1,0:T(8,128)(2,1)S(1)}, bf16[512,128]{1,0:T(8,128)(2,1)S(1)}, u32[]{:S(2)}, u32[]{:S(2)}) %collective-permute-start.3) | collective-permute-done | bytes 131104 | tf_op jit(solution)/shard_map/ppermute | solution.py:296
  24.9 2.7 %collective-permute-done.2 = bf16[512,128]{1,0:T(8,128)(2,1)S(1)} collective-permute-done((bf16[512,128]{1,0:T(8,128)(2,1)S(1)}, bf16[512,128]{1,0:T(8,128)(2,1)S(1)}, u32[]{:S(2)}, u32[]{:S(2)}) %collective-permute-start.2) | collective-permute-done | bytes 131104 | tf_op jit(solution)/shard_map/ppermute | solution.py:296
  27.5 1.0 %collective-permute-done.1 = bf16[512,128]{1,0:T(8,128)(2,1)S(1)} collective-permute-done((bf16[512,128]{1,0:T(8,128)(2,1)S(1)}, bf16[512,128]{1,0:T(8,128)(2,1)S(1)}, u32[]{:S(2)}, u32[]{:S(2)}) %collective-permute-start.1) | collective-permute-done | bytes 131104 | tf_op jit(solution)/shard_map/ppermute | solution.py:296
  28.7 1.9 %collective-permute-done.4.other = bf16[4,512,128]{2,1,0:T(8,128)(2,1)S(1)} collective-permute-done((bf16[4,512,128]{2,1,0:T(8,128)(2,1)S(1)}, bf16[4,512,128]{2,1,0:T(8,128)(2,1)S(1)}, u32[]{:S(2)}, u32[]{:S(2)}) %collective-permute-start.4) | collective-permute-done | bytes 524320 | tf_op jit(solution)/shard_map/ppermute | solution.py:296
  30.6 7.9 %shard_map.70 = (bf16[4,512,128]{2,1,0:T(8,128)(2,1)S(1)}, bf16[4,512,128]{2,1,0:T(8,128)(2,1)S(1)}, bf16[4,512,128]{2,1,0:T(8,128)(2,1)S(1)}, bf16[4,512,128]{2,1,0:T(8,128)(2,1)S(1)}) custom-call(s32[8,128]{1,0:T(8,128)S(1)} %get-tuple-element.14.rows, s32[512]{0:T(512)S(1)} %copy-done.2, s32[1]{0:T(128)S(6)} %copy.7.counts, ...), custom_call_target="tpu_custom_call" | custom-call | flops 268435456 | bytes 8388608 | tf_op jit(solution)/shard_map/pallas_call | solution.py:151
  38.6 2.6 %collective-permute-start.6 = (bf16[4,512,128]{2,1,0:T(8,128)(2,1)S(1)}, bf16[4,512,128]{2,1,0:T(8,128)(2,1)S(1)}, u32[]{:S(2)}, u32[]{:S(2)}) collective-permute-start(bf16[4,512,128]{2,1,0:T(8,128)(2,1)S(1)} %get-tuple-element.18), channel_id=1, source_target_pairs={{0,1},{1,2},{2,3},{3,0},{4,5},{5,6},{6,7},{7,4},{8,9},{9,10},{10,1... | collective-permute-start | bytes 1572872 | tf_op jit(solution)/shard_map/ppermute | solution.py:323
  41.2 2.6 %collective-permute-start.7 = (bf16[4,512,128]{2,1,0:T(8,128)(2,1)S(1)}, bf16[4,512,128]{2,1,0:T(8,128)(2,1)S(1)}, u32[]{:S(2)}, u32[]{:S(2)}) collective-permute-start(bf16[4,512,128]{2,1,0:T(8,128)(2,1)S(1)} %get-tuple-element.19), channel_id=1, source_target_pairs={{0,3},{1,0},{2,1},{3,2},{4,7},{5,4},{6,5},{7,6},{8,11},{9,8},{10,9... | collective-permute-start | bytes 1572872 | tf_op jit(solution)/shard_map/ppermute | solution.py:323
  43.8 5.6 %collective-permute-done.5.refs_1_ = bf16[4,512,128]{2,1,0:T(8,128)(2,1)S(1)} collective-permute-done((bf16[4,512,128]{2,1,0:T(8,128)(2,1)S(1)}, bf16[4,512,128]{2,1,0:T(8,128)(2,1)S(1)}, u32[]{:S(2)}, u32[]{:S(2)}) %collective-permute-start.5) | collective-permute-done | bytes 524320 | tf_op jit(solution)/shard_map/ppermute | solution.py:323
  49.4 5.5 %collective-permute-done.6.refs_2_ = bf16[4,512,128]{2,1,0:T(8,128)(2,1)S(1)} collective-permute-done((bf16[4,512,128]{2,1,0:T(8,128)(2,1)S(1)}, bf16[4,512,128]{2,1,0:T(8,128)(2,1)S(1)}, u32[]{:S(2)}, u32[]{:S(2)}) %collective-permute-start.6) | collective-permute-done | bytes 524320 | tf_op jit(solution)/shard_map/ppermute | solution.py:323
  55.2 1.6 %collective-permute-start.8 = (bf16[512,128]{1,0:T(8,128)(2,1)S(1)}, bf16[512,128]{1,0:T(8,128)(2,1)S(1)}, u32[]{:S(2)}, u32[]{:S(2)}) collective-permute-start(bf16[512,128]{1,0:T(8,128)(2,1)S(1)} %get-tuple-element.21), channel_id=1, source_target_pairs={{0,8},{1,9},{2,10},{3,11},{4,12},{5,13},{6,14},{7,15},{8,0},{9,1},... | collective-permute-start | bytes 393224 | tf_op jit(solution)/shard_map/ppermute | solution.py:323
  57.0 3.0 %collective-permute-start.10 = (bf16[512,128]{1,0:T(8,128)(2,1)S(1)}, bf16[512,128]{1,0:T(8,128)(2,1)S(1)}, u32[]{:S(2)}, u32[]{:S(2)}) collective-permute-start(bf16[512,128]{1,0:T(8,128)(2,1)S(1)} %get-tuple-element.23), channel_id=1, source_target_pairs={{0,12},{1,13},{2,14},{3,15},{4,0},{5,1},{6,2},{7,3},{8,4},{9,5},{1... | collective-permute-start | bytes 393224 | tf_op jit(solution)/shard_map/ppermute | solution.py:323
  60.0 1.7 %collective-permute-done.8.refs_1_ = bf16[512,128]{1,0:T(8,128)(2,1)S(1)} collective-permute-done((bf16[512,128]{1,0:T(8,128)(2,1)S(1)}, bf16[512,128]{1,0:T(8,128)(2,1)S(1)}, u32[]{:S(2)}, u32[]{:S(2)}) %collective-permute-start.8) | collective-permute-done | bytes 131104 | tf_op jit(solution)/shard_map/ppermute | solution.py:323
  61.7 1.4 %collective-permute-done.9.refs_2_ = bf16[512,128]{1,0:T(8,128)(2,1)S(1)} collective-permute-done((bf16[512,128]{1,0:T(8,128)(2,1)S(1)}, bf16[512,128]{1,0:T(8,128)(2,1)S(1)}, u32[]{:S(2)}, u32[]{:S(2)}) %collective-permute-start.9) | collective-permute-done | bytes 131104 | tf_op jit(solution)/shard_map/ppermute | solution.py:323
  63.9 14.1 %all_to_all.5 = f32[16,32,128]{2,1,0:T(8,128)S(1)} all-to-all(f32[16,32,128]{2,1,0:T(8,128)S(1)} %get-tuple-element.24), channel_id=1, replica_groups=mesh['z'=4,'core'=2,'y'=4,'x'=4] {'y','x'}, dimensions={0} | all-to-all | bytes 524288 | tf_op jit(solution)/shard_map/all_to_all | solution.py:339
  78.1 1.2 %collective-permute-done.11 = f32[32,128]{1,0:T(8,128)S(1)} collective-permute-done((f32[32,128]{1,0:T(8,128)S(1)}, f32[32,128]{1,0:T(8,128)S(1)}, u32[]{:S(2)}, u32[]{:S(2)}) %collective-permute-start.11) | collective-permute-done | bytes 16416 | tf_op jit(solution)/shard_map/ppermute | solution.py:296
  80.3 1.3 %collective-permute-start.12 = (f32[32,128]{1,0:T(8,128)S(1)}, f32[32,128]{1,0:T(8,128)S(1)}, u32[]{:S(2)}, u32[]{:S(2)}) collective-permute-start(f32[32,128]{1,0:T(8,128)S(1)} %add.3.g0), channel_id=1, source_target_pairs={{0,32},{32,64},{64,96},{96,0},{1,33},{33,65},{65,97},{97,1},{2,34}... | collective-permute-start | bytes 49160 | tf_op jit(solution)/shard_map/ppermute | solution.py:296
  81.7 1.4 %collective-permute-done.14.g3 = f32[32,128]{1,0:T(8,128)S(1)} collective-permute-done((f32[32,128]{1,0:T(8,128)S(1)}, f32[32,128]{1,0:T(8,128)S(1)}, u32[]{:S(2)}, u32[]{:S(2)}) %collective-permute-start.14) | collective-permute-done | bytes 16416 | tf_op jit(solution)/shard_map/ppermute | solution.py:296
  83.0 1.9 %collective-permute-done.13.g2 = f32[32,128]{1,0:T(8,128)S(1)} collective-permute-done((f32[32,128]{1,0:T(8,128)S(1)}, f32[32,128]{1,0:T(8,128)S(1)}, u32[]{:S(2)}, u32[]{:S(2)}) %collective-permute-start.13) | collective-permute-done | bytes 16416 | tf_op jit(solution)/shard_map/ppermute | solution.py:296
  85.7 2.8 %shard_map.73 = (f32[64,1024]{1,0:T(8,128)}, f32[64,64]{1,0:T(8,128)}) custom-call(f32[32,128]{1,0:T(8,128)S(1)} %add.3.g0, f32[32,128]{1,0:T(8,128)S(1)} %collective-permute-done.12.g1, f32[32,128]{1,0:T(8,128)S(1)} %collective-permute-done.13.g2, f32[32,128]{1,0:T(8,128)S(1)} %collective-permute-done.14.g3, f32[64,1024]{1,0:T(8,128)S(1)} %get-tuple-element.25.image), custom_call_target="tpu_custom_call" | custom-call | tf_op jit(solution)/shard_map/pallas_call | solution.py:282
  (24 shorter events, 4.3 us)
Async XLA Ops:
  0.6 7.9 %collective-permute-start = (bf16[64,1024]{1,0:T(8,128)(2,1)}, bf16[64,1024]{1,0:T(8,128)(2,1)S(1)}, u32[]{:S(2)}, u32[]{:S(2)}) collective-permute-start(bf16[64,1024]{1,0:T(8,128)(2,1)} %refs_4_.1), channel_id=1, source_target_pairs={{0,0},{1,32},{2,64},{3,96},{4,48},{5,80},{6,112},{7,16},{8,65},{9,... | collective-permute-start | bytes 393224 | tf_op jit(solution)/shard_map/ppermute | solution.py:308
  2.8 2.2 %copy-start = (bf16[512,4096]{1,0:T(8,128)(2,1)S(1)}, bf16[512,4096]{1,0:T(8,128)(2,1)}, u32[]{:S(2)}) copy-start(bf16[512,4096]{1,0:T(8,128)(2,1)} %values.1) | copy-start | bytes 12582916
  5.0 0.7 copy-start.3
  5.7 24.9 %copy-start.2 = (s32[512]{0:T(512)S(1)}, s32[512]{0:T(512)}, u32[]{:S(2)}) copy-start(s32[512]{0:T(512)} %tiles.1) | copy-start | bytes 6148
  8.7 16.2 %collective-permute-start.3 = (bf16[512,128]{1,0:T(8,128)(2,1)S(1)}, bf16[512,128]{1,0:T(8,128)(2,1)S(1)}, u32[]{:S(2)}, u32[]{:S(2)}) collective-permute-start(bf16[512,128]{1,0:T(8,128)(2,1)S(1)} %shard_map.69), channel_id=1, source_target_pairs={{0,96},{32,0},{64,32},{96,64},{1,97},{33,1},{65,33},{97,65},{2,98}... | collective-permute-start | bytes 393224 | tf_op jit(solution)/shard_map/ppermute | solution.py:296
  21.0 6.6 %collective-permute-start.2 = (bf16[512,128]{1,0:T(8,128)(2,1)S(1)}, bf16[512,128]{1,0:T(8,128)(2,1)S(1)}, u32[]{:S(2)}, u32[]{:S(2)}) collective-permute-start(bf16[512,128]{1,0:T(8,128)(2,1)S(1)} %shard_map.69), channel_id=1, source_target_pairs={{0,64},{32,96},{64,0},{96,32},{1,65},{33,97},{65,1},{97,33},{2,66}... | collective-permute-start | bytes 393224 | tf_op jit(solution)/shard_map/ppermute | solution.py:296
  21.0 7.6 %collective-permute-start.1 = (bf16[512,128]{1,0:T(8,128)(2,1)S(1)}, bf16[512,128]{1,0:T(8,128)(2,1)S(1)}, u32[]{:S(2)}, u32[]{:S(2)}) collective-permute-start(bf16[512,128]{1,0:T(8,128)(2,1)S(1)} %shard_map.69), channel_id=1, source_target_pairs={{0,32},{32,64},{64,96},{96,0},{1,33},{33,65},{65,97},{97,1},{2,34}... | collective-permute-start | bytes 393224 | tf_op jit(solution)/shard_map/ppermute | solution.py:296
  28.5 34.6 %copy-start.1 = (bf16[64,1024]{1,0:T(8,128)(2,1)S(1)}, bf16[64,1024]{1,0:T(8,128)(2,1)}, u32[]{:S(2)}) copy-start(bf16[64,1024]{1,0:T(8,128)(2,1)} %refs_4_.1) | copy-start | bytes 393220
  28.6 2.0 %collective-permute-start.4 = (bf16[4,512,128]{2,1,0:T(8,128)(2,1)S(1)}, bf16[4,512,128]{2,1,0:T(8,128)(2,1)S(1)}, u32[]{:S(2)}, u32[]{:S(2)}) collective-permute-start(bf16[4,512,128]{2,1,0:T(8,128)(2,1)S(1)} %pad_maximum_fusion.own), channel_id=1, source_target_pairs={{0,16},{16,0},{1,17},{17,1},{2,18},{18,2},{3,19},{19,3},{4,20},{20... | collective-permute-start | bytes 1572872 | tf_op jit(solution)/shard_map/ppermute | solution.py:296
  38.5 10.9 %collective-permute-start.5 = (bf16[4,512,128]{2,1,0:T(8,128)(2,1)S(1)}, bf16[4,512,128]{2,1,0:T(8,128)(2,1)S(1)}, u32[]{:S(2)}, u32[]{:S(2)}) collective-permute-start(bf16[4,512,128]{2,1,0:T(8,128)(2,1)S(1)} %get-tuple-element.17), channel_id=1, source_target_pairs={{0,2},{1,3},{2,0},{3,1},{4,6},{5,7},{6,4},{7,5},{8,10},{9,11},{10,... | collective-permute-start | bytes 1572872 | tf_op jit(solution)/shard_map/ppermute | solution.py:323
  38.6 16.3 %collective-permute-start.6 = (bf16[4,512,128]{2,1,0:T(8,128)(2,1)S(1)}, bf16[4,512,128]{2,1,0:T(8,128)(2,1)S(1)}, u32[]{:S(2)}, u32[]{:S(2)}) collective-permute-start(bf16[4,512,128]{2,1,0:T(8,128)(2,1)S(1)} %get-tuple-element.18), channel_id=1, source_target_pairs={{0,1},{1,2},{2,3},{3,0},{4,5},{5,6},{6,7},{7,4},{8,9},{9,10},{10,1... | collective-permute-start | bytes 1572872 | tf_op jit(solution)/shard_map/ppermute | solution.py:323
  41.2 13.7 %collective-permute-start.7 = (bf16[4,512,128]{2,1,0:T(8,128)(2,1)S(1)}, bf16[4,512,128]{2,1,0:T(8,128)(2,1)S(1)}, u32[]{:S(2)}, u32[]{:S(2)}) collective-permute-start(bf16[4,512,128]{2,1,0:T(8,128)(2,1)S(1)} %get-tuple-element.19), channel_id=1, source_target_pairs={{0,3},{1,0},{2,1},{3,2},{4,7},{5,4},{6,5},{7,6},{8,11},{9,8},{10,9... | collective-permute-start | bytes 1572872 | tf_op jit(solution)/shard_map/ppermute | solution.py:323
  55.2 6.6 %collective-permute-start.8 = (bf16[512,128]{1,0:T(8,128)(2,1)S(1)}, bf16[512,128]{1,0:T(8,128)(2,1)S(1)}, u32[]{:S(2)}, u32[]{:S(2)}) collective-permute-start(bf16[512,128]{1,0:T(8,128)(2,1)S(1)} %get-tuple-element.21), channel_id=1, source_target_pairs={{0,8},{1,9},{2,10},{3,11},{4,12},{5,13},{6,14},{7,15},{8,0},{9,1},... | collective-permute-start | bytes 393224 | tf_op jit(solution)/shard_map/ppermute | solution.py:323
  56.8 6.3 %collective-permute-start.9 = (bf16[512,128]{1,0:T(8,128)(2,1)S(1)}, bf16[512,128]{1,0:T(8,128)(2,1)S(1)}, u32[]{:S(2)}, u32[]{:S(2)}) collective-permute-start(bf16[512,128]{1,0:T(8,128)(2,1)S(1)} %get-tuple-element.22), channel_id=1, source_target_pairs={{0,4},{1,5},{2,6},{3,7},{4,8},{5,9},{6,10},{7,11},{8,12},{9,13},{1... | collective-permute-start | bytes 393224 | tf_op jit(solution)/shard_map/ppermute | solution.py:323
  57.0 6.1 %collective-permute-start.10 = (bf16[512,128]{1,0:T(8,128)(2,1)S(1)}, bf16[512,128]{1,0:T(8,128)(2,1)S(1)}, u32[]{:S(2)}, u32[]{:S(2)}) collective-permute-start(bf16[512,128]{1,0:T(8,128)(2,1)S(1)} %get-tuple-element.23), channel_id=1, source_target_pairs={{0,12},{1,13},{2,14},{3,15},{4,0},{5,1},{6,2},{7,3},{8,4},{9,5},{1... | collective-permute-start | bytes 393224 | tf_op jit(solution)/shard_map/ppermute | solution.py:323
  78.0 1.3 %collective-permute-start.11 = (f32[32,128]{1,0:T(8,128)S(1)}, f32[32,128]{1,0:T(8,128)S(1)}, u32[]{:S(2)}, u32[]{:S(2)}) collective-permute-start(f32[32,128]{1,0:T(8,128)S(1)} %reduce_sum.9), channel_id=1, source_target_pairs={{0,16},{16,0},{1,17},{17,1},{2,18},{18,2},{3,19},{19,3},{4,20},{20... | collective-permute-start | bytes 49160 | tf_op jit(solution)/shard_map/ppermute | solution.py:296
  79.3 3.7 %collective-permute-start.14 = (f32[32,128]{1,0:T(8,128)S(1)}, f32[32,128]{1,0:T(8,128)S(1)}, u32[]{:S(2)}, u32[]{:S(2)}) collective-permute-start(f32[32,128]{1,0:T(8,128)S(1)} %add.3.g0), channel_id=1, source_target_pairs={{0,96},{32,0},{64,32},{96,64},{1,97},{33,1},{65,33},{97,65},{2,98}... | collective-permute-start | bytes 49160 | tf_op jit(solution)/shard_map/ppermute | solution.py:296
  79.7 5.2 %collective-permute-start.13 = (f32[32,128]{1,0:T(8,128)S(1)}, f32[32,128]{1,0:T(8,128)S(1)}, u32[]{:S(2)}, u32[]{:S(2)}) collective-permute-start(f32[32,128]{1,0:T(8,128)S(1)} %add.3.g0), channel_id=1, source_target_pairs={{0,64},{32,96},{64,0},{96,32},{1,65},{33,97},{65,1},{97,33},{2,66}... | collective-permute-start | bytes 49160 | tf_op jit(solution)/shard_map/ppermute | solution.py:296
  80.3 5.4 %collective-permute-start.12 = (f32[32,128]{1,0:T(8,128)S(1)}, f32[32,128]{1,0:T(8,128)S(1)}, u32[]{:S(2)}, u32[]{:S(2)}) collective-permute-start(f32[32,128]{1,0:T(8,128)S(1)} %add.3.g0), channel_id=1, source_target_pairs={{0,32},{32,64},{64,96},{96,0},{1,33},{33,65},{65,97},{97,1},{2,34}... | collective-permute-start | bytes 49160 | tf_op jit(solution)/shard_map/ppermute | solution.py:296

commit v5 on v4

--- a/solution.py
+++ b/solution.py
@@ -17,25 +17,55 @@
 HALF = BS // 2
 PART = 512
 PITCH = 40
-UNROLL = 32
+ORDER = (2, 1, 3, 0)
+FIRST = 12
+UNROLL = 64
 AXES = ("z", "core", "y", "x")
 F32 = jnp.float32
 BF16 = jnp.bfloat16
 
 
-def values_kernel(starts, counts, values, out, rows, spread):
+def values_kernel(starts, counts, values, out, rows, order, spread):
     @pl.when(pl.program_id(0) == 0)
     def _():
-        slots = lax.broadcasted_iota(jnp.int32, (8, 128), 0) * 128
-        slots = slots + lax.broadcasted_iota(jnp.int32, (8, 128), 1)
+        core, y, x = lax.axis_index("core"), lax.axis_index("y"), lax.axis_index("x")
+        sub = lax.broadcasted_iota(jnp.int32, (8, 128), 0)
+        lane = lax.broadcasted_iota(jnp.int32, (8, 128), 1)
+        slots = sub * 128 + lane
+        place = slots
+        shift_rows = jnp.zeros_like(slots)
+        live = slots < 0
+        filled = 0
+        steps = []
+        for number in range(COLS):
+            if number == FIRST:
+                steps.append(lax.div(filled + UNROLL - 1, UNROLL))
+                filled = steps[0] * UNROLL
+            far, index = ORDER[number // 4], number % 4
+            to_x, to_y = lax.rem(x + far, 4), lax.rem(y + far, 4)
+            chunk = jnp.where(core == 0, index * 4 + to_x, to_y * 4 + index)
+            low = starts[chunk * 16]
+            after = starts[jnp.minimum(chunk * 16 + 16, RBLK - 1)]
+            high = jnp.where(chunk == COLS - 1, counts[0], after)
+            here = slots >= filled
+            place = jnp.where(here, slots - filled + low, place)
+            shift_rows = jnp.where(here, 16 * (number % FIRST) - 16 * chunk, shift_rows)
+            live = jnp.logical_or(
+                jnp.logical_and(live, jnp.logical_not(here)),
+                jnp.logical_and(here, slots < filled + high - low),
+            )
+            filled = filled + high - low
+        steps.append(lax.div(filled - steps[0] * UNROLL + UNROLL - 1, UNROLL))
 
         def count_up(step, total):
             for offset in range(8):
-                total = total + jnp.where(slots >= starts[step * 8 + offset], 1, 0)
+                total = total + jnp.where(place >= starts[step * 8 + offset], 1, 0)
             return total
 
         total = lax.fori_loop(0, RBLK // 8, count_up, jnp.full((8, 128), -1, jnp.int32))
-        rows[...] = jnp.where(slots < counts[0], total, RBLK)
+        rows[...] = jnp.where(live, total + shift_rows, FIRST * 16)
+        place = jnp.where(live, place, 0)
+        order[...] = jnp.where(sub == 7, jnp.where(lane == 0, steps[0], steps[1]), place)
 
     for group in range(values.shape[0] // 16):
         for tile in range(HALF):
@@ -57,9 +87,11 @@
         out_specs=[
             pl.BlockSpec((step * HALF, 128), lambda i: (i, 0)),
             pl.BlockSpec((8, 128), lambda i: (0, 0)),
+            pl.BlockSpec((8, 128), lambda i: (0, 0)),
         ],
         out_shape=[
             jax.ShapeDtypeStruct((CAP * HALF, 128), BF16),
+            jax.ShapeDtypeStruct((8, 128), jnp.int32),
             jax.ShapeDtypeStruct((8, 128), jnp.int32),
         ],
         scratch_shapes=[pltpu.VMEM((16 * PITCH, 128), F32)],
@@ -93,20 +125,18 @@
     )(panel, rows)
 
 
-def multiply_kernel(rows, tiles, counts, own, other, values, *rest):
-    outs, (weights, total) = rest[:4], rest[4:]
+def fill_weights(own, other, table, weights):
     z, core = lax.axis_index("z"), lax.axis_index("core")
     y, x = lax.axis_index("y"), lax.axis_index("x")
     low = lax.broadcasted_iota(jnp.int32, (HALF, 128), 1) < BS
     zero = jnp.zeros((HALF, 128), F32)
 
     for side, band in enumerate((own, other)):
-
         side = core if side == 0 else 1 - core
-        start = z + 12 - y - 2 * lax.rem(x, 2) - side
-
-        def fill(turn, carry, side=side, start=start, band=band):
-            piece = side * 4 + lax.rem(start - turn, 4)
+
+        def fill(turn, carry, side=side, band=band):
+            source = lax.rem(z + 4 - turn, 4) * 2 + side
+            piece = table[source * COLS + y * 4 + x]
             for block in range(PIECE // BS):
                 pair = band[turn, block * HALF : (block + 1) * HALF, :].astype(F32)
                 swapped = pltpu.roll(pair, BS, 1)
@@ -119,49 +149,70 @@
             return carry
 
         lax.fori_loop(0, 4, fill, 0)
+
+
+def add_products(first, steps, rows, order, tiles, values, weights, total):
     total[...] = jnp.zeros_like(total)
 
     def add_group(index, carry):
+        group = (first + index) * UNROLL
+        major, minor = lax.div(group, 128), lax.rem(group, 128)
         products = []
         for offset in range(UNROLL):
-            slot = index * UNROLL + offset
+            slot = order[major, minor + offset]
             block = values[pl.ds(pl.multiple_of(slot * HALF, HALF), HALF), :]
             tile = weights[pl.ds(pl.multiple_of(tiles[slot] * 128, 128), 128), :]
             products.append(jnp.dot(block, tile, preferred_element_type=F32))
         for offset in range(UNROLL):
-            slot = index * UNROLL + offset
-            where = pl.ds(pl.multiple_of(rows[lax.div(slot, 128), lax.rem(slot, 128)] * HALF, HALF), HALF)
+            where = pl.ds(pl.multiple_of(rows[major, minor + offset] * HALF, HALF), HALF)
             total[where, :] = total[where, :] + products[offset]
         return carry
 
-    rounds = lax.div(counts[0] + UNROLL - 1, UNROLL)
-    lax.fori_loop(0, rounds, add_group, 0)
-    for shift in range(4):
-        to_x = lax.rem(x + shift, 4)
-        to_y = lax.rem(y + shift, 4)
+    lax.fori_loop(0, steps, add_group, 0)
+
+
+def write_chunks(total, outs):
+    for number, out in enumerate(outs):
         for index in range(4):
-            chunk = jnp.where(core == 0, index * 4 + to_x, to_y * 4 + index)
-            first = pl.multiple_of(chunk * PART, PART)
-            outs[shift][index] = total[pl.ds(first, PART), :].astype(BF16)
-
-
-def multiply(rows, tiles, counts, own, other, values):
+            first = (number * 4 + index) * PART
+            out[index] = total[first : first + PART, :].astype(BF16)
+
+
+def first_kernel(rows, order, tiles, table, own, other, values, weights, out0, out1, out2, total):
+    fill_weights(own, other, table, weights)
+    add_products(0, order[7, 0], rows, order, tiles, values, weights, total)
+    write_chunks(total, (out0, out1, out2))
+
+
+def second_kernel(rows, order, tiles, weights, values, out0, total):
+    add_products(order[7, 0], order[7, 1], rows, order, tiles, values, weights, total)
+    write_chunks(total, (out0,))
+
+
+def multiply(rows, tiles, order, own, other, values):
     smem = pl.BlockSpec(memory_space=pltpu.SMEM)
     vmem = pl.BlockSpec(memory_space=pltpu.VMEM)
-    return pl.pallas_call(
-        multiply_kernel,
-        in_specs=[smem] * 3 + [vmem] * 3,
+    chunks = [jax.ShapeDtypeStruct((4, PART, 128), BF16)] * 3
+    total = pltpu.VMEM(((FIRST * 16 + 1) * HALF, 128), F32)
+    params = pltpu.CompilerParams(vmem_limit_bytes=16 * 1024 * 1024)
+    weights, part2, part1, part3 = pl.pallas_call(
+        first_kernel,
+        in_specs=[smem] * 4 + [vmem] * 3,
         out_specs=[vmem] * 4,
-        out_shape=[jax.ShapeDtypeStruct((4, PART, 128), BF16)] * 4,
-        scratch_shapes=[
-            pltpu.VMEM((CBLK * 128, 128), BF16),
-            pltpu.VMEM(((RBLK + 1) * HALF, 128), F32),
-        ],
-        compiler_params=pltpu.CompilerParams(vmem_limit_bytes=24 * 1024 * 1024),
-        cost_estimate=pl.CostEstimate(
-            flops=2 * CAP * BS * BS * K, bytes_accessed=8 * 1024 * 1024, transcendentals=0
-        ),
-    )(rows, tiles, counts, own, other, values)
+        out_shape=[jax.ShapeDtypeStruct((CBLK * 128, 128), BF16)] + chunks,
+        scratch_shapes=[total],
+        compiler_params=params,
+    )(rows, order, tiles, jnp.array(placement()[1], jnp.int32), own, other, values)
+    (part0,) = pl.pallas_call(
+        second_kernel,
+        in_specs=[smem] * 3 + [vmem] * 2,
+        out_specs=[vmem],
+        out_shape=chunks[:1],
+        scratch_shapes=[total],
+        compiler_params=params,
+        cost_estimate=pl.CostEstimate(flops=0, bytes_accessed=16 * 1024 * 1024, transcendentals=0),
+    )(rows, order, tiles, weights, values)
+    return part0, part1, part2, part3
 
 
 def stage_kernel(*refs):
@@ -296,16 +347,29 @@
     return lax.ppermute(value, axis, [(i, (i + shift) % size) for i in range(size)])
 
 
+def ring(a, b):
+    return min((a - b) % 4, (b - a) % 4)
+
+
+def placement():
+    pairs, table = [], [0] * (8 * COLS)
+    for y in range(4):
+        for x in range(4):
+            row = y * 2 + x // 2
+            pieces = []
+            for piece in range(8):
+                from_y, from_x = 2 * (x % 2) + piece // 4, piece % 4
+                pieces.append((-ring(from_y, y) - ring(from_x, x), piece, from_y * 4 + from_x))
+            places = sorted((ring(z, y), z, core) for z in range(4) for core in range(2))
+            for (_, piece, source), (_, z, core) in zip(sorted(pieces), places):
+                target = (z * 2 + core) * COLS + y * 4 + x
+                pairs.append((row * COLS + source, target))
+                table[target] = piece
+    return pairs, table
+
+
 def gather_band(panel, rows):
-    pairs = []
-    for z in range(4):
-        for core in range(2):
-            for y in range(4):
-                for x in range(4):
-                    source = (z * 2 + core) * COLS + y * 4 + x
-                    target = ((z + y + x) % 4 * 2 + y % 2) * COLS + z * 4 + 2 * core + y // 2
-                    pairs.append((source, target))
-    piece = transpose_panel(lax.ppermute(panel, AXES, pairs), rows)
+    piece = transpose_panel(lax.ppermute(panel, AXES, placement()[0]), rows)
     own = jnp.stack([piece] + [shifted(piece, "z", turn) for turn in range(1, 4)])
     return own, shifted(own, "core", 1, 2)
 
@@ -329,12 +393,11 @@
 
 
 def per_device(panel, block_values, row_starts, block_columns, block_counts):
-    values, rows = relayout_values(row_starts, block_counts, block_values)
+    values, rows, order = relayout_values(row_starts, block_counts, block_values)
     own, other = gather_band(panel, rows)
-    partial = multiply(rows, block_columns, block_counts, own, other, values)
-    order = (2, 1, 3)
-    sums = stage_sums([partial[0]] + [across(partial[shift], shift, True) for shift in order])
-    arrived = [sums[0]] + [across(sums[shift], shift, False) for shift in order]
+    partial = multiply(rows, block_columns, order, own, other, values)
+    sums = stage_sums([partial[0]] + [across(partial[shift], shift, True) for shift in ORDER[:3]])
+    arrived = [sums[0]] + [across(sums[shift], shift, False) for shift in ORDER[:3]]
     image, gram = finish_image(arrived, panel)
     gram = jnp.sum(lax.all_to_all(gram, ("y", "x"), 0, 0, tiled=True), axis=0)
     gram = gram + shifted(gram, "core", 1, 2)

time: 89 us -> 87.5 us (0.983)
  Pallas kernels: 14.6 us -> 13.4 us
    ppermute x1, starting transfers between devices: 1.56 us -> 3.48 us  [gather_band(): piece = transpose_panel(lax.ppermute(panel, AXES, placement()[0]), rows)]
    ppermute x8, starting transfers between devices: 15.7 us -> 13.9 us  [shifted(): lax.ppermute(value, axis, [(i, (i + shift) % size) for i in range(size)])]
    pallas_call x1 -> x2, Pallas kernels: 7.89 us -> 6.5 us  [the longest x1 4.12 us: multiply(): pl.pallas_call(first_kernel, in_specs=[smem] * 4 + [vmem] * 3, out_specs=...]
    unnamed x8 -> x10, local copies, waits for them, and re-layouts: 2.87 us -> 2.87 us
  transfers between devices with their start and end apart: 15 -> 15, of which waited for: 12 -> 14; matrix products, arithmetic and copies ran while one was open for 0% -> 0% of each run, Pallas kernels for 3% -> 6%
where the time goes in v5:
time: 87.5 us; the launch traced here: 87.2 us
  waiting for transfers between devices  27.5 us (31%)
  starting transfers between devices  27.3 us (31%)
  blocking collectives  14.7 us (17%)
  Pallas kernels  13.4 us (15%)
  local copies, waits for them, and re-layouts  2.87 us (3%)
  between operations  1.39 us (2%)
    all_to_all x1, blocking collectives, per_device(): gram = jnp.sum(lax.all_to_all(gram, ('y', 'x'), 0, 0, tiled=True), axis=0)  14.7 us
    ppermute x8, starting transfers between devices, shifted(): lax.ppermute(value, axis, [(i, (i + shift) % size) for i in range(size)])  13.9 us
    ppermute x8, waiting for transfers between devices, shifted(): lax.ppermute(value, axis, [(i, (i + shift) % size) for i in range(size)])  13.8 us
    ppermute x6, waiting for transfers between devices, across(): return lax.ppermute(value, AXES, pairs)  13.7 us
    ppermute x6, starting transfers between devices, across(): return lax.ppermute(value, AXES, pairs)  9.92 us
    pallas_call x1, Pallas kernels, multiply(): pl.pallas_call(first_kernel, in_specs=[smem] * 4 + [vmem] * 3, out_specs=...  4.12 us
    ppermute x1, starting transfers between devices, gather_band(): piece = transpose_panel(lax.ppermute(panel, AXES, placement()[0]), rows)  3.48 us
    pallas_call x1, Pallas kernels, relayout_values(): pl.pallas_call(values_kernel, grid=(CAP // step,), in_specs=[smem, smem,...  2.91 us
  transfers between devices with their start and end apart: 15, of which 14 were waited for; matrix products, arithmetic and copies ran while one was open for 0% of the time, Pallas kernels for 6%

profile of v5, /device:TPU:0, one launch (start us, length us, event | category | flops | bytes accessed | tf_op | source)
XLA Modules:
  0.0 87.2 jit_solution(11529414565841268734)
XLA Ops:
  0.6 3.5 %collective-permute-start = (bf16[64,1024]{1,0:T(8,128)(2,1)}, bf16[64,1024]{1,0:T(8,128)(2,1)S(1)}, u32[]{:S(2)}, u32[]{:S(2)}) collective-permute-start(bf16[64,1024]{1,0:T(8,128)(2,1)} %refs_4_.1), channel_id=1, source_target_pairs={{6,0},{2,16},{5,32},{7,48},{1,96},{3,112},{4,64},{0,80},{11,1},{8,... | collective-permute-start | bytes 393224 | tf_op jit(solution)/shard_map/ppermute | solution.py:372
  4.8 2.2 %copy-done = bf16[512,4096]{1,0:T(8,128)(2,1)S(1)} copy-done((bf16[512,4096]{1,0:T(8,128)(2,1)S(1)}, bf16[512,4096]{1,0:T(8,128)(2,1)}, u32[]{:S(2)}) %copy-start) | copy-done | bytes 4194328
  7.6 2.9 %shard_map.77 = (bf16[16384,128]{1,0:T(8,128)(2,1)S(1)}, s32[8,128]{1,0:T(8,128)S(1)}, s32[8,128]{1,0:T(8,128)S(1)}) custom-call(s32[256]{0:T(256)S(1)} %copy-done.3, s32[1]{0:T(128)S(6)} %copy.8.counts, bf16[512,4096]{1,0:T(8,128)(2,1)S(1)} %copy-done), custom_call_target="tpu_custom_call" | custom-call | bytes 25165824 | tf_op jit(solution)/shard_map/pallas_call | solution.py:83
  10.8 9.4 %collective-permute-start.3 = (bf16[512,128]{1,0:T(8,128)(2,1)S(1)}, bf16[512,128]{1,0:T(8,128)(2,1)S(1)}, u32[]{:S(2)}, u32[]{:S(2)}) collective-permute-start(bf16[512,128]{1,0:T(8,128)(2,1)S(1)} %shard_map.78), channel_id=1, source_target_pairs={{0,96},{32,0},{64,32},{96,64},{1,97},{33,1},{65,33},{97,65},{2,98}... | collective-permute-start | bytes 393224 | tf_op jit(solution)/shard_map/ppermute | solution.py:347
  21.2 3.0 %collective-permute-done.3 = bf16[512,128]{1,0:T(8,128)(2,1)S(1)} collective-permute-done((bf16[512,128]{1,0:T(8,128)(2,1)S(1)}, bf16[512,128]{1,0:T(8,128)(2,1)S(1)}, u32[]{:S(2)}, u32[]{:S(2)}) %collective-permute-start.3) | collective-permute-done | bytes 131104 | tf_op jit(solution)/shard_map/ppermute | solution.py:347
  24.2 2.7 %collective-permute-done.2 = bf16[512,128]{1,0:T(8,128)(2,1)S(1)} collective-permute-done((bf16[512,128]{1,0:T(8,128)(2,1)S(1)}, bf16[512,128]{1,0:T(8,128)(2,1)S(1)}, u32[]{:S(2)}, u32[]{:S(2)}) %collective-permute-start.2) | collective-permute-done | bytes 131104 | tf_op jit(solution)/shard_map/ppermute | solution.py:347
  26.8 1.0 %collective-permute-done.1 = bf16[512,128]{1,0:T(8,128)(2,1)S(1)} collective-permute-done((bf16[512,128]{1,0:T(8,128)(2,1)S(1)}, bf16[512,128]{1,0:T(8,128)(2,1)S(1)}, u32[]{:S(2)}, u32[]{:S(2)}) %collective-permute-start.1) | collective-permute-done | bytes 131104 | tf_op jit(solution)/shard_map/ppermute | solution.py:347
  28.0 1.9 %collective-permute-done.4.other = bf16[4,512,128]{2,1,0:T(8,128)(2,1)S(1)} collective-permute-done((bf16[4,512,128]{2,1,0:T(8,128)(2,1)S(1)}, bf16[4,512,128]{2,1,0:T(8,128)(2,1)S(1)}, u32[]{:S(2)}, u32[]{:S(2)}) %collective-permute-start.4) | collective-permute-done | bytes 524320 | tf_op jit(solution)/shard_map/ppermute | solution.py:347
  29.9 4.1 %shard_map.79 = (bf16[16384,128]{1,0:T(8,128)(2,1)S(1)}, bf16[4,512,128]{2,1,0:T(8,128)(2,1)S(1)}, bf16[4,512,128]{2,1,0:T(8,128)(2,1)S(1)}, bf16[4,512,128]{2,1,0:T(8,128)(2,1)S(1)}) custom-call(s32[8,128]{1,0:T(8,128)S(1)} %get-tuple-element.15.rows, s32[8,128]{1,0:T(8,128)S(1)} %get-tuple-element.16.order, s32[512]{0:T(512)S(1)} %copy-done.2, ...), custom_call_target="tpu_custom_call" | custom-call | tf_op jit(solution)/shard_map/pallas_call | solution.py:198
  34.7 3.9 %collective-permute-start.6 = (bf16[4,512,128]{2,1,0:T(8,128)(2,1)S(1)}, bf16[4,512,128]{2,1,0:T(8,128)(2,1)S(1)}, u32[]{:S(2)}, u32[]{:S(2)}) collective-permute-start(bf16[4,512,128]{2,1,0:T(8,128)(2,1)S(1)} %get-tuple-element.20), channel_id=1, source_target_pairs={{0,1},{1,2},{2,3},{3,0},{4,5},{5,6},{6,7},{7,4},{8,9},{9,10},{10,1... | collective-permute-start | bytes 1572872 | tf_op jit(solution)/shard_map/ppermute | solution.py:387
  39.0 2.4 %shard_map.80.refs_0_ = bf16[4,512,128]{2,1,0:T(8,128)(2,1)S(1)} custom-call(s32[8,128]{1,0:T(8,128)S(1)} %get-tuple-element.15.rows, s32[8,128]{1,0:T(8,128)S(1)} %get-tuple-element.16.order, s32[512]{0:T(512)S(1)} %copy-done.2, bf16[16384,128]{1,0:T(8,128)(2,1)S(1)} %get-tuple-element.18.weights, bf16[16384,128]{1,0:T(8,128)(2,1)S(1)} %get-tuple-element.17.values), custom_call_target="tpu_custom_call" | custom-call | bytes 16777216 | tf_op jit(solution)/shard_map/pallas_call | solution.py:206
  41.4 3.5 %collective-permute-done.5.refs_1_ = bf16[4,512,128]{2,1,0:T(8,128)(2,1)S(1)} collective-permute-done((bf16[4,512,128]{2,1,0:T(8,128)(2,1)S(1)}, bf16[4,512,128]{2,1,0:T(8,128)(2,1)S(1)}, u32[]{:S(2)}, u32[]{:S(2)}) %collective-permute-start.5) | collective-permute-done | bytes 524320 | tf_op jit(solution)/shard_map/ppermute | solution.py:387
  44.9 5.5 %collective-permute-done.6.refs_2_ = bf16[4,512,128]{2,1,0:T(8,128)(2,1)S(1)} collective-permute-done((bf16[4,512,128]{2,1,0:T(8,128)(2,1)S(1)}, bf16[4,512,128]{2,1,0:T(8,128)(2,1)S(1)}, u32[]{:S(2)}, u32[]{:S(2)}) %collective-permute-start.6) | collective-permute-done | bytes 524320 | tf_op jit(solution)/shard_map/ppermute | solution.py:387
  51.7 1.4 %collective-permute-start.8 = (bf16[512,128]{1,0:T(8,128)(2,1)S(1)}, bf16[512,128]{1,0:T(8,128)(2,1)S(1)}, u32[]{:S(2)}, u32[]{:S(2)}) collective-permute-start(bf16[512,128]{1,0:T(8,128)(2,1)S(1)} %get-tuple-element.23), channel_id=1, source_target_pairs={{0,8},{1,9},{2,10},{3,11},{4,12},{5,13},{6,14},{7,15},{8,0},{9,1},... | collective-permute-start | bytes 393224 | tf_op jit(solution)/shard_map/ppermute | solution.py:387
  53.0 2.3 %collective-permute-start.9 = (bf16[512,128]{1,0:T(8,128)(2,1)S(1)}, bf16[512,128]{1,0:T(8,128)(2,1)S(1)}, u32[]{:S(2)}, u32[]{:S(2)}) collective-permute-start(bf16[512,128]{1,0:T(8,128)(2,1)S(1)} %get-tuple-element.24), channel_id=1, source_target_pairs={{0,4},{1,5},{2,6},{3,7},{4,8},{5,9},{6,10},{7,11},{8,12},{9,13},{1... | collective-permute-start | bytes 393224 | tf_op jit(solution)/shard_map/ppermute | solution.py:387
  55.3 1.3 %collective-permute-start.10 = (bf16[512,128]{1,0:T(8,128)(2,1)S(1)}, bf16[512,128]{1,0:T(8,128)(2,1)S(1)}, u32[]{:S(2)}, u32[]{:S(2)}) collective-permute-start(bf16[512,128]{1,0:T(8,128)(2,1)S(1)} %get-tuple-element.25), channel_id=1, source_target_pairs={{0,12},{1,13},{2,14},{3,15},{4,0},{5,1},{6,2},{7,3},{8,4},{9,5},{1... | collective-permute-start | bytes 393224 | tf_op jit(solution)/shard_map/ppermute | solution.py:387
  56.6 1.6 %collective-permute-done.8.refs_1_ = bf16[512,128]{1,0:T(8,128)(2,1)S(1)} collective-permute-done((bf16[512,128]{1,0:T(8,128)(2,1)S(1)}, bf16[512,128]{1,0:T(8,128)(2,1)S(1)}, u32[]{:S(2)}, u32[]{:S(2)}) %collective-permute-start.8) | collective-permute-done | bytes 131104 | tf_op jit(solution)/shard_map/ppermute | solution.py:387
  58.2 1.4 %collective-permute-done.9.refs_2_ = bf16[512,128]{1,0:T(8,128)(2,1)S(1)} collective-permute-done((bf16[512,128]{1,0:T(8,128)(2,1)S(1)}, bf16[512,128]{1,0:T(8,128)(2,1)S(1)}, u32[]{:S(2)}, u32[]{:S(2)}) %collective-permute-start.9) | collective-permute-done | bytes 131104 | tf_op jit(solution)/shard_map/ppermute | solution.py:387
  61.0 14.7 %all_to_all.5 = f32[16,32,128]{2,1,0:T(8,128)S(1)} all-to-all(f32[16,32,128]{2,1,0:T(8,128)S(1)} %get-tuple-element.26), channel_id=1, replica_groups=mesh['z'=4,'core'=2,'y'=4,'x'=4] {'y','x'}, dimensions={0} | all-to-all | bytes 524288 | tf_op jit(solution)/shard_map/all_to_all | solution.py:402
  75.9 1.2 %collective-permute-done.11 = f32[32,128]{1,0:T(8,128)S(1)} collective-permute-done((f32[32,128]{1,0:T(8,128)S(1)}, f32[32,128]{1,0:T(8,128)S(1)}, u32[]{:S(2)}, u32[]{:S(2)}) %collective-permute-start.11) | collective-permute-done | bytes 16416 | tf_op jit(solution)/shard_map/ppermute | solution.py:347
  77.9 1.6 %collective-permute-start.13 = (f32[32,128]{1,0:T(8,128)S(1)}, f32[32,128]{1,0:T(8,128)S(1)}, u32[]{:S(2)}, u32[]{:S(2)}) collective-permute-start(f32[32,128]{1,0:T(8,128)S(1)} %add.3.g0), channel_id=1, source_target_pairs={{0,64},{32,96},{64,0},{96,32},{1,65},{33,97},{65,1},{97,33},{2,66}... | collective-permute-start | bytes 49160 | tf_op jit(solution)/shard_map/ppermute | solution.py:347
  80.8 2.5 %collective-permute-done.13.g2 = f32[32,128]{1,0:T(8,128)S(1)} collective-permute-done((f32[32,128]{1,0:T(8,128)S(1)}, f32[32,128]{1,0:T(8,128)S(1)}, u32[]{:S(2)}, u32[]{:S(2)}) %collective-permute-start.13) | collective-permute-done | bytes 16416 | tf_op jit(solution)/shard_map/ppermute | solution.py:347
  83.3 1.2 %collective-permute-done.12.g1 = f32[32,128]{1,0:T(8,128)S(1)} collective-permute-done((f32[32,128]{1,0:T(8,128)S(1)}, f32[32,128]{1,0:T(8,128)S(1)}, u32[]{:S(2)}, u32[]{:S(2)}) %collective-permute-start.12) | collective-permute-done | bytes 16416 | tf_op jit(solution)/shard_map/ppermute | solution.py:347
  84.5 2.8 %shard_map.83 = (f32[64,1024]{1,0:T(8,128)}, f32[64,64]{1,0:T(8,128)}) custom-call(f32[32,128]{1,0:T(8,128)S(1)} %add.3.g0, f32[32,128]{1,0:T(8,128)S(1)} %collective-permute-done.12.g1, f32[32,128]{1,0:T(8,128)S(1)} %collective-permute-done.13.g2, f32[32,128]{1,0:T(8,128)S(1)} %collective-permute-done.14.g3, f32[64,1024]{1,0:T(8,128)S(1)} %get-tuple-element.27.image), custom_call_target="tpu_custom_call" | custom-call | tf_op jit(solution)/shard_map/pallas_call | solution.py:333
  (27 shorter events, 8.0 us)
Async XLA Ops:
  0.6 29.3 %copy-start.4 = (s32[128]{0:T(128)S(1)}, s32[128]{0:T(128)}, u32[]{:S(2)}) copy-start(s32[128]{0:T(128)} %constant.4.clone.table) | copy-start | bytes 1540
  0.6 9.9 %collective-permute-start = (bf16[64,1024]{1,0:T(8,128)(2,1)}, bf16[64,1024]{1,0:T(8,128)(2,1)S(1)}, u32[]{:S(2)}, u32[]{:S(2)}) collective-permute-start(bf16[64,1024]{1,0:T(8,128)(2,1)} %refs_4_.1), channel_id=1, source_target_pairs={{6,0},{2,16},{5,32},{7,48},{1,96},{3,112},{4,64},{0,80},{11,1},{8,... | collective-permute-start | bytes 393224 | tf_op jit(solution)/shard_map/ppermute | solution.py:372
  4.8 2.2 %copy-start = (bf16[512,4096]{1,0:T(8,128)(2,1)S(1)}, bf16[512,4096]{1,0:T(8,128)(2,1)}, u32[]{:S(2)}) copy-start(bf16[512,4096]{1,0:T(8,128)(2,1)} %values.1) | copy-start | bytes 12582916
  7.0 0.7 copy-start.3
  7.6 22.3 %copy-start.2 = (s32[512]{0:T(512)S(1)}, s32[512]{0:T(512)}, u32[]{:S(2)}) copy-start(s32[512]{0:T(512)} %tiles.3) | copy-start | bytes 6148
  10.8 13.4 %collective-permute-start.3 = (bf16[512,128]{1,0:T(8,128)(2,1)S(1)}, bf16[512,128]{1,0:T(8,128)(2,1)S(1)}, u32[]{:S(2)}, u32[]{:S(2)}) collective-permute-start(bf16[512,128]{1,0:T(8,128)(2,1)S(1)} %shard_map.78), channel_id=1, source_target_pairs={{0,96},{32,0},{64,32},{96,64},{1,97},{33,1},{65,33},{97,65},{2,98}... | collective-permute-start | bytes 393224 | tf_op jit(solution)/shard_map/ppermute | solution.py:347
  20.2 6.6 %collective-permute-start.2 = (bf16[512,128]{1,0:T(8,128)(2,1)S(1)}, bf16[512,128]{1,0:T(8,128)(2,1)S(1)}, u32[]{:S(2)}, u32[]{:S(2)}) collective-permute-start(bf16[512,128]{1,0:T(8,128)(2,1)S(1)} %shard_map.78), channel_id=1, source_target_pairs={{0,64},{32,96},{64,0},{96,32},{1,65},{33,97},{65,1},{97,33},{2,66}... | collective-permute-start | bytes 393224 | tf_op jit(solution)/shard_map/ppermute | solution.py:347
  20.2 7.6 %collective-permute-start.1 = (bf16[512,128]{1,0:T(8,128)(2,1)S(1)}, bf16[512,128]{1,0:T(8,128)(2,1)S(1)}, u32[]{:S(2)}, u32[]{:S(2)}) collective-permute-start(bf16[512,128]{1,0:T(8,128)(2,1)S(1)} %shard_map.78), channel_id=1, source_target_pairs={{0,32},{32,64},{64,96},{96,0},{1,33},{33,65},{65,97},{97,1},{2,34}... | collective-permute-start | bytes 393224 | tf_op jit(solution)/shard_map/ppermute | solution.py:347
  27.9 2.0 %collective-permute-start.4 = (bf16[4,512,128]{2,1,0:T(8,128)(2,1)S(1)}, bf16[4,512,128]{2,1,0:T(8,128)(2,1)S(1)}, u32[]{:S(2)}, u32[]{:S(2)}) collective-permute-start(bf16[4,512,128]{2,1,0:T(8,128)(2,1)S(1)} %pad_maximum_fusion.own), channel_id=1, source_target_pairs={{0,16},{16,0},{1,17},{17,1},{2,18},{18,2},{3,19},{19,3},{4,20},{20... | collective-permute-start | bytes 1572872 | tf_op jit(solution)/shard_map/ppermute | solution.py:347
  34.0 10.9 %collective-permute-start.5 = (bf16[4,512,128]{2,1,0:T(8,128)(2,1)S(1)}, bf16[4,512,128]{2,1,0:T(8,128)(2,1)S(1)}, u32[]{:S(2)}, u32[]{:S(2)}) collective-permute-start(bf16[4,512,128]{2,1,0:T(8,128)(2,1)S(1)} %get-tuple-element.19), channel_id=1, source_target_pairs={{0,2},{1,3},{2,0},{3,1},{4,6},{5,7},{6,4},{7,5},{8,10},{9,11},{10,... | collective-permute-start | bytes 1572872 | tf_op jit(solution)/shard_map/ppermute | solution.py:387
  34.7 15.7 %collective-permute-start.6 = (bf16[4,512,128]{2,1,0:T(8,128)(2,1)S(1)}, bf16[4,512,128]{2,1,0:T(8,128)(2,1)S(1)}, u32[]{:S(2)}, u32[]{:S(2)}) collective-permute-start(bf16[4,512,128]{2,1,0:T(8,128)(2,1)S(1)} %get-tuple-element.20), channel_id=1, source_target_pairs={{0,1},{1,2},{2,3},{3,0},{4,5},{5,6},{6,7},{7,4},{8,9},{9,10},{10,1... | collective-permute-start | bytes 1572872 | tf_op jit(solution)/shard_map/ppermute | solution.py:387
  38.6 12.8 %collective-permute-start.7 = (bf16[4,512,128]{2,1,0:T(8,128)(2,1)S(1)}, bf16[4,512,128]{2,1,0:T(8,128)(2,1)S(1)}, u32[]{:S(2)}, u32[]{:S(2)}) collective-permute-start(bf16[4,512,128]{2,1,0:T(8,128)(2,1)S(1)} %get-tuple-element.21), channel_id=1, source_target_pairs={{0,3},{1,0},{2,1},{3,2},{4,7},{5,4},{6,5},{7,6},{8,11},{9,8},{10,9... | collective-permute-start | bytes 1572872 | tf_op jit(solution)/shard_map/ppermute | solution.py:387
  39.0 21.3 %copy-start.1 = (bf16[64,1024]{1,0:T(8,128)(2,1)S(1)}, bf16[64,1024]{1,0:T(8,128)(2,1)}, u32[]{:S(2)}) copy-start(bf16[64,1024]{1,0:T(8,128)(2,1)} %refs_4_.1) | copy-start | bytes 393220
  51.7 6.6 %collective-permute-start.8 = (bf16[512,128]{1,0:T(8,128)(2,1)S(1)}, bf16[512,128]{1,0:T(8,128)(2,1)S(1)}, u32[]{:S(2)}, u32[]{:S(2)}) collective-permute-start(bf16[512,128]{1,0:T(8,128)(2,1)S(1)} %get-tuple-element.23), channel_id=1, source_target_pairs={{0,8},{1,9},{2,10},{3,11},{4,12},{5,13},{6,14},{7,15},{8,0},{9,1},... | collective-permute-start | bytes 393224 | tf_op jit(solution)/shard_map/ppermute | solution.py:387
  53.0 6.6 %collective-permute-start.9 = (bf16[512,128]{1,0:T(8,128)(2,1)S(1)}, bf16[512,128]{1,0:T(8,128)(2,1)S(1)}, u32[]{:S(2)}, u32[]{:S(2)}) collective-permute-start(bf16[512,128]{1,0:T(8,128)(2,1)S(1)} %get-tuple-element.24), channel_id=1, source_target_pairs={{0,4},{1,5},{2,6},{3,7},{4,8},{5,9},{6,10},{7,11},{8,12},{9,13},{1... | collective-permute-start | bytes 393224 | tf_op jit(solution)/shard_map/ppermute | solution.py:387
  55.3 5.0 %collective-permute-start.10 = (bf16[512,128]{1,0:T(8,128)(2,1)S(1)}, bf16[512,128]{1,0:T(8,128)(2,1)S(1)}, u32[]{:S(2)}, u32[]{:S(2)}) collective-permute-start(bf16[512,128]{1,0:T(8,128)(2,1)S(1)} %get-tuple-element.25), channel_id=1, source_target_pairs={{0,12},{1,13},{2,14},{3,15},{4,0},{5,1},{6,2},{7,3},{8,4},{9,5},{1... | collective-permute-start | bytes 393224 | tf_op jit(solution)/shard_map/ppermute | solution.py:387
  75.8 1.3 %collective-permute-start.11 = (f32[32,128]{1,0:T(8,128)S(1)}, f32[32,128]{1,0:T(8,128)S(1)}, u32[]{:S(2)}, u32[]{:S(2)}) collective-permute-start(f32[32,128]{1,0:T(8,128)S(1)} %reduce_sum.9), channel_id=1, source_target_pairs={{0,16},{16,0},{1,17},{17,1},{2,18},{18,2},{3,19},{19,3},{4,20},{20... | collective-permute-start | bytes 49160 | tf_op jit(solution)/shard_map/ppermute | solution.py:347
  77.0 3.7 %collective-permute-start.14 = (f32[32,128]{1,0:T(8,128)S(1)}, f32[32,128]{1,0:T(8,128)S(1)}, u32[]{:S(2)}, u32[]{:S(2)}) collective-permute-start(f32[32,128]{1,0:T(8,128)S(1)} %add.3.g0), channel_id=1, source_target_pairs={{0,96},{32,0},{64,32},{96,64},{1,97},{33,1},{65,33},{97,65},{2,98}... | collective-permute-start | bytes 49160 | tf_op jit(solution)/shard_map/ppermute | solution.py:347
  77.9 5.3 %collective-permute-start.13 = (f32[32,128]{1,0:T(8,128)S(1)}, f32[32,128]{1,0:T(8,128)S(1)}, u32[]{:S(2)}, u32[]{:S(2)}) collective-permute-start(f32[32,128]{1,0:T(8,128)S(1)} %add.3.g0), channel_id=1, source_target_pairs={{0,64},{32,96},{64,0},{96,32},{1,65},{33,97},{65,1},{97,33},{2,66}... | collective-permute-start | bytes 49160 | tf_op jit(solution)/shard_map/ppermute | solution.py:347
  79.5 4.9 %collective-permute-start.12 = (f32[32,128]{1,0:T(8,128)S(1)}, f32[32,128]{1,0:T(8,128)S(1)}, u32[]{:S(2)}, u32[]{:S(2)}) collective-permute-start(f32[32,128]{1,0:T(8,128)S(1)} %add.3.g0), channel_id=1, source_target_pairs={{0,32},{32,64},{64,96},{96,0},{1,33},{33,65},{65,97},{97,1},{2,34}... | collective-permute-start | bytes 49160 | tf_op jit(solution)/shard_map/ppermute | solution.py:347

commit v6 on v5

--- a/solution.py
+++ b/solution.py
@@ -125,30 +125,49 @@
     )(panel, rows)
 
 
-def fill_weights(own, other, table, weights):
+PIECE_ROWS = PIECE // BS * 128
+
+
+def piece_place(turn, mine, table):
     z, core = lax.axis_index("z"), lax.axis_index("core")
     y, x = lax.axis_index("y"), lax.axis_index("x")
+    side = core if mine else 1 - core
+    return table[(lax.rem(z + 4 - turn, 4) * 2 + side) * COLS + y * 4 + x]
+
+
+def fill_weights(band, place, weights):
     low = lax.broadcasted_iota(jnp.int32, (HALF, 128), 1) < BS
     zero = jnp.zeros((HALF, 128), F32)
 
-    for side, band in enumerate((own, other)):
-        side = core if side == 0 else 1 - core
-
-        def fill(turn, carry, side=side, band=band):
-            source = lax.rem(z + 4 - turn, 4) * 2 + side
-            piece = table[source * COLS + y * 4 + x]
-            for block in range(PIECE // BS):
-                pair = band[turn, block * HALF : (block + 1) * HALF, :].astype(F32)
-                swapped = pltpu.roll(pair, BS, 1)
-                tile = piece * (PIECE // BS) + block
-                first = pl.multiple_of(tile * 128, 128)
-                weights[pl.ds(first, HALF), :] = jnp.where(low, pair, zero).astype(BF16)
-                weights[pl.ds(first + 32, HALF), :] = jnp.where(low, swapped, zero).astype(BF16)
-                weights[pl.ds(first + 64, HALF), :] = jnp.where(low, zero, swapped).astype(BF16)
-                weights[pl.ds(first + 96, HALF), :] = jnp.where(low, zero, pair).astype(BF16)
-            return carry
-
-        lax.fori_loop(0, 4, fill, 0)
+    def fill(turn, carry):
+        piece = place(turn)
+        for block in range(PIECE // BS):
+            pair = band[turn, block * HALF : (block + 1) * HALF, :].astype(F32)
+            swapped = pltpu.roll(pair, BS, 1)
+            tile = piece * (PIECE // BS) + block
+            first = pl.multiple_of(tile * 128, 128)
+            weights[pl.ds(first, HALF), :] = jnp.where(low, pair, zero).astype(BF16)
+            weights[pl.ds(first + 32, HALF), :] = jnp.where(low, swapped, zero).astype(BF16)
+            weights[pl.ds(first + 64, HALF), :] = jnp.where(low, zero, swapped).astype(BF16)
+            weights[pl.ds(first + 96, HALF), :] = jnp.where(low, zero, pair).astype(BF16)
+        return carry
+
+    lax.fori_loop(0, 4, fill, 0)
+
+
+def own_kernel(own, weights):
+    fill_weights(own, lambda turn: turn, weights)
+
+
+def own_weights(own):
+    vmem = pl.BlockSpec(memory_space=pltpu.VMEM)
+    return pl.pallas_call(
+        own_kernel,
+        in_specs=[vmem],
+        out_specs=vmem,
+        out_shape=jax.ShapeDtypeStruct((4 * PIECE_ROWS, 128), BF16),
+        compiler_params=pltpu.CompilerParams(vmem_limit_bytes=16 * 1024 * 1024),
+    )(own)
 
 
 def add_products(first, steps, rows, order, tiles, values, weights, total):
@@ -178,8 +197,18 @@
             out[index] = total[first : first + PART, :].astype(BF16)
 
 
-def first_kernel(rows, order, tiles, table, own, other, values, weights, out0, out1, out2, total):
-    fill_weights(own, other, table, weights)
+def first_kernel(rows, order, tiles, table, other, values, half, weights, out0, out1, out2, total, sems):
+    copies = []
+    for turn in range(4):
+        first = pl.multiple_of(piece_place(turn, True, table) * PIECE_ROWS, PIECE_ROWS)
+        source = half.at[pl.ds(turn * PIECE_ROWS, PIECE_ROWS), :]
+        target = weights.at[pl.ds(first, PIECE_ROWS), :]
+        copies.append(pltpu.make_async_copy(source, target, sems.at[turn]))
+    for copy in copies:
+        copy.start()
+    fill_weights(other, lambda turn: piece_place(turn, False, table), weights)
+    for copy in copies:
+        copy.wait()
     add_products(0, order[7, 0], rows, order, tiles, values, weights, total)
     write_chunks(total, (out0, out1, out2))
 
@@ -195,14 +224,16 @@
     chunks = [jax.ShapeDtypeStruct((4, PART, 128), BF16)] * 3
     total = pltpu.VMEM(((FIRST * 16 + 1) * HALF, 128), F32)
     params = pltpu.CompilerParams(vmem_limit_bytes=16 * 1024 * 1024)
+    table = jnp.array(placement()[1], jnp.int32)
+    half = own_weights(own)
     weights, part2, part1, part3 = pl.pallas_call(
         first_kernel,
         in_specs=[smem] * 4 + [vmem] * 3,
         out_specs=[vmem] * 4,
         out_shape=[jax.ShapeDtypeStruct((CBLK * 128, 128), BF16)] + chunks,
-        scratch_shapes=[total],
+        scratch_shapes=[total, pltpu.SemaphoreType.DMA((4,))],
         compiler_params=params,
-    )(rows, order, tiles, jnp.array(placement()[1], jnp.int32), own, other, values)
+    )(rows, order, tiles, table, other, values, half)
     (part0,) = pl.pallas_call(
         second_kernel,
         in_specs=[smem] * 3 + [vmem] * 2,

time: 87.5 us -> 87.7 us (level)
  starting transfers between devices: 27.3 us -> 29.3 us
  waiting for transfers between devices: 27.5 us -> 25.8 us
    ppermute x6, starting transfers between devices: 9.92 us -> 11.3 us  [across(): return lax.ppermute(value, AXES, pairs)]
    ppermute x8, waiting for transfers between devices: 13.8 us -> 12.8 us  [shifted(): lax.ppermute(value, axis, [(i, (i + shift) % size) for i in range(size)])]
  transfers between devices with their start and end apart: 15 -> 15, of which waited for: 14 -> 13; matrix products, arithmetic and copies ran while one was open for 0% -> 0% of each run, Pallas kernels for 6% -> 6%
where the time goes in v6:
time: 87.7 us; the launch traced here: 87.8 us
  starting transfers between devices  29.3 us (33%)
  waiting for transfers between devices  25.8 us (29%)
  blocking collectives  15.4 us (18%)
  Pallas kernels  12.9 us (15%)
  local copies, waits for them, and re-layouts  2.87 us (3%)
  between operations  1.4 us (2%)
    all_to_all x1, blocking collectives, per_device(): gram = jnp.sum(lax.all_to_all(gram, ('y', 'x'), 0, 0, tiled=True), axis=0)  15.4 us
    ppermute x8, starting transfers between devices, shifted(): lax.ppermute(value, axis, [(i, (i + shift) % size) for i in range(size)])  14.5 us
    ppermute x6, waiting for transfers between devices, across(): return lax.ppermute(value, AXES, pairs)  13 us
    ppermute x8, waiting for transfers between devices, shifted(): lax.ppermute(value, axis, [(i, (i + shift) % size) for i in range(size)])  12.8 us
    ppermute x6, starting transfers between devices, across(): return lax.ppermute(value, AXES, pairs)  11.3 us
    pallas_call x1, Pallas kernels, multiply(): pl.pallas_call(first_kernel, in_specs=[smem] * 4 + [vmem] * 3, out_specs=...  3.87 us
    ppermute x1, starting transfers between devices, gather_band(): piece = transpose_panel(lax.ppermute(panel, AXES, placement()[0]), rows)  3.48 us
    pallas_call x1, Pallas kernels, relayout_values(): pl.pallas_call(values_kernel, grid=(CAP // step,), in_specs=[smem, smem,...  2.9 us
  transfers between devices with their start and end apart: 15, of which 13 were waited for; matrix products, arithmetic and copies ran while one was open for 0% of the time, Pallas kernels for 6%

profile of v6, /device:TPU:0, one launch (start us, length us, event | category | flops | bytes accessed | tf_op | source)
XLA Modules:
  0.0 87.8 jit_solution(15325179987784472632)
XLA Ops:
  0.6 3.5 %collective-permute-start = (bf16[64,1024]{1,0:T(8,128)(2,1)}, bf16[64,1024]{1,0:T(8,128)(2,1)S(1)}, u32[]{:S(2)}, u32[]{:S(2)}) collective-permute-start(bf16[64,1024]{1,0:T(8,128)(2,1)} %refs_4_.1), channel_id=1, source_target_pairs={{6,0},{2,16},{5,32},{7,48},{1,96},{3,112},{4,64},{0,80},{11,1},{8,... | collective-permute-start | bytes 393224 | tf_op jit(solution)/shard_map/ppermute | solution.py:403
  4.8 2.2 %copy-done = bf16[512,4096]{1,0:T(8,128)(2,1)S(1)} copy-done((bf16[512,4096]{1,0:T(8,128)(2,1)S(1)}, bf16[512,4096]{1,0:T(8,128)(2,1)}, u32[]{:S(2)}) %copy-start) | copy-done | bytes 4194328
  7.6 2.9 %shard_map.77 = (bf16[16384,128]{1,0:T(8,128)(2,1)S(1)}, s32[8,128]{1,0:T(8,128)S(1)}, s32[8,128]{1,0:T(8,128)S(1)}) custom-call(s32[256]{0:T(256)S(1)} %copy-done.3, s32[1]{0:T(128)S(6)} %copy.8.counts, bf16[512,4096]{1,0:T(8,128)(2,1)S(1)} %copy-done), custom_call_target="tpu_custom_call" | custom-call | bytes 25165824 | tf_op jit(solution)/shard_map/pallas_call | solution.py:83
  10.8 9.4 %collective-permute-start.3 = (bf16[512,128]{1,0:T(8,128)(2,1)S(1)}, bf16[512,128]{1,0:T(8,128)(2,1)S(1)}, u32[]{:S(2)}, u32[]{:S(2)}) collective-permute-start(bf16[512,128]{1,0:T(8,128)(2,1)S(1)} %shard_map.78), channel_id=1, source_target_pairs={{0,96},{32,0},{64,32},{96,64},{1,97},{33,1},{65,33},{97,65},{2,98}... | collective-permute-start | bytes 393224 | tf_op jit(solution)/shard_map/ppermute | solution.py:378
  21.2 3.0 %collective-permute-done.3 = bf16[512,128]{1,0:T(8,128)(2,1)S(1)} collective-permute-done((bf16[512,128]{1,0:T(8,128)(2,1)S(1)}, bf16[512,128]{1,0:T(8,128)(2,1)S(1)}, u32[]{:S(2)}, u32[]{:S(2)}) %collective-permute-start.3) | collective-permute-done | bytes 131104 | tf_op jit(solution)/shard_map/ppermute | solution.py:378
  24.2 2.7 %collective-permute-done.2 = bf16[512,128]{1,0:T(8,128)(2,1)S(1)} collective-permute-done((bf16[512,128]{1,0:T(8,128)(2,1)S(1)}, bf16[512,128]{1,0:T(8,128)(2,1)S(1)}, u32[]{:S(2)}, u32[]{:S(2)}) %collective-permute-start.2) | collective-permute-done | bytes 131104 | tf_op jit(solution)/shard_map/ppermute | solution.py:378
  28.5 1.4 %collective-permute-done.4.other = bf16[4,512,128]{2,1,0:T(8,128)(2,1)S(1)} collective-permute-done((bf16[4,512,128]{2,1,0:T(8,128)(2,1)S(1)}, bf16[4,512,128]{2,1,0:T(8,128)(2,1)S(1)}, u32[]{:S(2)}, u32[]{:S(2)}) %collective-permute-start.4) | collective-permute-done | bytes 524320 | tf_op jit(solution)/shard_map/ppermute | solution.py:378
  29.9 3.9 %shard_map.80 = (bf16[16384,128]{1,0:T(8,128)(2,1)S(1)}, bf16[4,512,128]{2,1,0:T(8,128)(2,1)S(1)}, bf16[4,512,128]{2,1,0:T(8,128)(2,1)S(1)}, bf16[4,512,128]{2,1,0:T(8,128)(2,1)S(1)}) custom-call(s32[8,128]{1,0:T(8,128)S(1)} %get-tuple-element.15.rows, s32[8,128]{1,0:T(8,128)S(1)} %get-tuple-element.16.order, s32[512]{0:T(512)S(1)} %copy-done.2, ...), custom_call_target="tpu_custom_call" | custom-call | tf_op jit(solution)/shard_map/pallas_call | solution.py:229
  33.9 4.4 %collective-permute-start.6 = (bf16[4,512,128]{2,1,0:T(8,128)(2,1)S(1)}, bf16[4,512,128]{2,1,0:T(8,128)(2,1)S(1)}, u32[]{:S(2)}, u32[]{:S(2)}) collective-permute-start(bf16[4,512,128]{2,1,0:T(8,128)(2,1)S(1)} %get-tuple-element.20), channel_id=1, source_target_pairs={{0,1},{1,2},{2,3},{3,0},{4,5},{5,6},{6,7},{7,4},{8,9},{9,10},{10,1... | collective-permute-start | bytes 1572872 | tf_op jit(solution)/shard_map/ppermute | solution.py:418
  38.3 1.8 %collective-permute-start.7 = (bf16[4,512,128]{2,1,0:T(8,128)(2,1)S(1)}, bf16[4,512,128]{2,1,0:T(8,128)(2,1)S(1)}, u32[]{:S(2)}, u32[]{:S(2)}) collective-permute-start(bf16[4,512,128]{2,1,0:T(8,128)(2,1)S(1)} %get-tuple-element.21), channel_id=1, source_target_pairs={{0,3},{1,0},{2,1},{3,2},{4,7},{5,4},{6,5},{7,6},{8,11},{9,8},{10,9... | collective-permute-start | bytes 1572872 | tf_op jit(solution)/shard_map/ppermute | solution.py:418
  40.1 1.6 %shard_map.81.refs_0_ = bf16[4,512,128]{2,1,0:T(8,128)(2,1)S(1)} custom-call(s32[8,128]{1,0:T(8,128)S(1)} %get-tuple-element.15.rows, s32[8,128]{1,0:T(8,128)S(1)} %get-tuple-element.16.order, s32[512]{0:T(512)S(1)} %copy-done.2, bf16[16384,128]{1,0:T(8,128)(2,1)S(1)} %get-tuple-element.18.weights, bf16[16384,128]{1,0:T(8,128)(2,1)S(1)} %get-tuple-element.17.values), custom_call_target="tpu_custom_call" | custom-call | bytes 16777216 | tf_op jit(solution)/shard_map/pallas_call | solution.py:237
  41.8 2.8 %collective-permute-done.5.refs_1_ = bf16[4,512,128]{2,1,0:T(8,128)(2,1)S(1)} collective-permute-done((bf16[4,512,128]{2,1,0:T(8,128)(2,1)S(1)}, bf16[4,512,128]{2,1,0:T(8,128)(2,1)S(1)}, u32[]{:S(2)}, u32[]{:S(2)}) %collective-permute-start.5) | collective-permute-done | bytes 524320 | tf_op jit(solution)/shard_map/ppermute | solution.py:418
  44.6 5.5 %collective-permute-done.6.refs_2_ = bf16[4,512,128]{2,1,0:T(8,128)(2,1)S(1)} collective-permute-done((bf16[4,512,128]{2,1,0:T(8,128)(2,1)S(1)}, bf16[4,512,128]{2,1,0:T(8,128)(2,1)S(1)}, u32[]{:S(2)}, u32[]{:S(2)}) %collective-permute-start.6) | collective-permute-done | bytes 524320 | tf_op jit(solution)/shard_map/ppermute | solution.py:418
  51.4 1.4 %collective-permute-start.8 = (bf16[512,128]{1,0:T(8,128)(2,1)S(1)}, bf16[512,128]{1,0:T(8,128)(2,1)S(1)}, u32[]{:S(2)}, u32[]{:S(2)}) collective-permute-start(bf16[512,128]{1,0:T(8,128)(2,1)S(1)} %get-tuple-element.23), channel_id=1, source_target_pairs={{0,8},{1,9},{2,10},{3,11},{4,12},{5,13},{6,14},{7,15},{8,0},{9,1},... | collective-permute-start | bytes 393224 | tf_op jit(solution)/shard_map/ppermute | solution.py:418
  52.8 2.3 %collective-permute-start.9 = (bf16[512,128]{1,0:T(8,128)(2,1)S(1)}, bf16[512,128]{1,0:T(8,128)(2,1)S(1)}, u32[]{:S(2)}, u32[]{:S(2)}) collective-permute-start(bf16[512,128]{1,0:T(8,128)(2,1)S(1)} %get-tuple-element.24), channel_id=1, source_target_pairs={{0,4},{1,5},{2,6},{3,7},{4,8},{5,9},{6,10},{7,11},{8,12},{9,13},{1... | collective-permute-start | bytes 393224 | tf_op jit(solution)/shard_map/ppermute | solution.py:418
  55.0 1.3 %collective-permute-start.10 = (bf16[512,128]{1,0:T(8,128)(2,1)S(1)}, bf16[512,128]{1,0:T(8,128)(2,1)S(1)}, u32[]{:S(2)}, u32[]{:S(2)}) collective-permute-start(bf16[512,128]{1,0:T(8,128)(2,1)S(1)} %get-tuple-element.25), channel_id=1, source_target_pairs={{0,12},{1,13},{2,14},{3,15},{4,0},{5,1},{6,2},{7,3},{8,4},{9,5},{1... | collective-permute-start | bytes 393224 | tf_op jit(solution)/shard_map/ppermute | solution.py:418
  56.3 1.6 %collective-permute-done.8.refs_1_ = bf16[512,128]{1,0:T(8,128)(2,1)S(1)} collective-permute-done((bf16[512,128]{1,0:T(8,128)(2,1)S(1)}, bf16[512,128]{1,0:T(8,128)(2,1)S(1)}, u32[]{:S(2)}, u32[]{:S(2)}) %collective-permute-start.8) | collective-permute-done | bytes 131104 | tf_op jit(solution)/shard_map/ppermute | solution.py:418
  57.9 1.4 %collective-permute-done.9.refs_2_ = bf16[512,128]{1,0:T(8,128)(2,1)S(1)} collective-permute-done((bf16[512,128]{1,0:T(8,128)(2,1)S(1)}, bf16[512,128]{1,0:T(8,128)(2,1)S(1)}, u32[]{:S(2)}, u32[]{:S(2)}) %collective-permute-start.9) | collective-permute-done | bytes 131104 | tf_op jit(solution)/shard_map/ppermute | solution.py:418
  60.7 15.4 %all_to_all.5 = f32[16,32,128]{2,1,0:T(8,128)S(1)} all-to-all(f32[16,32,128]{2,1,0:T(8,128)S(1)} %get-tuple-element.26), channel_id=1, replica_groups=mesh['z'=4,'core'=2,'y'=4,'x'=4] {'y','x'}, dimensions={0} | all-to-all | bytes 524288 | tf_op jit(solution)/shard_map/all_to_all | solution.py:433
  77.6 2.4 %collective-permute-start.13 = (f32[32,128]{1,0:T(8,128)S(1)}, f32[32,128]{1,0:T(8,128)S(1)}, u32[]{:S(2)}, u32[]{:S(2)}) collective-permute-start(f32[32,128]{1,0:T(8,128)S(1)} %add.3.g0), channel_id=1, source_target_pairs={{0,64},{32,96},{64,0},{96,32},{1,65},{33,97},{65,1},{97,33},{2,66}... | collective-permute-start | bytes 49160 | tf_op jit(solution)/shard_map/ppermute | solution.py:378
  80.0 1.3 %collective-permute-start.12 = (f32[32,128]{1,0:T(8,128)S(1)}, f32[32,128]{1,0:T(8,128)S(1)}, u32[]{:S(2)}, u32[]{:S(2)}) collective-permute-start(f32[32,128]{1,0:T(8,128)S(1)} %add.3.g0), channel_id=1, source_target_pairs={{0,32},{32,64},{64,96},{96,0},{1,33},{33,65},{65,97},{97,1},{2,34}... | collective-permute-start | bytes 49160 | tf_op jit(solution)/shard_map/ppermute | solution.py:378
  81.4 1.5 %collective-permute-done.13.g2 = f32[32,128]{1,0:T(8,128)S(1)} collective-permute-done((f32[32,128]{1,0:T(8,128)S(1)}, f32[32,128]{1,0:T(8,128)S(1)}, u32[]{:S(2)}, u32[]{:S(2)}) %collective-permute-start.13) | collective-permute-done | bytes 16416 | tf_op jit(solution)/shard_map/ppermute | solution.py:378
  82.9 2.1 %collective-permute-done.12.g1 = f32[32,128]{1,0:T(8,128)S(1)} collective-permute-done((f32[32,128]{1,0:T(8,128)S(1)}, f32[32,128]{1,0:T(8,128)S(1)}, u32[]{:S(2)}, u32[]{:S(2)}) %collective-permute-start.12) | collective-permute-done | bytes 16416 | tf_op jit(solution)/shard_map/ppermute | solution.py:378
  85.0 2.8 %shard_map.84 = (f32[64,1024]{1,0:T(8,128)}, f32[64,64]{1,0:T(8,128)}) custom-call(f32[32,128]{1,0:T(8,128)S(1)} %add.3.g0, f32[32,128]{1,0:T(8,128)S(1)} %collective-permute-done.12.g1, f32[32,128]{1,0:T(8,128)S(1)} %collective-permute-done.13.g2, f32[32,128]{1,0:T(8,128)S(1)} %collective-permute-done.14.g3, f32[64,1024]{1,0:T(8,128)S(1)} %get-tuple-element.27.image), custom_call_target="tpu_custom_call" | custom-call | tf_op jit(solution)/shard_map/pallas_call | solution.py:364
  (28 shorter events, 7.7 us)
Async XLA Ops:
  0.6 29.3 %copy-start.4 = (s32[128]{0:T(128)S(1)}, s32[128]{0:T(128)}, u32[]{:S(2)}) copy-start(s32[128]{0:T(128)} %constant.4.clone.table) | copy-start | bytes 1540
  0.6 9.9 %collective-permute-start = (bf16[64,1024]{1,0:T(8,128)(2,1)}, bf16[64,1024]{1,0:T(8,128)(2,1)S(1)}, u32[]{:S(2)}, u32[]{:S(2)}) collective-permute-start(bf16[64,1024]{1,0:T(8,128)(2,1)} %refs_4_.1), channel_id=1, source_target_pairs={{6,0},{2,16},{5,32},{7,48},{1,96},{3,112},{4,64},{0,80},{11,1},{8,... | collective-permute-start | bytes 393224 | tf_op jit(solution)/shard_map/ppermute | solution.py:403
  4.8 2.2 %copy-start = (bf16[512,4096]{1,0:T(8,128)(2,1)S(1)}, bf16[512,4096]{1,0:T(8,128)(2,1)}, u32[]{:S(2)}) copy-start(bf16[512,4096]{1,0:T(8,128)(2,1)} %values.1) | copy-start | bytes 12582916
  7.0 0.7 copy-start.3
  7.6 22.3 %copy-start.2 = (s32[512]{0:T(512)S(1)}, s32[512]{0:T(512)}, u32[]{:S(2)}) copy-start(s32[512]{0:T(512)} %tiles.3) | copy-start | bytes 6148
  10.8 13.4 %collective-permute-start.3 = (bf16[512,128]{1,0:T(8,128)(2,1)S(1)}, bf16[512,128]{1,0:T(8,128)(2,1)S(1)}, u32[]{:S(2)}, u32[]{:S(2)}) collective-permute-start(bf16[512,128]{1,0:T(8,128)(2,1)S(1)} %shard_map.78), channel_id=1, source_target_pairs={{0,96},{32,0},{64,32},{96,64},{1,97},{33,1},{65,33},{97,65},{2,98}... | collective-permute-start | bytes 393224 | tf_op jit(solution)/shard_map/ppermute | solution.py:378
  20.2 6.6 %collective-permute-start.2 = (bf16[512,128]{1,0:T(8,128)(2,1)S(1)}, bf16[512,128]{1,0:T(8,128)(2,1)S(1)}, u32[]{:S(2)}, u32[]{:S(2)}) collective-permute-start(bf16[512,128]{1,0:T(8,128)(2,1)S(1)} %shard_map.78), channel_id=1, source_target_pairs={{0,64},{32,96},{64,0},{96,32},{1,65},{33,97},{65,1},{97,33},{2,66}... | collective-permute-start | bytes 393224 | tf_op jit(solution)/shard_map/ppermute | solution.py:378
  20.2 7.6 %collective-permute-start.1 = (bf16[512,128]{1,0:T(8,128)(2,1)S(1)}, bf16[512,128]{1,0:T(8,128)(2,1)S(1)}, u32[]{:S(2)}, u32[]{:S(2)}) collective-permute-start(bf16[512,128]{1,0:T(8,128)(2,1)S(1)} %shard_map.78), channel_id=1, source_target_pairs={{0,32},{32,64},{64,96},{96,0},{1,33},{33,65},{65,97},{97,1},{2,34}... | collective-permute-start | bytes 393224 | tf_op jit(solution)/shard_map/ppermute | solution.py:378
  27.9 2.0 %collective-permute-start.4 = (bf16[4,512,128]{2,1,0:T(8,128)(2,1)S(1)}, bf16[4,512,128]{2,1,0:T(8,128)(2,1)S(1)}, u32[]{:S(2)}, u32[]{:S(2)}) collective-permute-start(bf16[4,512,128]{2,1,0:T(8,128)(2,1)S(1)} %pad_maximum_fusion.own), channel_id=1, source_target_pairs={{0,16},{16,0},{1,17},{17,1},{2,18},{18,2},{3,19},{19,3},{4,20},{20... | collective-permute-start | bytes 1572872 | tf_op jit(solution)/shard_map/ppermute | solution.py:378
  33.8 10.9 %collective-permute-start.5 = (bf16[4,512,128]{2,1,0:T(8,128)(2,1)S(1)}, bf16[4,512,128]{2,1,0:T(8,128)(2,1)S(1)}, u32[]{:S(2)}, u32[]{:S(2)}) collective-permute-start(bf16[4,512,128]{2,1,0:T(8,128)(2,1)S(1)} %get-tuple-element.19), channel_id=1, source_target_pairs={{0,2},{1,3},{2,0},{3,1},{4,6},{5,7},{6,4},{7,5},{8,10},{9,11},{10,... | collective-permute-start | bytes 1572872 | tf_op jit(solution)/shard_map/ppermute | solution.py:418
  33.9 16.3 %collective-permute-start.6 = (bf16[4,512,128]{2,1,0:T(8,128)(2,1)S(1)}, bf16[4,512,128]{2,1,0:T(8,128)(2,1)S(1)}, u32[]{:S(2)}, u32[]{:S(2)}) collective-permute-start(bf16[4,512,128]{2,1,0:T(8,128)(2,1)S(1)} %get-tuple-element.20), channel_id=1, source_target_pairs={{0,1},{1,2},{2,3},{3,0},{4,5},{5,6},{6,7},{7,4},{8,9},{9,10},{10,1... | collective-permute-start | bytes 1572872 | tf_op jit(solution)/shard_map/ppermute | solution.py:418
  38.3 12.8 %collective-permute-start.7 = (bf16[4,512,128]{2,1,0:T(8,128)(2,1)S(1)}, bf16[4,512,128]{2,1,0:T(8,128)(2,1)S(1)}, u32[]{:S(2)}, u32[]{:S(2)}) collective-permute-start(bf16[4,512,128]{2,1,0:T(8,128)(2,1)S(1)} %get-tuple-element.21), channel_id=1, source_target_pairs={{0,3},{1,0},{2,1},{3,2},{4,7},{5,4},{6,5},{7,6},{8,11},{9,8},{10,9... | collective-permute-start | bytes 1572872 | tf_op jit(solution)/shard_map/ppermute | solution.py:418
  40.1 19.8 %copy-start.1 = (bf16[64,1024]{1,0:T(8,128)(2,1)S(1)}, bf16[64,1024]{1,0:T(8,128)(2,1)}, u32[]{:S(2)}) copy-start(bf16[64,1024]{1,0:T(8,128)(2,1)} %refs_4_.1) | copy-start | bytes 393220
  51.4 6.6 %collective-permute-start.8 = (bf16[512,128]{1,0:T(8,128)(2,1)S(1)}, bf16[512,128]{1,0:T(8,128)(2,1)S(1)}, u32[]{:S(2)}, u32[]{:S(2)}) collective-permute-start(bf16[512,128]{1,0:T(8,128)(2,1)S(1)} %get-tuple-element.23), channel_id=1, source_target_pairs={{0,8},{1,9},{2,10},{3,11},{4,12},{5,13},{6,14},{7,15},{8,0},{9,1},... | collective-permute-start | bytes 393224 | tf_op jit(solution)/shard_map/ppermute | solution.py:418
  52.8 6.6 %collective-permute-start.9 = (bf16[512,128]{1,0:T(8,128)(2,1)S(1)}, bf16[512,128]{1,0:T(8,128)(2,1)S(1)}, u32[]{:S(2)}, u32[]{:S(2)}) collective-permute-start(bf16[512,128]{1,0:T(8,128)(2,1)S(1)} %get-tuple-element.24), channel_id=1, source_target_pairs={{0,4},{1,5},{2,6},{3,7},{4,8},{5,9},{6,10},{7,11},{8,12},{9,13},{1... | collective-permute-start | bytes 393224 | tf_op jit(solution)/shard_map/ppermute | solution.py:418
  55.0 5.0 %collective-permute-start.10 = (bf16[512,128]{1,0:T(8,128)(2,1)S(1)}, bf16[512,128]{1,0:T(8,128)(2,1)S(1)}, u32[]{:S(2)}, u32[]{:S(2)}) collective-permute-start(bf16[512,128]{1,0:T(8,128)(2,1)S(1)} %get-tuple-element.25), channel_id=1, source_target_pairs={{0,12},{1,13},{2,14},{3,15},{4,0},{5,1},{6,2},{7,3},{8,4},{9,5},{1... | collective-permute-start | bytes 393224 | tf_op jit(solution)/shard_map/ppermute | solution.py:418
  76.2 1.3 %collective-permute-start.11 = (f32[32,128]{1,0:T(8,128)S(1)}, f32[32,128]{1,0:T(8,128)S(1)}, u32[]{:S(2)}, u32[]{:S(2)}) collective-permute-start(f32[32,128]{1,0:T(8,128)S(1)} %reduce_sum.9), channel_id=1, source_target_pairs={{0,16},{16,0},{1,17},{17,1},{2,18},{18,2},{3,19},{19,3},{4,20},{20... | collective-permute-start | bytes 49160 | tf_op jit(solution)/shard_map/ppermute | solution.py:378
  77.4 4.0 %collective-permute-start.14 = (f32[32,128]{1,0:T(8,128)S(1)}, f32[32,128]{1,0:T(8,128)S(1)}, u32[]{:S(2)}, u32[]{:S(2)}) collective-permute-start(f32[32,128]{1,0:T(8,128)S(1)} %add.3.g0), channel_id=1, source_target_pairs={{0,96},{32,0},{64,32},{96,64},{1,97},{33,1},{65,33},{97,65},{2,98}... | collective-permute-start | bytes 49160 | tf_op jit(solution)/shard_map/ppermute | solution.py:378
  77.6 5.2 %collective-permute-start.13 = (f32[32,128]{1,0:T(8,128)S(1)}, f32[32,128]{1,0:T(8,128)S(1)}, u32[]{:S(2)}, u32[]{:S(2)}) collective-permute-start(f32[32,128]{1,0:T(8,128)S(1)} %add.3.g0), channel_id=1, source_target_pairs={{0,64},{32,96},{64,0},{96,32},{1,65},{33,97},{65,1},{97,33},{2,66}... | collective-permute-start | bytes 49160 | tf_op jit(solution)/shard_map/ppermute | solution.py:378
  80.0 4.9 %collective-permute-start.12 = (f32[32,128]{1,0:T(8,128)S(1)}, f32[32,128]{1,0:T(8,128)S(1)}, u32[]{:S(2)}, u32[]{:S(2)}) collective-permute-start(f32[32,128]{1,0:T(8,128)S(1)} %add.3.g0), channel_id=1, source_target_pairs={{0,32},{32,64},{64,96},{96,0},{1,33},{33,65},{65,97},{97,1},{2,34}... | collective-permute-start | bytes 49160 | tf_op jit(solution)/shard_map/ppermute | solution.py:378

commit v7 on v6

--- a/solution.py
+++ b/solution.py
@@ -428,7 +428,7 @@
     own, other = gather_band(panel, rows)
     partial = multiply(rows, block_columns, order, own, other, values)
     sums = stage_sums([partial[0]] + [across(partial[shift], shift, True) for shift in ORDER[:3]])
-    arrived = [sums[0]] + [across(sums[shift], shift, False) for shift in ORDER[:3]]
+    arrived = [sums[0]] + [across(sums[shift], shift, False) for shift in (1, 2, 3)]
     image, gram = finish_image(arrived, panel)
     gram = jnp.sum(lax.all_to_all(gram, ("y", "x"), 0, 0, tiled=True), axis=0)
     gram = gram + shifted(gram, "core", 1, 2)

time: 87.7 us -> 87.9 us (level)
  starting transfers between devices: 29.3 us -> 24.2 us
  Pallas kernels: 12.9 us -> 16.5 us
  waiting for transfers between devices: 25.8 us -> 28 us
  blocking collectives: 15.4 us -> 14.4 us
    ppermute x6, starting transfers between devices: 11.3 us -> 7.47 us  [across(): return lax.ppermute(value, AXES, pairs)]
    pallas_call x1, Pallas kernels: 3.87 us -> 5.99 us  [multiply(): pl.pallas_call(first_kernel, in_specs=[smem] * 4 + [vmem] * 3, out_specs=...]
    pallas_call x1, Pallas kernels: 1.65 us -> 3.09 us  [multiply(): pl.pallas_call(second_kernel, in_specs=[smem] * 3 + [vmem] * 2, out_specs...]
    ppermute x8, starting transfers between devices: 14.5 us -> 13.2 us  [shifted(): lax.ppermute(value, axis, [(i, (i + shift) % size) for i in range(size)])]
    ppermute x6, waiting for transfers between devices: 13 us -> 14.1 us  [across(): return lax.ppermute(value, AXES, pairs)]
    ppermute x8, waiting for transfers between devices: 12.8 us -> 13.9 us  [shifted(): lax.ppermute(value, axis, [(i, (i + shift) % size) for i in range(size)])]
    all_to_all x1, blocking collectives: 15.4 us -> 14.4 us  [per_device(): gram = jnp.sum(lax.all_to_all(gram, ('y', 'x'), 0, 0, tiled=True), axis=0)]
  transfers between devices with their start and end apart: 15 -> 15, of which waited for: 13 -> 13; matrix products, arithmetic and copies ran while one was open for 0% -> 0% of each run, Pallas kernels for 6% -> 7%
where the time goes in v7:
time: 87.9 us; the launch traced here: 87.4 us
  waiting for transfers between devices  28 us (32%)
  starting transfers between devices  24.2 us (28%)
  Pallas kernels  16.5 us (19%)
  blocking collectives  14.4 us (16%)
  local copies, waits for them, and re-layouts  2.87 us (3%)
  between operations  1.41 us (2%)
    all_to_all x1, blocking collectives, per_device(): gram = jnp.sum(lax.all_to_all(gram, ('y', 'x'), 0, 0, tiled=True), axis=0)  14.4 us
    ppermute x6, waiting for transfers between devices, across(): return lax.ppermute(value, AXES, pairs)  14.1 us
    ppermute x8, waiting for transfers between devices, shifted(): lax.ppermute(value, axis, [(i, (i + shift) % size) for i in range(size)])  13.9 us
    ppermute x8, starting transfers between devices, shifted(): lax.ppermute(value, axis, [(i, (i + shift) % size) for i in range(size)])  13.2 us
    ppermute x6, starting transfers between devices, across(): return lax.ppermute(value, AXES, pairs)  7.47 us
    pallas_call x1, Pallas kernels, multiply(): pl.pallas_call(first_kernel, in_specs=[smem] * 4 + [vmem] * 3, out_specs=...  5.99 us
    ppermute x1, starting transfers between devices, gather_band(): piece = transpose_panel(lax.ppermute(panel, AXES, placement()[0]), rows)  3.48 us
    pallas_call x1, Pallas kernels, multiply(): pl.pallas_call(second_kernel, in_specs=[smem] * 3 + [vmem] * 2, out_specs...  3.09 us
  transfers between devices with their start and end apart: 15, of which 13 were waited for; matrix products, arithmetic and copies ran while one was open for 0% of the time, Pallas kernels for 7%

profile of v7, /device:TPU:0, one launch (start us, length us, event | category | flops | bytes accessed | tf_op | source)
XLA Modules:
  0.0 87.4 jit_solution(10657816918823617063)
XLA Ops:
  0.6 3.5 %collective-permute-start = (bf16[64,1024]{1,0:T(8,128)(2,1)}, bf16[64,1024]{1,0:T(8,128)(2,1)S(1)}, u32[]{:S(2)}, u32[]{:S(2)}) collective-permute-start(bf16[64,1024]{1,0:T(8,128)(2,1)} %refs_4_.1), channel_id=1, source_target_pairs={{6,0},{2,16},{5,32},{7,48},{1,96},{3,112},{4,64},{0,80},{11,1},{8,... | collective-permute-start | bytes 393224 | tf_op jit(solution)/shard_map/ppermute | solution.py:403
  4.8 2.2 %copy-done = bf16[512,4096]{1,0:T(8,128)(2,1)S(1)} copy-done((bf16[512,4096]{1,0:T(8,128)(2,1)S(1)}, bf16[512,4096]{1,0:T(8,128)(2,1)}, u32[]{:S(2)}) %copy-start) | copy-done | bytes 4194328
  7.6 2.9 %shard_map.77 = (bf16[16384,128]{1,0:T(8,128)(2,1)S(1)}, s32[8,128]{1,0:T(8,128)S(1)}, s32[8,128]{1,0:T(8,128)S(1)}) custom-call(s32[256]{0:T(256)S(1)} %copy-done.3, s32[1]{0:T(128)S(6)} %copy.8.counts, bf16[512,4096]{1,0:T(8,128)(2,1)S(1)} %copy-done), custom_call_target="tpu_custom_call" | custom-call | bytes 25165824 | tf_op jit(solution)/shard_map/pallas_call | solution.py:83
  10.8 9.4 %collective-permute-start.3 = (bf16[512,128]{1,0:T(8,128)(2,1)S(1)}, bf16[512,128]{1,0:T(8,128)(2,1)S(1)}, u32[]{:S(2)}, u32[]{:S(2)}) collective-permute-start(bf16[512,128]{1,0:T(8,128)(2,1)S(1)} %shard_map.78), channel_id=1, source_target_pairs={{0,96},{32,0},{64,32},{96,64},{1,97},{33,1},{65,33},{97,65},{2,98}... | collective-permute-start | bytes 393224 | tf_op jit(solution)/shard_map/ppermute | solution.py:378
  21.2 3.0 %collective-permute-done.3 = bf16[512,128]{1,0:T(8,128)(2,1)S(1)} collective-permute-done((bf16[512,128]{1,0:T(8,128)(2,1)S(1)}, bf16[512,128]{1,0:T(8,128)(2,1)S(1)}, u32[]{:S(2)}, u32[]{:S(2)}) %collective-permute-start.3) | collective-permute-done | bytes 131104 | tf_op jit(solution)/shard_map/ppermute | solution.py:378
  24.2 2.7 %collective-permute-done.2 = bf16[512,128]{1,0:T(8,128)(2,1)S(1)} collective-permute-done((bf16[512,128]{1,0:T(8,128)(2,1)S(1)}, bf16[512,128]{1,0:T(8,128)(2,1)S(1)}, u32[]{:S(2)}, u32[]{:S(2)}) %collective-permute-start.2) | collective-permute-done | bytes 131104 | tf_op jit(solution)/shard_map/ppermute | solution.py:378
  28.5 1.4 %collective-permute-done.4.other = bf16[4,512,128]{2,1,0:T(8,128)(2,1)S(1)} collective-permute-done((bf16[4,512,128]{2,1,0:T(8,128)(2,1)S(1)}, bf16[4,512,128]{2,1,0:T(8,128)(2,1)S(1)}, u32[]{:S(2)}, u32[]{:S(2)}) %collective-permute-start.4) | collective-permute-done | bytes 524320 | tf_op jit(solution)/shard_map/ppermute | solution.py:378
  29.9 6.0 %shard_map.80 = (bf16[16384,128]{1,0:T(8,128)(2,1)S(1)}, bf16[4,512,128]{2,1,0:T(8,128)(2,1)S(1)}, bf16[4,512,128]{2,1,0:T(8,128)(2,1)S(1)}, bf16[4,512,128]{2,1,0:T(8,128)(2,1)S(1)}) custom-call(s32[8,128]{1,0:T(8,128)S(1)} %get-tuple-element.15.rows, s32[8,128]{1,0:T(8,128)S(1)} %get-tuple-element.16.order, s32[512]{0:T(512)S(1)} %copy-done.2, ...), custom_call_target="tpu_custom_call" | custom-call | tf_op jit(solution)/shard_map/pallas_call | solution.py:229
  36.0 1.6 %collective-permute-start.6 = (bf16[4,512,128]{2,1,0:T(8,128)(2,1)S(1)}, bf16[4,512,128]{2,1,0:T(8,128)(2,1)S(1)}, u32[]{:S(2)}, u32[]{:S(2)}) collective-permute-start(bf16[4,512,128]{2,1,0:T(8,128)(2,1)S(1)} %get-tuple-element.20), channel_id=1, source_target_pairs={{0,1},{1,2},{2,3},{3,0},{4,5},{5,6},{6,7},{7,4},{8,9},{9,10},{10,1... | collective-permute-start | bytes 1572872 | tf_op jit(solution)/shard_map/ppermute | solution.py:418
  37.6 1.7 %collective-permute-start.7 = (bf16[4,512,128]{2,1,0:T(8,128)(2,1)S(1)}, bf16[4,512,128]{2,1,0:T(8,128)(2,1)S(1)}, u32[]{:S(2)}, u32[]{:S(2)}) collective-permute-start(bf16[4,512,128]{2,1,0:T(8,128)(2,1)S(1)} %get-tuple-element.21), channel_id=1, source_target_pairs={{0,3},{1,0},{2,1},{3,2},{4,7},{5,4},{6,5},{7,6},{8,11},{9,8},{10,9... | collective-permute-start | bytes 1572872 | tf_op jit(solution)/shard_map/ppermute | solution.py:418
  39.3 3.1 %shard_map.81.refs_0_ = bf16[4,512,128]{2,1,0:T(8,128)(2,1)S(1)} custom-call(s32[8,128]{1,0:T(8,128)S(1)} %get-tuple-element.15.rows, s32[8,128]{1,0:T(8,128)S(1)} %get-tuple-element.16.order, s32[512]{0:T(512)S(1)} %copy-done.2, bf16[16384,128]{1,0:T(8,128)(2,1)S(1)} %get-tuple-element.18.weights, bf16[16384,128]{1,0:T(8,128)(2,1)S(1)} %get-tuple-element.17.values), custom_call_target="tpu_custom_call" | custom-call | bytes 16777216 | tf_op jit(solution)/shard_map/pallas_call | solution.py:237
  42.4 4.4 %collective-permute-done.5.refs_1_ = bf16[4,512,128]{2,1,0:T(8,128)(2,1)S(1)} collective-permute-done((bf16[4,512,128]{2,1,0:T(8,128)(2,1)S(1)}, bf16[4,512,128]{2,1,0:T(8,128)(2,1)S(1)}, u32[]{:S(2)}, u32[]{:S(2)}) %collective-permute-start.5) | collective-permute-done | bytes 524320 | tf_op jit(solution)/shard_map/ppermute | solution.py:418
  46.8 5.3 %collective-permute-done.6.refs_2_ = bf16[4,512,128]{2,1,0:T(8,128)(2,1)S(1)} collective-permute-done((bf16[4,512,128]{2,1,0:T(8,128)(2,1)S(1)}, bf16[4,512,128]{2,1,0:T(8,128)(2,1)S(1)}, u32[]{:S(2)}, u32[]{:S(2)}) %collective-permute-start.6) | collective-permute-done | bytes 524320 | tf_op jit(solution)/shard_map/ppermute | solution.py:418
  52.3 1.3 %collective-permute-start.8 = (bf16[512,128]{1,0:T(8,128)(2,1)S(1)}, bf16[512,128]{1,0:T(8,128)(2,1)S(1)}, u32[]{:S(2)}, u32[]{:S(2)}) collective-permute-start(bf16[512,128]{1,0:T(8,128)(2,1)S(1)} %get-tuple-element.23), channel_id=1, source_target_pairs={{0,4},{1,5},{2,6},{3,7},{4,8},{5,9},{6,10},{7,11},{8,12},{9,13},{1... | collective-permute-start | bytes 393224 | tf_op jit(solution)/shard_map/ppermute | solution.py:418
  53.6 2.0 %collective-permute-start.9 = (bf16[512,128]{1,0:T(8,128)(2,1)S(1)}, bf16[512,128]{1,0:T(8,128)(2,1)S(1)}, u32[]{:S(2)}, u32[]{:S(2)}) collective-permute-start(bf16[512,128]{1,0:T(8,128)(2,1)S(1)} %get-tuple-element.24), channel_id=1, source_target_pairs={{0,8},{1,9},{2,10},{3,11},{4,12},{5,13},{6,14},{7,15},{8,0},{9,1},... | collective-permute-start | bytes 393224 | tf_op jit(solution)/shard_map/ppermute | solution.py:418
  56.4 2.2 %collective-permute-done.8.refs_1_ = bf16[512,128]{1,0:T(8,128)(2,1)S(1)} collective-permute-done((bf16[512,128]{1,0:T(8,128)(2,1)S(1)}, bf16[512,128]{1,0:T(8,128)(2,1)S(1)}, u32[]{:S(2)}, u32[]{:S(2)}) %collective-permute-start.8) | collective-permute-done | bytes 131104 | tf_op jit(solution)/shard_map/ppermute | solution.py:418
  58.6 1.5 %collective-permute-done.9.refs_2_ = bf16[512,128]{1,0:T(8,128)(2,1)S(1)} collective-permute-done((bf16[512,128]{1,0:T(8,128)(2,1)S(1)}, bf16[512,128]{1,0:T(8,128)(2,1)S(1)}, u32[]{:S(2)}, u32[]{:S(2)}) %collective-permute-start.9) | collective-permute-done | bytes 131104 | tf_op jit(solution)/shard_map/ppermute | solution.py:418
  61.6 14.4 %all_to_all.5 = f32[16,32,128]{2,1,0:T(8,128)S(1)} all-to-all(f32[16,32,128]{2,1,0:T(8,128)S(1)} %get-tuple-element.26), channel_id=1, replica_groups=mesh['z'=4,'core'=2,'y'=4,'x'=4] {'y','x'}, dimensions={0} | all-to-all | bytes 524288 | tf_op jit(solution)/shard_map/all_to_all | solution.py:433
  76.1 1.2 %collective-permute-done.11 = f32[32,128]{1,0:T(8,128)S(1)} collective-permute-done((f32[32,128]{1,0:T(8,128)S(1)}, f32[32,128]{1,0:T(8,128)S(1)}, u32[]{:S(2)}, u32[]{:S(2)}) %collective-permute-start.11) | collective-permute-done | bytes 16416 | tf_op jit(solution)/shard_map/ppermute | solution.py:378
  77.7 2.0 %collective-permute-start.13 = (f32[32,128]{1,0:T(8,128)S(1)}, f32[32,128]{1,0:T(8,128)S(1)}, u32[]{:S(2)}, u32[]{:S(2)}) collective-permute-start(f32[32,128]{1,0:T(8,128)S(1)} %add.3.g0), channel_id=1, source_target_pairs={{0,64},{32,96},{64,0},{96,32},{1,65},{33,97},{65,1},{97,33},{2,66}... | collective-permute-start | bytes 49160 | tf_op jit(solution)/shard_map/ppermute | solution.py:378
  79.9 1.1 %collective-permute-done.14.g3 = f32[32,128]{1,0:T(8,128)S(1)} collective-permute-done((f32[32,128]{1,0:T(8,128)S(1)}, f32[32,128]{1,0:T(8,128)S(1)}, u32[]{:S(2)}, u32[]{:S(2)}) %collective-permute-start.14) | collective-permute-done | bytes 16416 | tf_op jit(solution)/shard_map/ppermute | solution.py:378
  81.0 2.0 %collective-permute-done.13.g2 = f32[32,128]{1,0:T(8,128)S(1)} collective-permute-done((f32[32,128]{1,0:T(8,128)S(1)}, f32[32,128]{1,0:T(8,128)S(1)}, u32[]{:S(2)}, u32[]{:S(2)}) %collective-permute-start.13) | collective-permute-done | bytes 16416 | tf_op jit(solution)/shard_map/ppermute | solution.py:378
  82.9 1.7 %collective-permute-done.12.g1 = f32[32,128]{1,0:T(8,128)S(1)} collective-permute-done((f32[32,128]{1,0:T(8,128)S(1)}, f32[32,128]{1,0:T(8,128)S(1)}, u32[]{:S(2)}, u32[]{:S(2)}) %collective-permute-start.12) | collective-permute-done | bytes 16416 | tf_op jit(solution)/shard_map/ppermute | solution.py:378
  84.6 2.8 %shard_map.84 = (f32[64,1024]{1,0:T(8,128)}, f32[64,64]{1,0:T(8,128)}) custom-call(f32[32,128]{1,0:T(8,128)S(1)} %add.3.g0, f32[32,128]{1,0:T(8,128)S(1)} %collective-permute-done.12.g1, f32[32,128]{1,0:T(8,128)S(1)} %collective-permute-done.13.g2, f32[32,128]{1,0:T(8,128)S(1)} %collective-permute-done.14.g3, f32[64,1024]{1,0:T(8,128)S(1)} %get-tuple-element.27.image), custom_call_target="tpu_custom_call" | custom-call | tf_op jit(solution)/shard_map/pallas_call | solution.py:364
  (28 shorter events, 6.9 us)
Async XLA Ops:
  0.6 29.3 %copy-start.4 = (s32[128]{0:T(128)S(1)}, s32[128]{0:T(128)}, u32[]{:S(2)}) copy-start(s32[128]{0:T(128)} %constant.4.clone.table) | copy-start | bytes 1540
  0.6 9.9 %collective-permute-start = (bf16[64,1024]{1,0:T(8,128)(2,1)}, bf16[64,1024]{1,0:T(8,128)(2,1)S(1)}, u32[]{:S(2)}, u32[]{:S(2)}) collective-permute-start(bf16[64,1024]{1,0:T(8,128)(2,1)} %refs_4_.1), channel_id=1, source_target_pairs={{6,0},{2,16},{5,32},{7,48},{1,96},{3,112},{4,64},{0,80},{11,1},{8,... | collective-permute-start | bytes 393224 | tf_op jit(solution)/shard_map/ppermute | solution.py:403
  4.8 2.2 %copy-start = (bf16[512,4096]{1,0:T(8,128)(2,1)S(1)}, bf16[512,4096]{1,0:T(8,128)(2,1)}, u32[]{:S(2)}) copy-start(bf16[512,4096]{1,0:T(8,128)(2,1)} %values.1) | copy-start | bytes 12582916
  7.0 0.7 copy-start.3
  7.6 22.3 %copy-start.2 = (s32[512]{0:T(512)S(1)}, s32[512]{0:T(512)}, u32[]{:S(2)}) copy-start(s32[512]{0:T(512)} %tiles.3) | copy-start | bytes 6148
  10.8 13.4 %collective-permute-start.3 = (bf16[512,128]{1,0:T(8,128)(2,1)S(1)}, bf16[512,128]{1,0:T(8,128)(2,1)S(1)}, u32[]{:S(2)}, u32[]{:S(2)}) collective-permute-start(bf16[512,128]{1,0:T(8,128)(2,1)S(1)} %shard_map.78), channel_id=1, source_target_pairs={{0,96},{32,0},{64,32},{96,64},{1,97},{33,1},{65,33},{97,65},{2,98}... | collective-permute-start | bytes 393224 | tf_op jit(solution)/shard_map/ppermute | solution.py:378
  20.2 6.6 %collective-permute-start.2 = (bf16[512,128]{1,0:T(8,128)(2,1)S(1)}, bf16[512,128]{1,0:T(8,128)(2,1)S(1)}, u32[]{:S(2)}, u32[]{:S(2)}) collective-permute-start(bf16[512,128]{1,0:T(8,128)(2,1)S(1)} %shard_map.78), channel_id=1, source_target_pairs={{0,64},{32,96},{64,0},{96,32},{1,65},{33,97},{65,1},{97,33},{2,66}... | collective-permute-start | bytes 393224 | tf_op jit(solution)/shard_map/ppermute | solution.py:378
  20.2 7.6 %collective-permute-start.1 = (bf16[512,128]{1,0:T(8,128)(2,1)S(1)}, bf16[512,128]{1,0:T(8,128)(2,1)S(1)}, u32[]{:S(2)}, u32[]{:S(2)}) collective-permute-start(bf16[512,128]{1,0:T(8,128)(2,1)S(1)} %shard_map.78), channel_id=1, source_target_pairs={{0,32},{32,64},{64,96},{96,0},{1,33},{33,65},{65,97},{97,1},{2,34}... | collective-permute-start | bytes 393224 | tf_op jit(solution)/shard_map/ppermute | solution.py:378
  27.9 2.0 %collective-permute-start.4 = (bf16[4,512,128]{2,1,0:T(8,128)(2,1)S(1)}, bf16[4,512,128]{2,1,0:T(8,128)(2,1)S(1)}, u32[]{:S(2)}, u32[]{:S(2)}) collective-permute-start(bf16[4,512,128]{2,1,0:T(8,128)(2,1)S(1)} %pad_maximum_fusion.own), channel_id=1, source_target_pairs={{0,16},{16,0},{1,17},{17,1},{2,18},{18,2},{3,19},{19,3},{4,20},{20... | collective-permute-start | bytes 1572872 | tf_op jit(solution)/shard_map/ppermute | solution.py:378
  35.9 10.9 %collective-permute-start.5 = (bf16[4,512,128]{2,1,0:T(8,128)(2,1)S(1)}, bf16[4,512,128]{2,1,0:T(8,128)(2,1)S(1)}, u32[]{:S(2)}, u32[]{:S(2)}) collective-permute-start(bf16[4,512,128]{2,1,0:T(8,128)(2,1)S(1)} %get-tuple-element.19), channel_id=1, source_target_pairs={{0,2},{1,3},{2,0},{3,1},{4,6},{5,7},{6,4},{7,5},{8,10},{9,11},{10,... | collective-permute-start | bytes 1572872 | tf_op jit(solution)/shard_map/ppermute | solution.py:418
  36.0 16.1 %collective-permute-start.6 = (bf16[4,512,128]{2,1,0:T(8,128)(2,1)S(1)}, bf16[4,512,128]{2,1,0:T(8,128)(2,1)S(1)}, u32[]{:S(2)}, u32[]{:S(2)}) collective-permute-start(bf16[4,512,128]{2,1,0:T(8,128)(2,1)S(1)} %get-tuple-element.20), channel_id=1, source_target_pairs={{0,1},{1,2},{2,3},{3,0},{4,5},{5,6},{6,7},{7,4},{8,9},{9,10},{10,1... | collective-permute-start | bytes 1572872 | tf_op jit(solution)/shard_map/ppermute | solution.py:418
  37.6 14.5 %collective-permute-start.7 = (bf16[4,512,128]{2,1,0:T(8,128)(2,1)S(1)}, bf16[4,512,128]{2,1,0:T(8,128)(2,1)S(1)}, u32[]{:S(2)}, u32[]{:S(2)}) collective-permute-start(bf16[4,512,128]{2,1,0:T(8,128)(2,1)S(1)} %get-tuple-element.21), channel_id=1, source_target_pairs={{0,3},{1,0},{2,1},{3,2},{4,7},{5,4},{6,5},{7,6},{8,11},{9,8},{10,9... | collective-permute-start | bytes 1572872 | tf_op jit(solution)/shard_map/ppermute | solution.py:418
  39.3 21.5 %copy-start.1 = (bf16[64,1024]{1,0:T(8,128)(2,1)S(1)}, bf16[64,1024]{1,0:T(8,128)(2,1)}, u32[]{:S(2)}) copy-start(bf16[64,1024]{1,0:T(8,128)(2,1)} %refs_4_.1) | copy-start | bytes 393220
  52.3 6.2 %collective-permute-start.8 = (bf16[512,128]{1,0:T(8,128)(2,1)S(1)}, bf16[512,128]{1,0:T(8,128)(2,1)S(1)}, u32[]{:S(2)}, u32[]{:S(2)}) collective-permute-start(bf16[512,128]{1,0:T(8,128)(2,1)S(1)} %get-tuple-element.23), channel_id=1, source_target_pairs={{0,4},{1,5},{2,6},{3,7},{4,8},{5,9},{6,10},{7,11},{8,12},{9,13},{1... | collective-permute-start | bytes 393224 | tf_op jit(solution)/shard_map/ppermute | solution.py:418
  53.6 6.5 %collective-permute-start.9 = (bf16[512,128]{1,0:T(8,128)(2,1)S(1)}, bf16[512,128]{1,0:T(8,128)(2,1)S(1)}, u32[]{:S(2)}, u32[]{:S(2)}) collective-permute-start(bf16[512,128]{1,0:T(8,128)(2,1)S(1)} %get-tuple-element.24), channel_id=1, source_target_pairs={{0,8},{1,9},{2,10},{3,11},{4,12},{5,13},{6,14},{7,15},{8,0},{9,1},... | collective-permute-start | bytes 393224 | tf_op jit(solution)/shard_map/ppermute | solution.py:418
  55.6 5.2 %collective-permute-start.10 = (bf16[512,128]{1,0:T(8,128)(2,1)S(1)}, bf16[512,128]{1,0:T(8,128)(2,1)S(1)}, u32[]{:S(2)}, u32[]{:S(2)}) collective-permute-start(bf16[512,128]{1,0:T(8,128)(2,1)S(1)} %get-tuple-element.25), channel_id=1, source_target_pairs={{0,12},{1,13},{2,14},{3,15},{4,0},{5,1},{6,2},{7,3},{8,4},{9,5},{1... | collective-permute-start | bytes 393224 | tf_op jit(solution)/shard_map/ppermute | solution.py:418
  76.0 1.3 %collective-permute-start.11 = (f32[32,128]{1,0:T(8,128)S(1)}, f32[32,128]{1,0:T(8,128)S(1)}, u32[]{:S(2)}, u32[]{:S(2)}) collective-permute-start(f32[32,128]{1,0:T(8,128)S(1)} %reduce_sum.9), channel_id=1, source_target_pairs={{0,16},{16,0},{1,17},{17,1},{2,18},{18,2},{3,19},{19,3},{4,20},{20... | collective-permute-start | bytes 49160 | tf_op jit(solution)/shard_map/ppermute | solution.py:378
  77.3 3.7 %collective-permute-start.14 = (f32[32,128]{1,0:T(8,128)S(1)}, f32[32,128]{1,0:T(8,128)S(1)}, u32[]{:S(2)}, u32[]{:S(2)}) collective-permute-start(f32[32,128]{1,0:T(8,128)S(1)} %add.3.g0), channel_id=1, source_target_pairs={{0,96},{32,0},{64,32},{96,64},{1,97},{33,1},{65,33},{97,65},{2,98}... | collective-permute-start | bytes 49160 | tf_op jit(solution)/shard_map/ppermute | solution.py:378
  77.7 5.2 %collective-permute-start.13 = (f32[32,128]{1,0:T(8,128)S(1)}, f32[32,128]{1,0:T(8,128)S(1)}, u32[]{:S(2)}, u32[]{:S(2)}) collective-permute-start(f32[32,128]{1,0:T(8,128)S(1)} %add.3.g0), channel_id=1, source_target_pairs={{0,64},{32,96},{64,0},{96,32},{1,65},{33,97},{65,1},{97,33},{2,66}... | collective-permute-start | bytes 49160 | tf_op jit(solution)/shard_map/ppermute | solution.py:378
  79.7 4.9 %collective-permute-start.12 = (f32[32,128]{1,0:T(8,128)S(1)}, f32[32,128]{1,0:T(8,128)S(1)}, u32[]{:S(2)}, u32[]{:S(2)}) collective-permute-start(f32[32,128]{1,0:T(8,128)S(1)} %add.3.g0), channel_id=1, source_target_pairs={{0,32},{32,64},{64,96},{96,0},{1,33},{33,65},{65,97},{97,1},{2,34}... | collective-permute-start | bytes 49160 | tf_op jit(solution)/shard_map/ppermute | solution.py:378

commit v8 on v6

--- a/solution.py
+++ b/solution.py
@@ -19,7 +19,7 @@
 PITCH = 40
 ORDER = (2, 1, 3, 0)
 FIRST = 12
-UNROLL = 64
+UNROLL = 128
 AXES = ("z", "core", "y", "x")
 F32 = jnp.float32
 BF16 = jnp.bfloat16

time: 87.7 us -> 87.2 us (level)
  blocking collectives: 15.4 us -> 13.4 us
  starting transfers between devices: 29.3 us -> 28.1 us
  waiting for transfers between devices: 25.8 us -> 27 us
  Pallas kernels: 12.9 us -> 14 us
    all_to_all x1, blocking collectives: 15.4 us -> 13.4 us  [per_device(): gram = jnp.sum(lax.all_to_all(gram, ('y', 'x'), 0, 0, tiled=True), axis=0)]
where the time goes in v8:
time: 87.2 us; the launch traced here: 86.8 us
  starting transfers between devices  28.1 us (32%)
  waiting for transfers between devices  27 us (31%)
  Pallas kernels  14 us (16%)
  blocking collectives  13.4 us (15%)
  local copies, waits for them, and re-layouts  2.87 us (3%)
  between operations  1.4 us (2%)
    ppermute x8, starting transfers between devices, shifted(): lax.ppermute(value, axis, [(i, (i + shift) % size) for i in range(size)])  13.7 us
    ppermute x8, waiting for transfers between devices, shifted(): lax.ppermute(value, axis, [(i, (i + shift) % size) for i in range(size)])  13.5 us
    ppermute x6, waiting for transfers between devices, across(): return lax.ppermute(value, AXES, pairs)  13.5 us
    all_to_all x1, blocking collectives, per_device(): gram = jnp.sum(lax.all_to_all(gram, ('y', 'x'), 0, 0, tiled=True), axis=0)  13.4 us
    ppermute x6, starting transfers between devices, across(): return lax.ppermute(value, AXES, pairs)  11 us
    pallas_call x1, Pallas kernels, multiply(): pl.pallas_call(first_kernel, in_specs=[smem] * 4 + [vmem] * 3, out_specs=...  4.32 us
    ppermute x1, starting transfers between devices, gather_band(): piece = transpose_panel(lax.ppermute(panel, AXES, placement()[0]), rows)  3.48 us
    pallas_call x1, Pallas kernels, relayout_values(): pl.pallas_call(values_kernel, grid=(CAP // step,), in_specs=[smem, smem,...  2.9 us
  transfers between devices with their start and end apart: 15, of which 13 were waited for; matrix products, arithmetic and copies ran while one was open for 0% of the time, Pallas kernels for 6%

profile of v8, /device:TPU:0, one launch (start us, length us, event | category | flops | bytes accessed | tf_op | source)
XLA Modules:
  0.0 86.8 jit_solution(17253855752298708463)
XLA Ops:
  0.6 3.5 %collective-permute-start = (bf16[64,1024]{1,0:T(8,128)(2,1)}, bf16[64,1024]{1,0:T(8,128)(2,1)S(1)}, u32[]{:S(2)}, u32[]{:S(2)}) collective-permute-start(bf16[64,1024]{1,0:T(8,128)(2,1)} %refs_4_.1), channel_id=1, source_target_pairs={{6,0},{2,16},{5,32},{7,48},{1,96},{3,112},{4,64},{0,80},{11,1},{8,... | collective-permute-start | bytes 393224 | tf_op jit(solution)/shard_map/ppermute | solution.py:403
  4.8 2.2 %copy-done = bf16[512,4096]{1,0:T(8,128)(2,1)S(1)} copy-done((bf16[512,4096]{1,0:T(8,128)(2,1)S(1)}, bf16[512,4096]{1,0:T(8,128)(2,1)}, u32[]{:S(2)}) %copy-start) | copy-done | bytes 4194328
  7.6 2.9 %shard_map.77 = (bf16[16384,128]{1,0:T(8,128)(2,1)S(1)}, s32[8,128]{1,0:T(8,128)S(1)}, s32[8,128]{1,0:T(8,128)S(1)}) custom-call(s32[256]{0:T(256)S(1)} %copy-done.3, s32[1]{0:T(128)S(6)} %copy.8.counts, bf16[512,4096]{1,0:T(8,128)(2,1)S(1)} %copy-done), custom_call_target="tpu_custom_call" | custom-call | bytes 25165824 | tf_op jit(solution)/shard_map/pallas_call | solution.py:83
  10.8 9.4 %collective-permute-start.3 = (bf16[512,128]{1,0:T(8,128)(2,1)S(1)}, bf16[512,128]{1,0:T(8,128)(2,1)S(1)}, u32[]{:S(2)}, u32[]{:S(2)}) collective-permute-start(bf16[512,128]{1,0:T(8,128)(2,1)S(1)} %shard_map.78), channel_id=1, source_target_pairs={{0,96},{32,0},{64,32},{96,64},{1,97},{33,1},{65,33},{97,65},{2,98}... | collective-permute-start | bytes 393224 | tf_op jit(solution)/shard_map/ppermute | solution.py:378
  20.2 0.9 %collective-permute-start.1 = (bf16[512,128]{1,0:T(8,128)(2,1)S(1)}, bf16[512,128]{1,0:T(8,128)(2,1)S(1)}, u32[]{:S(2)}, u32[]{:S(2)}) collective-permute-start(bf16[512,128]{1,0:T(8,128)(2,1)S(1)} %shard_map.78), channel_id=1, source_target_pairs={{0,32},{32,64},{64,96},{96,0},{1,33},{33,65},{65,97},{97,1},{2,34}... | collective-permute-start | bytes 393224 | tf_op jit(solution)/shard_map/ppermute | solution.py:378
  21.2 3.0 %collective-permute-done.3 = bf16[512,128]{1,0:T(8,128)(2,1)S(1)} collective-permute-done((bf16[512,128]{1,0:T(8,128)(2,1)S(1)}, bf16[512,128]{1,0:T(8,128)(2,1)S(1)}, u32[]{:S(2)}, u32[]{:S(2)}) %collective-permute-start.3) | collective-permute-done | bytes 131104 | tf_op jit(solution)/shard_map/ppermute | solution.py:378
  24.2 2.7 %collective-permute-done.2 = bf16[512,128]{1,0:T(8,128)(2,1)S(1)} collective-permute-done((bf16[512,128]{1,0:T(8,128)(2,1)S(1)}, bf16[512,128]{1,0:T(8,128)(2,1)S(1)}, u32[]{:S(2)}, u32[]{:S(2)}) %collective-permute-start.2) | collective-permute-done | bytes 131104 | tf_op jit(solution)/shard_map/ppermute | solution.py:378
  26.8 1.0 %collective-permute-done.1 = bf16[512,128]{1,0:T(8,128)(2,1)S(1)} collective-permute-done((bf16[512,128]{1,0:T(8,128)(2,1)S(1)}, bf16[512,128]{1,0:T(8,128)(2,1)S(1)}, u32[]{:S(2)}, u32[]{:S(2)}) %collective-permute-start.1) | collective-permute-done | bytes 131104 | tf_op jit(solution)/shard_map/ppermute | solution.py:378
  28.5 1.4 %collective-permute-done.4.other = bf16[4,512,128]{2,1,0:T(8,128)(2,1)S(1)} collective-permute-done((bf16[4,512,128]{2,1,0:T(8,128)(2,1)S(1)}, bf16[4,512,128]{2,1,0:T(8,128)(2,1)S(1)}, u32[]{:S(2)}, u32[]{:S(2)}) %collective-permute-start.4) | collective-permute-done | bytes 524320 | tf_op jit(solution)/shard_map/ppermute | solution.py:378
  29.9 4.3 %shard_map.80 = (bf16[16384,128]{1,0:T(8,128)(2,1)S(1)}, bf16[4,512,128]{2,1,0:T(8,128)(2,1)S(1)}, bf16[4,512,128]{2,1,0:T(8,128)(2,1)S(1)}, bf16[4,512,128]{2,1,0:T(8,128)(2,1)S(1)}) custom-call(s32[8,128]{1,0:T(8,128)S(1)} %get-tuple-element.15.rows, s32[8,128]{1,0:T(8,128)S(1)} %get-tuple-element.16.order, s32[512]{0:T(512)S(1)} %copy-done.2, ...), custom_call_target="tpu_custom_call" | custom-call | tf_op jit(solution)/shard_map/pallas_call | solution.py:229
  34.3 4.5 %collective-permute-start.6 = (bf16[4,512,128]{2,1,0:T(8,128)(2,1)S(1)}, bf16[4,512,128]{2,1,0:T(8,128)(2,1)S(1)}, u32[]{:S(2)}, u32[]{:S(2)}) collective-permute-start(bf16[4,512,128]{2,1,0:T(8,128)(2,1)S(1)} %get-tuple-element.20), channel_id=1, source_target_pairs={{0,1},{1,2},{2,3},{3,0},{4,5},{5,6},{6,7},{7,4},{8,9},{9,10},{10,1... | collective-permute-start | bytes 1572872 | tf_op jit(solution)/shard_map/ppermute | solution.py:418
  38.8 2.3 %shard_map.81.refs_0_ = bf16[4,512,128]{2,1,0:T(8,128)(2,1)S(1)} custom-call(s32[8,128]{1,0:T(8,128)S(1)} %get-tuple-element.15.rows, s32[8,128]{1,0:T(8,128)S(1)} %get-tuple-element.16.order, s32[512]{0:T(512)S(1)} %copy-done.2, bf16[16384,128]{1,0:T(8,128)(2,1)S(1)} %get-tuple-element.18.weights, bf16[16384,128]{1,0:T(8,128)(2,1)S(1)} %get-tuple-element.17.values), custom_call_target="tpu_custom_call" | custom-call | bytes 16777216 | tf_op jit(solution)/shard_map/pallas_call | solution.py:237
  41.1 4.0 %collective-permute-done.5.refs_1_ = bf16[4,512,128]{2,1,0:T(8,128)(2,1)S(1)} collective-permute-done((bf16[4,512,128]{2,1,0:T(8,128)(2,1)S(1)}, bf16[4,512,128]{2,1,0:T(8,128)(2,1)S(1)}, u32[]{:S(2)}, u32[]{:S(2)}) %collective-permute-start.5) | collective-permute-done | bytes 524320 | tf_op jit(solution)/shard_map/ppermute | solution.py:418
  45.1 5.5 %collective-permute-done.6.refs_2_ = bf16[4,512,128]{2,1,0:T(8,128)(2,1)S(1)} collective-permute-done((bf16[4,512,128]{2,1,0:T(8,128)(2,1)S(1)}, bf16[4,512,128]{2,1,0:T(8,128)(2,1)S(1)}, u32[]{:S(2)}, u32[]{:S(2)}) %collective-permute-start.6) | collective-permute-done | bytes 524320 | tf_op jit(solution)/shard_map/ppermute | solution.py:418
  50.6 1.0 %collective-permute-done.7.refs_3_ = bf16[4,512,128]{2,1,0:T(8,128)(2,1)S(1)} collective-permute-done((bf16[4,512,128]{2,1,0:T(8,128)(2,1)S(1)}, bf16[4,512,128]{2,1,0:T(8,128)(2,1)S(1)}, u32[]{:S(2)}, u32[]{:S(2)}) %collective-permute-start.7) | collective-permute-done | bytes 524320 | tf_op jit(solution)/shard_map/ppermute | solution.py:418
  51.9 3.2 %collective-permute-start.8 = (bf16[512,128]{1,0:T(8,128)(2,1)S(1)}, bf16[512,128]{1,0:T(8,128)(2,1)S(1)}, u32[]{:S(2)}, u32[]{:S(2)}) collective-permute-start(bf16[512,128]{1,0:T(8,128)(2,1)S(1)} %get-tuple-element.23), channel_id=1, source_target_pairs={{0,8},{1,9},{2,10},{3,11},{4,12},{5,13},{6,14},{7,15},{8,0},{9,1},... | collective-permute-start | bytes 393224 | tf_op jit(solution)/shard_map/ppermute | solution.py:418
  55.1 3.2 %collective-permute-start.10 = (bf16[512,128]{1,0:T(8,128)(2,1)S(1)}, bf16[512,128]{1,0:T(8,128)(2,1)S(1)}, u32[]{:S(2)}, u32[]{:S(2)}) collective-permute-start(bf16[512,128]{1,0:T(8,128)(2,1)S(1)} %get-tuple-element.25), channel_id=1, source_target_pairs={{0,12},{1,13},{2,14},{3,15},{4,0},{5,1},{6,2},{7,3},{8,4},{9,5},{1... | collective-permute-start | bytes 393224 | tf_op jit(solution)/shard_map/ppermute | solution.py:418
  58.4 2.8 %collective-permute-done.9.refs_2_ = bf16[512,128]{1,0:T(8,128)(2,1)S(1)} collective-permute-done((bf16[512,128]{1,0:T(8,128)(2,1)S(1)}, bf16[512,128]{1,0:T(8,128)(2,1)S(1)}, u32[]{:S(2)}, u32[]{:S(2)}) %collective-permute-start.9) | collective-permute-done | bytes 131104 | tf_op jit(solution)/shard_map/ppermute | solution.py:418
  62.0 13.4 %all_to_all.5 = f32[16,32,128]{2,1,0:T(8,128)S(1)} all-to-all(f32[16,32,128]{2,1,0:T(8,128)S(1)} %get-tuple-element.26), channel_id=1, replica_groups=mesh['z'=4,'core'=2,'y'=4,'x'=4] {'y','x'}, dimensions={0} | all-to-all | bytes 524288 | tf_op jit(solution)/shard_map/all_to_all | solution.py:433
  75.5 1.2 %collective-permute-done.11 = f32[32,128]{1,0:T(8,128)S(1)} collective-permute-done((f32[32,128]{1,0:T(8,128)S(1)}, f32[32,128]{1,0:T(8,128)S(1)}, u32[]{:S(2)}, u32[]{:S(2)}) %collective-permute-start.11) | collective-permute-done | bytes 16416 | tf_op jit(solution)/shard_map/ppermute | solution.py:378
  77.5 1.6 %collective-permute-start.13 = (f32[32,128]{1,0:T(8,128)S(1)}, f32[32,128]{1,0:T(8,128)S(1)}, u32[]{:S(2)}, u32[]{:S(2)}) collective-permute-start(f32[32,128]{1,0:T(8,128)S(1)} %add.3.g0), channel_id=1, source_target_pairs={{0,64},{32,96},{64,0},{96,32},{1,65},{33,97},{65,1},{97,33},{2,66}... | collective-permute-start | bytes 49160 | tf_op jit(solution)/shard_map/ppermute | solution.py:378
  80.6 2.3 %collective-permute-done.13.g2 = f32[32,128]{1,0:T(8,128)S(1)} collective-permute-done((f32[32,128]{1,0:T(8,128)S(1)}, f32[32,128]{1,0:T(8,128)S(1)}, u32[]{:S(2)}, u32[]{:S(2)}) %collective-permute-start.13) | collective-permute-done | bytes 16416 | tf_op jit(solution)/shard_map/ppermute | solution.py:378
  82.9 1.2 %collective-permute-done.12.g1 = f32[32,128]{1,0:T(8,128)S(1)} collective-permute-done((f32[32,128]{1,0:T(8,128)S(1)}, f32[32,128]{1,0:T(8,128)S(1)}, u32[]{:S(2)}, u32[]{:S(2)}) %collective-permute-start.12) | collective-permute-done | bytes 16416 | tf_op jit(solution)/shard_map/ppermute | solution.py:378
  84.0 2.8 %shard_map.84 = (f32[64,1024]{1,0:T(8,128)}, f32[64,64]{1,0:T(8,128)}) custom-call(f32[32,128]{1,0:T(8,128)S(1)} %add.3.g0, f32[32,128]{1,0:T(8,128)S(1)} %collective-permute-done.12.g1, f32[32,128]{1,0:T(8,128)S(1)} %collective-permute-done.13.g2, f32[32,128]{1,0:T(8,128)S(1)} %collective-permute-done.14.g3, f32[64,1024]{1,0:T(8,128)S(1)} %get-tuple-element.27.image), custom_call_target="tpu_custom_call" | custom-call | tf_op jit(solution)/shard_map/pallas_call | solution.py:364
  (28 shorter events, 5.2 us)
Async XLA Ops:
  0.6 29.3 %copy-start.4 = (s32[128]{0:T(128)S(1)}, s32[128]{0:T(128)}, u32[]{:S(2)}) copy-start(s32[128]{0:T(128)} %constant.4.clone.table) | copy-start | bytes 1540
  0.6 9.9 %collective-permute-start = (bf16[64,1024]{1,0:T(8,128)(2,1)}, bf16[64,1024]{1,0:T(8,128)(2,1)S(1)}, u32[]{:S(2)}, u32[]{:S(2)}) collective-permute-start(bf16[64,1024]{1,0:T(8,128)(2,1)} %refs_4_.1), channel_id=1, source_target_pairs={{6,0},{2,16},{5,32},{7,48},{1,96},{3,112},{4,64},{0,80},{11,1},{8,... | collective-permute-start | bytes 393224 | tf_op jit(solution)/shard_map/ppermute | solution.py:403
  4.8 2.2 %copy-start = (bf16[512,4096]{1,0:T(8,128)(2,1)S(1)}, bf16[512,4096]{1,0:T(8,128)(2,1)}, u32[]{:S(2)}) copy-start(bf16[512,4096]{1,0:T(8,128)(2,1)} %values.1) | copy-start | bytes 12582916
  7.0 0.7 copy-start.3
  7.6 22.3 %copy-start.2 = (s32[512]{0:T(512)S(1)}, s32[512]{0:T(512)}, u32[]{:S(2)}) copy-start(s32[512]{0:T(512)} %tiles.3) | copy-start | bytes 6148
  10.8 13.4 %collective-permute-start.3 = (bf16[512,128]{1,0:T(8,128)(2,1)S(1)}, bf16[512,128]{1,0:T(8,128)(2,1)S(1)}, u32[]{:S(2)}, u32[]{:S(2)}) collective-permute-start(bf16[512,128]{1,0:T(8,128)(2,1)S(1)} %shard_map.78), channel_id=1, source_target_pairs={{0,96},{32,0},{64,32},{96,64},{1,97},{33,1},{65,33},{97,65},{2,98}... | collective-permute-start | bytes 393224 | tf_op jit(solution)/shard_map/ppermute | solution.py:378
  20.2 6.6 %collective-permute-start.2 = (bf16[512,128]{1,0:T(8,128)(2,1)S(1)}, bf16[512,128]{1,0:T(8,128)(2,1)S(1)}, u32[]{:S(2)}, u32[]{:S(2)}) collective-permute-start(bf16[512,128]{1,0:T(8,128)(2,1)S(1)} %shard_map.78), channel_id=1, source_target_pairs={{0,64},{32,96},{64,0},{96,32},{1,65},{33,97},{65,1},{97,33},{2,66}... | collective-permute-start | bytes 393224 | tf_op jit(solution)/shard_map/ppermute | solution.py:378
  20.2 7.6 %collective-permute-start.1 = (bf16[512,128]{1,0:T(8,128)(2,1)S(1)}, bf16[512,128]{1,0:T(8,128)(2,1)S(1)}, u32[]{:S(2)}, u32[]{:S(2)}) collective-permute-start(bf16[512,128]{1,0:T(8,128)(2,1)S(1)} %shard_map.78), channel_id=1, source_target_pairs={{0,32},{32,64},{64,96},{96,0},{1,33},{33,65},{65,97},{97,1},{2,34}... | collective-permute-start | bytes 393224 | tf_op jit(solution)/shard_map/ppermute | solution.py:378
  27.9 2.0 %collective-permute-start.4 = (bf16[4,512,128]{2,1,0:T(8,128)(2,1)S(1)}, bf16[4,512,128]{2,1,0:T(8,128)(2,1)S(1)}, u32[]{:S(2)}, u32[]{:S(2)}) collective-permute-start(bf16[4,512,128]{2,1,0:T(8,128)(2,1)S(1)} %pad_maximum_fusion.own), channel_id=1, source_target_pairs={{0,16},{16,0},{1,17},{17,1},{2,18},{18,2},{3,19},{19,3},{4,20},{20... | collective-permute-start | bytes 1572872 | tf_op jit(solution)/shard_map/ppermute | solution.py:378
  34.2 10.9 %collective-permute-start.5 = (bf16[4,512,128]{2,1,0:T(8,128)(2,1)S(1)}, bf16[4,512,128]{2,1,0:T(8,128)(2,1)S(1)}, u32[]{:S(2)}, u32[]{:S(2)}) collective-permute-start(bf16[4,512,128]{2,1,0:T(8,128)(2,1)S(1)} %get-tuple-element.19), channel_id=1, source_target_pairs={{0,2},{1,3},{2,0},{3,1},{4,6},{5,7},{6,4},{7,5},{8,10},{9,11},{10,... | collective-permute-start | bytes 1572872 | tf_op jit(solution)/shard_map/ppermute | solution.py:418
  34.3 16.3 %collective-permute-start.6 = (bf16[4,512,128]{2,1,0:T(8,128)(2,1)S(1)}, bf16[4,512,128]{2,1,0:T(8,128)(2,1)S(1)}, u32[]{:S(2)}, u32[]{:S(2)}) collective-permute-start(bf16[4,512,128]{2,1,0:T(8,128)(2,1)S(1)} %get-tuple-element.20), channel_id=1, source_target_pairs={{0,1},{1,2},{2,3},{3,0},{4,5},{5,6},{6,7},{7,4},{8,9},{9,10},{10,1... | collective-permute-start | bytes 1572872 | tf_op jit(solution)/shard_map/ppermute | solution.py:418
  38.8 12.8 %collective-permute-start.7 = (bf16[4,512,128]{2,1,0:T(8,128)(2,1)S(1)}, bf16[4,512,128]{2,1,0:T(8,128)(2,1)S(1)}, u32[]{:S(2)}, u32[]{:S(2)}) collective-permute-start(bf16[4,512,128]{2,1,0:T(8,128)(2,1)S(1)} %get-tuple-element.21), channel_id=1, source_target_pairs={{0,3},{1,0},{2,1},{3,2},{4,7},{5,4},{6,5},{7,6},{8,11},{9,8},{10,9... | collective-permute-start | bytes 1572872 | tf_op jit(solution)/shard_map/ppermute | solution.py:418
  38.8 22.4 %copy-start.1 = (bf16[64,1024]{1,0:T(8,128)(2,1)S(1)}, bf16[64,1024]{1,0:T(8,128)(2,1)}, u32[]{:S(2)}) copy-start(bf16[64,1024]{1,0:T(8,128)(2,1)} %refs_4_.1) | copy-start | bytes 393220
  51.9 6.6 %collective-permute-start.8 = (bf16[512,128]{1,0:T(8,128)(2,1)S(1)}, bf16[512,128]{1,0:T(8,128)(2,1)S(1)}, u32[]{:S(2)}, u32[]{:S(2)}) collective-permute-start(bf16[512,128]{1,0:T(8,128)(2,1)S(1)} %get-tuple-element.23), channel_id=1, source_target_pairs={{0,8},{1,9},{2,10},{3,11},{4,12},{5,13},{6,14},{7,15},{8,0},{9,1},... | collective-permute-start | bytes 393224 | tf_op jit(solution)/shard_map/ppermute | solution.py:418
  55.1 6.2 %collective-permute-start.9 = (bf16[512,128]{1,0:T(8,128)(2,1)S(1)}, bf16[512,128]{1,0:T(8,128)(2,1)S(1)}, u32[]{:S(2)}, u32[]{:S(2)}) collective-permute-start(bf16[512,128]{1,0:T(8,128)(2,1)S(1)} %get-tuple-element.24), channel_id=1, source_target_pairs={{0,4},{1,5},{2,6},{3,7},{4,8},{5,9},{6,10},{7,11},{8,12},{9,13},{1... | collective-permute-start | bytes 393224 | tf_op jit(solution)/shard_map/ppermute | solution.py:418
  55.1 6.2 %collective-permute-start.10 = (bf16[512,128]{1,0:T(8,128)(2,1)S(1)}, bf16[512,128]{1,0:T(8,128)(2,1)S(1)}, u32[]{:S(2)}, u32[]{:S(2)}) collective-permute-start(bf16[512,128]{1,0:T(8,128)(2,1)S(1)} %get-tuple-element.25), channel_id=1, source_target_pairs={{0,12},{1,13},{2,14},{3,15},{4,0},{5,1},{6,2},{7,3},{8,4},{9,5},{1... | collective-permute-start | bytes 393224 | tf_op jit(solution)/shard_map/ppermute | solution.py:418
  75.4 1.3 %collective-permute-start.11 = (f32[32,128]{1,0:T(8,128)S(1)}, f32[32,128]{1,0:T(8,128)S(1)}, u32[]{:S(2)}, u32[]{:S(2)}) collective-permute-start(f32[32,128]{1,0:T(8,128)S(1)} %reduce_sum.9), channel_id=1, source_target_pairs={{0,16},{16,0},{1,17},{17,1},{2,18},{18,2},{3,19},{19,3},{4,20},{20... | collective-permute-start | bytes 49160 | tf_op jit(solution)/shard_map/ppermute | solution.py:378
  76.6 3.9 %collective-permute-start.14 = (f32[32,128]{1,0:T(8,128)S(1)}, f32[32,128]{1,0:T(8,128)S(1)}, u32[]{:S(2)}, u32[]{:S(2)}) collective-permute-start(f32[32,128]{1,0:T(8,128)S(1)} %add.3.g0), channel_id=1, source_target_pairs={{0,96},{32,0},{64,32},{96,64},{1,97},{33,1},{65,33},{97,65},{2,98}... | collective-permute-start | bytes 49160 | tf_op jit(solution)/shard_map/ppermute | solution.py:378
  77.5 5.3 %collective-permute-start.13 = (f32[32,128]{1,0:T(8,128)S(1)}, f32[32,128]{1,0:T(8,128)S(1)}, u32[]{:S(2)}, u32[]{:S(2)}) collective-permute-start(f32[32,128]{1,0:T(8,128)S(1)} %add.3.g0), channel_id=1, source_target_pairs={{0,64},{32,96},{64,0},{96,32},{1,65},{33,97},{65,1},{97,33},{2,66}... | collective-permute-start | bytes 49160 | tf_op jit(solution)/shard_map/ppermute | solution.py:378
  79.1 4.9 %collective-permute-start.12 = (f32[32,128]{1,0:T(8,128)S(1)}, f32[32,128]{1,0:T(8,128)S(1)}, u32[]{:S(2)}, u32[]{:S(2)}) collective-permute-start(f32[32,128]{1,0:T(8,128)S(1)} %add.3.g0), channel_id=1, source_target_pairs={{0,32},{32,64},{64,96},{96,0},{1,33},{33,65},{65,97},{97,1},{2,34}... | collective-permute-start | bytes 49160 | tf_op jit(solution)/shard_map/ppermute | solution.py:378
